TPU v7x, 32 devices: a whole 2x2x4 slice. The times are simulated.
32 devices in a mesh: dp: 8 (over y, x, core), mp: 4 (over z).
Axes of the slice: x: 2, y: 2, z: 4, core: 2. Of those that a mesh axis runs over, the one named last changes fastest.
Arguments:
- patches: bfloat16 [256, 14, 14, 256], P(('dp', 'mp')), may hold values from -6 to 6
- validity: int32 [256, 14, 14], P(('dp', 'mp')), may hold values from 0 to 1, as said below
- norm_gain: bfloat16 [2, 2, 256], P(None, None, 'mp'), may hold values from 0.099609375 to 1.8984375
- norm_shift: bfloat16 [2, 2, 256], P(None, None, 'mp'), may hold values from -3 to 3
- query_key_value_weight: bfloat16 [2, 256, 3, 256], P(None, None, None, 'mp'), may hold values from -0.375 to 0.375
- entry_bias: bfloat16 [2, 2, 256], P(None, None, 'mp'), may hold values from -3 to 3
- stencil: bfloat16 [2, 10, 256], P(None, None, 'mp'), may hold values from -2 to 2
- mixer_weight: bfloat16 [2, 256, 256], P(None, None, 'mp'), may hold values from -1 to 1
- branch_bias: bfloat16 [2, 2, 256], P(None, None, 'mp'), may hold values from -1.75 to 1.75
- expand_weight: bfloat16 [2, 256, 1024], P(None, None, 'mp'), may hold values from -0.375 to 0.375
- hidden_bias: bfloat16 [2, 1024], P(None, 'mp'), may hold values from -3 to 3
- reduce_weight: bfloat16 [2, 1024, 256], P(None, None, 'mp'), may hold values from -0.1875 to 0.1875
- cotangent: bfloat16 [256, 14, 14, 256], P(('dp', 'mp')), may hold values from -6 to 6
Outputs:
- output: bfloat16 [256, 14, 14, 256], P(('dp', 'mp'))
- patch_grad: bfloat16 [256, 14, 14, 256], P(('dp', 'mp'))
- gain_grad: float32 [2, 2, 256], P(None, None, 'mp')
- shift_grad: float32 [2, 2, 256], P(None, None, 'mp')
- packed_grad: float32 [2, 256, 3, 256], P(None, None, None, 'mp')
- entry_grad: float32 [2, 2, 256], P(None, None, 'mp')
- stencil_grad: float32 [2, 10, 256], P(None, None, 'mp')
- mixer_grad: float32 [2, 256, 256], P(None, None, 'mp')
- branch_grad: float32 [2, 2, 256], P(None, None, 'mp')
- expand_grad: float32 [2, 256, 1024], P(None, None, 'mp')
- hidden_grad: float32 [2, 1024], P(None, 'mp')
- reduce_grad: float32 [2, 1024, 256], P(None, None, 'mp')
Inputs may be any that keep to these rules, and one draw needn't show every extreme that they name: validity is 1 on the patches of a crop whose row is below h and whose column is below w, 0 elsewhere, where h and w are whole numbers of 8 to 14 drawn for each crop.
All inputs are finite; a program needn't handle non-finite values.
Results may differ from a plain program's by a relative error of at most 0.025.
Values may be sent and summed in bfloat16 or wider, within the bound.
No kernel may reach another device: no remote copies, remote signals or barrier semaphores. Data moves between devices by JAX's collectives and lax.ppermute only.
A program may use at most 192 MiB of HBM per device.

v0:
```python
import functools

import jax
import jax.numpy as jnp
from jax import lax
from jax.experimental import pallas as pl
from jax.experimental.pallas import tpu as pltpu
from jax.sharding import PartitionSpec as P

GRID = 14
STRIPE = 7
CELLS = GRID * GRID
CROPS = 8
ROWS = CELLS * CROPS
LINE = GRID * CROPS
HELD = ROWS + 112
WIN = 112
HALF_HEADS = 4
HEAD = 32
D = 256
FF = 1024
STEP_CROPS = 2
CHUNK = 784

norm_eps = 1e-05
masked_score = -1e30
root_half = 0.7071067811865476
inverse_root_tau = 0.3989422804014327
log2_e = 1.4426950408889634
factor = HEAD**-0.5

f32 = jnp.float32
bf16 = jnp.bfloat16

HALF_ATTN = 144
HALF_FF = 256
FF_ROWS = 512
UNIT = 800
LOW_ROWS = 288
GAIN, SHIFT, ENTRY, TAPS, BRANCH, HIDDEN = 0, 2, 4, 6, 16, 18


def dot(a, b):
    return lax.dot_general(a, b, (((1,), (0,)), ((), ())), preferred_element_type=f32)


def dot_nt(a, b):
    return lax.dot_general(a, b, (((1,), (1,)), ((), ())), preferred_element_type=f32)


def dot_tn(a, b):
    return lax.dot_general(a, b, (((0,), (0,)), ((), ())), preferred_element_type=f32)


def norm(x):
    center = x - jnp.mean(x, axis=-1, keepdims=True)
    spread = jnp.mean(center * center, axis=-1, keepdims=True)
    inverse = lax.rsqrt(spread + norm_eps)
    return center * inverse, inverse


def norm_back(grad, normal, inverse, gain):
    scaled = grad * gain
    return inverse * (
        scaled
        - jnp.mean(scaled, axis=-1, keepdims=True)
        - normal * jnp.mean(scaled * normal, axis=-1, keepdims=True)
    )


def column_sum(x):
    return jnp.sum(x.reshape(x.shape[0] // CROPS, CROPS, x.shape[1]), axis=0)


def window_row_inside(orient):
    row = lax.broadcasted_iota(jnp.int32, (WIN, 128), 0)
    return row < 98 if orient == 0 else row % 8 < STRIPE


def key_bias(orient, window, height, width):
    row = lax.broadcasted_iota(jnp.int32, (WIN, 128), 0)
    if orient == 0:
        line, column = row // GRID + window * STRIPE, row % GRID
    else:
        line, column = row // 8, row % 8 + window * STRIPE
    valid = window_row_inside(orient) & (line < height) & (column < width)
    return jnp.where(valid, 0.0, masked_score)


def load_window(ref, block, crop, orient, window):
    if orient == 0:
        return ref[block, pl.ds(98 * CROPS * window + crop, WIN, stride=CROPS), :]
    parts = [
        ref[block, pl.ds((line * GRID + window * STRIPE) * CROPS + crop, 8, stride=CROPS), :]
        for line in range(GRID)
    ]
    return jnp.concatenate(parts, axis=0)


def store_window(ref, block, crop, orient, window, x):
    if orient == 0:
        ref[block, pl.ds(98 * CROPS * window + crop, 98, stride=CROPS), :] = x[:98]
        return
    for line in range(GRID):
        at = (line * GRID + window * STRIPE) * CROPS + crop
        ref[block, pl.ds(at, STRIPE, stride=CROPS), :] = x[line * 8 : line * 8 + STRIPE]


def heads_apart(x, inside=None):
    lane = lax.broadcasted_iota(jnp.int32, (WIN, 128), 1) // HEAD
    rest = jnp.zeros((128 - WIN, 128), bf16)
    blocks = []
    for head in range(HALF_HEADS):
        keep = lane == head
        if inside is not None:
            keep = keep & inside
        blocks.append(jnp.where(keep, x, 0.0).astype(bf16))
        blocks.append(rest)
    return jnp.concatenate(blocks, axis=0)


def by_head(flat_turned, probs):
    parts = []
    for head in range(HALF_HEADS):
        parts.append(
            dot(flat_turned[head * HEAD : (head + 1) * HEAD], probs[:, head * 128 : (head + 1) * 128])
        )
    return jnp.concatenate(parts, axis=0)


def attend(queries, keys, values, biases):
    apart = [heads_apart(x) for x in queries]
    value_turned = [x.T.astype(bf16) for x in values]
    scores = [dot_nt(k.astype(bf16), q) for k, q in zip(keys, apart)]
    scores = [s * (factor * log2_e) + jnp.concatenate([b] * HALF_HEADS, axis=1) for s, b in zip(scores, biases)]
    peaks = [jnp.max(s, axis=0, keepdims=True) for s in scores]
    raised = [jnp.exp2(s - p) for s, p in zip(scores, peaks)]
    shares = [1.0 / jnp.sum(r, axis=0, keepdims=True) for r in raised]
    probs = [(r * s).astype(bf16) for r, s in zip(raised, shares)]
    outs = [by_head(v, p) for v, p in zip(value_turned, probs)]
    return [o.T[:WIN] for o in outs], probs


def attend_back(grads, queries, keys, values, probs, insides):
    grad_apart = [heads_apart(x, i) for x, i in zip(grads, insides)]
    grad_probs = [dot_nt(v, g) for v, g in zip(values, grad_apart)]
    key_turned = [x.astype(f32).T.astype(bf16) for x in keys]
    grad_value = [dot(p, g) for p, g in zip(probs, grad_apart)]
    wide = [p.astype(f32) for p in probs]
    inner = [jnp.sum(g * w, axis=0, keepdims=True) for g, w in zip(grad_probs, wide)]
    grad_scores = [(w * (g - i)).astype(bf16) for w, g, i in zip(wide, grad_probs, inner)]
    apart = [heads_apart(x) for x in queries]
    grad_key = [dot(s, q) * factor for s, q in zip(grad_scores, apart)]
    grad_query = [by_head(k, s) for k, s in zip(key_turned, grad_scores)]
    grad_query = [g.T[:WIN] * factor for g in grad_query]
    return grad_query, grad_key, grad_value


WINDOWS = [(orient, window) for orient in range(2) for window in range(2)]


def steps_along(x, orient):
    zero = jnp.zeros((CROPS, x.shape[1]), x.dtype)
    if orient == 0:
        return {-1: jnp.concatenate([zero, x[:-CROPS]], axis=0), 0: x, 1: jnp.concatenate([x[CROPS:], zero], axis=0)}
    half = LINE // 2
    left, right = x[:half], x[half:]
    return {
        -1: jnp.concatenate([zero, left[:-CROPS], zero, right[:-CROPS]], axis=0),
        0: x,
        1: jnp.concatenate([left[CROPS:], zero, right[CROPS:], zero], axis=0),
    }


def line_reaches(line, step, orient):
    if step == 0:
        return None
    stops = (GRID, STRIPE) if orient == 0 else (GRID,)
    edges = [(stop - 1) if step == 1 else (stop % GRID) for stop in stops]
    ok = line != edges[0]
    for edge in edges[1:]:
        ok = ok & (line != edge)
    return jnp.where(ok, 1.0, 0.0).astype(f32)


def line_at(ref, block, line):
    held = jnp.clip(line, 0, GRID - 1)
    return ref[block, pl.ds(pl.multiple_of(held * LINE, LINE), LINE), :]


def stencil_line(ref, block, taps, line, orient, back):
    total = None
    for step in (-1, 0, 1):
        moved = steps_along(line_at(ref, block, line + (-step if back else step)).astype(f32), orient)
        reach = line_reaches(line, -step if back else step, orient)
        for side in (-1, 0, 1):
            tap = taps[3 * (step + 1) + side + 1]
            if reach is not None:
                tap = tap * reach
            term = moved[-side if back else side] * tap
            total = term if total is None else total + term
    return total


def stencil_line_taps(ref, block, grad, line, orient):
    sums = []
    for step in (-1, 0, 1):
        moved = steps_along(line_at(ref, block, line + step).astype(f32), orient)
        reach = line_reaches(line, step, orient)
        for side in (-1, 0, 1):
            part = column_sum(grad * moved[side])
            sums.append(part if reach is None else part * reach)
    sums.append(column_sum(grad))
    return sums


def assemble_attn(layer, me, core, own, near, far, wqkv, wm, sm):
    qkv, mixer_t, vec = own

    def put(shard, blocks, at, mixer_rows, mixer_at):
        orient, part = lax.div(shard, 2), lax.rem(shard, 2)
        for i, block in enumerate(blocks):
            j = at + i
            row = orient * 384 + lax.div(j, 2) * 128 + part * 64 + lax.rem(j, 2) * 32
            wqkv[pl.ds(pl.multiple_of(row, 32), 32), :] = block
        wm[pl.ds(pl.multiple_of(shard * 64 + mixer_at, 32), mixer_rows.shape[0]), :] = mixer_rows

    put(me, [qkv[0, 32 * i : 32 * (i + 1)] for i in range(6)], jnp.int32(0), mixer_t[0], 0)
    sm[...] = vec[layer].astype(f32)
    for halves, which in ((near, core), (far, 1 - core)):
        for k, half in enumerate(halves, 1):
            shard = lax.rem(me + 4 - k, 4)
            put(shard, [half[32 * i : 32 * (i + 1)] for i in range(3)], 3 * which, half[96:128], 32 * which)
            sm[pl.ds(pl.multiple_of(16 * which, 16), 16), :] += half[128:144].astype(f32)


def assemble_ff(first, me, core, own, near, far, we, wr):
    expand, reduce_t = own
    we[me] = expand[0]
    wr[pl.ds(pl.multiple_of(me * 64, 64), 64), :] = reduce_t[0]
    for halves, which in ((near, core), (far, 1 - core)):
        for k, half in enumerate(halves, 1):
            shard = lax.rem(me + 4 - k, 4)
            we[shard, pl.ds(pl.multiple_of(128 * which, 128), 128), :] = half[first : first + 128]
            row = pl.multiple_of(shard * 64 + 32 * which, 32)
            for c in range(4):
                at = first + 128 + 32 * c
                wr[pl.ds(row, 32), c * 256 : (c + 1) * 256] = half[at : at + 32]


def assemble_top(me, attn_own, ff_own, rest, wqkv, wm, sm, we, wr):
    qkv, mixer_t, vec = attn_own
    expand, reduce_t = ff_own

    def put(shard, row, value):
        orient, part = lax.div(shard, 2), lax.rem(shard, 2)
        n = value.shape[0]
        if row < 192:
            at = orient * 384 + row // 64 * 128 + part * 64 + row % 64
            wqkv[pl.ds(pl.multiple_of(at, 16), n), :] = value
        elif row < 256:
            wm[pl.ds(pl.multiple_of(shard * 64 + row - 192, 16), n), :] = value
        elif row < 288:
            sm[row - 256 : row - 256 + n, :] += value.astype(f32)
        elif row < 544:
            we[shard, row - 288 : row - 288 + n, :] = value
        else:
            c, at = divmod(row - 544, 64)
            wr[pl.ds(pl.multiple_of(shard * 64 + at, 16), n), c * 256 : (c + 1) * 256] = value

    for p in range(3):
        put(me, 64 * p, qkv[0, 64 * p : 64 * (p + 1)])
    put(me, 192, mixer_t[0])
    sm[...] = vec[1].astype(f32)
    put(me, 288, expand[0])
    for c in range(4):
        put(me, 544 + 64 * c, reduce_t[0, :, c * 256 : (c + 1) * 256])
    dp, _, r, _ = rest.shape
    edges = list(range(0, 257, 64)) + [288] + [544 + 64 * c for c in range(5)]
    for k in range(3):
        shard = lax.rem(me + 3 - k, 4)
        for d in range(dp):
            for lo, hi in zip(edges[:-1], edges[1:]):
                a, b = max(lo, d * r), min(hi, (d + 1) * r)
                if a < b:
                    put(shard, a, rest[d, k, a - d * r : b - d * r])


def chunks():
    return [slice(at, at + CHUNK) for at in range(0, ROWS, CHUNK)]


def put_blocks(ref, rows, x):
    for block in range(x.shape[1] // 128):
        ref[block, rows, :] = x[:, block * 128 : (block + 1) * 128]


def project(x, wqkv, sm, qkv):
    zero = jnp.zeros((1, 128), f32)
    query_bias, value_bias = sm[ENTRY : ENTRY + 1], sm[ENTRY + 1 : ENTRY + 2]
    bias = jnp.concatenate(
        [query_bias[:, :128], zero, value_bias[:, :128], query_bias[:, 128:], zero, value_bias[:, 128:]], axis=1
    )
    for rows in chunks():
        normal, _ = norm(x[rows, :].astype(f32))
        a = (normal * sm[GAIN : GAIN + 1] + sm[SHIFT : SHIFT + 1]).astype(bf16)
        put_blocks(qkv, rows, dot_nt(a, wqkv[...]) + bias)
    qkv[:, ROWS:HELD, :] = jnp.zeros((6, HELD - ROWS, 128), f32)


def attend_crops(place, crops, slots, qkv, packed, probs_ref, out):
    at, lists = [], ([], [], [], [])
    for crop, slot in zip(crops, slots):
        height, width = place[2 + 2 * crop], place[3 + 2 * crop]
        for n, (orient, window) in enumerate(WINDOWS):
            three = [load_window(qkv, orient * 3 + p, crop, orient, window) for p in range(3)]
            packed[slot, n] = jnp.concatenate(three, axis=1).astype(bf16)
            entries = (*three, key_bias(orient, window, height, width))
            for held, new in zip(lists, entries):
                held.append(new)
            at.append((crop, slot, n, orient, window))
    outs, probs = attend(*lists)
    for (crop, slot, n, orient, window), o, p in zip(at, outs, probs):
        probs_ref[slot, n] = p
        store_window(out, orient, crop, orient, window, o)


def attend_crops_back(crops, slots, em, packed, probs_ref, e):
    at, lists = [], ([], [], [], [], [], [])
    for crop, slot in zip(crops, slots):
        for n, (orient, window) in enumerate(WINDOWS):
            grad = load_window(em, orient, crop, orient, window)
            entries = (
                grad, packed[slot, n, :, :128], packed[slot, n, :, 128:256], packed[slot, n, :, 256:],
                probs_ref[slot, n], window_row_inside(orient),
            )
            for held, new in zip(lists, entries):
                held.append(new)
            at.append((crop, orient, window))
    for (crop, orient, window), dq, dk, dv in zip(at, *attend_back(*lists)):
        for p, part in enumerate((dq, dk, dv)):
            store_window(e, orient * 3 + p, crop, orient, window, part)


def taps_of(sm, orient):
    lanes = slice(orient * 128, (orient + 1) * 128)
    return [sm[TAPS + t : TAPS + t + 1, lanes] for t in range(10)]


def mix(out, value, value_at, sm, mixed):
    taps = [taps_of(sm, orient) for orient in range(2)]

    def line(i, _):
        rows = pl.ds(pl.multiple_of(i * LINE, LINE), LINE)
        for orient in range(2):
            e_v = stencil_line(value, value_at[orient], taps[orient], i, orient, False) + taps[orient][9]
            mixed[rows, orient * 128 : (orient + 1) * 128] = (out[orient, rows, :] + e_v).astype(bf16)
        return 0

    lax.fori_loop(0, GRID, line, 0)


def mixer(x, mixed, wm, sm, middle):
    for rows in chunks():
        middle[rows, :] = x[rows, :].astype(f32) + (dot_nt(mixed[rows, :], wm[...]) + sm[BRANCH : BRANCH + 1])


def hidden(a2, we, sm, s):
    u = dot(a2, we[s]) + sm[HIDDEN + s : HIDDEN + s + 1]
    phi = 0.5 + 0.5 * lax.erf(u * root_half)
    return u, phi


def slope_of(u, phi):
    return phi + u * jnp.exp(-0.5 * u * u) * inverse_root_tau


def second_norm(middle, sm):
    normal, inverse = norm(middle)
    a2 = (normal * sm[GAIN + 1 : GAIN + 2] + sm[SHIFT + 1 : SHIFT + 2]).astype(bf16)
    return normal, inverse, a2


def ff_forward(middle, we, wr, sm, g_out=None, slope_out=None):
    _, _, a2 = second_norm(middle, sm)
    gs = []
    for s in range(4):
        u, phi = hidden(a2, we, sm, s)
        gs.append((u * phi).astype(bf16))
        if g_out is not None:
            g_out[s], slope_out[s] = gs[-1], slope_of(u, phi).astype(bf16)
    return middle + (dot_nt(jnp.concatenate(gs, axis=1), wr[...]) + sm[BRANCH + 1 : BRANCH + 2])


def ff_backward(grad, middle, we, wr, sm, acc_e, acc_r, vec, held=None):
    ey = grad.astype(bf16)
    vec[BRANCH + 1] += column_sum(grad)
    normal, inverse, a2 = second_norm(middle, sm)
    eus = []
    for s in range(4):
        if held is None:
            u, phi = hidden(a2, we, sm, s)
            g, slope = (u * phi).astype(bf16), slope_of(u, phi)
        else:
            g, slope = held(s)
        acc_r[s] += dot_tn(ey, g)
        eu_wide = dot(ey, wr[:, s * 256 : (s + 1) * 256]) * slope.astype(f32)
        vec[HIDDEN + s] += column_sum(eu_wide)
        eu = eu_wide.astype(bf16)
        acc_e[s] += dot_tn(a2, eu)
        eus.append(eu)
    back = None
    for s in range(4):
        term = dot_nt(eus[s], we[s])
        back = term if back is None else back + term
    vec[GAIN + 1] += column_sum(back * normal)
    vec[SHIFT + 1] += column_sum(back)
    return grad + norm_back(back, normal, inverse, sm[GAIN + 1 : GAIN + 2])


def mixer_back(grad, mixed, wm, acc_m, vec, em):
    for rows in chunks():
        here = grad[rows, :]
        eo = here.astype(bf16)
        vec[BRANCH] += column_sum(here)
        acc_m[...] += dot_tn(eo, mixed[rows, :])
        put_blocks(em, rows, dot(eo, wm[...]))
    em[:, ROWS:HELD, :] = jnp.zeros((2, HELD - ROWS, 128), f32)


def mix_back(em, value, value_at, sm, e, e_low, vec):
    taps = [taps_of(sm, orient) for orient in range(2)]

    def line(i, _):
        rows = pl.ds(pl.multiple_of(i * LINE, LINE), LINE)
        for orient in range(2):
            lanes = slice(orient * 128, (orient + 1) * 128)
            base = orient * 384
            eq, ek, ev = [e[orient * 3 + p, rows, :] for p in range(3)]
            ev = ev + stencil_line(em, orient, taps[orient], i, orient, True)
            e_low[rows, base : base + 384] = jnp.concatenate([eq, ek, ev], axis=1).astype(bf16)
            vec[ENTRY, :, lanes] += column_sum(eq)
            vec[ENTRY + 1, :, lanes] += column_sum(ev)
            for t, part in enumerate(stencil_line_taps(value, value_at[orient], em[orient, rows, :], i, orient)):
                vec[TAPS + t, :, lanes] += part
        return 0

    lax.fori_loop(0, GRID, line, 0)


def project_back(grad, x, e_low, wqkv, sm, acc_q, vec, out):
    for rows in chunks():
        normal, inverse = norm(x[rows, :].astype(f32))
        a = (normal * sm[GAIN : GAIN + 1] + sm[SHIFT : SHIFT + 1]).astype(bf16)
        e = e_low[rows, :]
        acc_q[...] += dot_tn(e, a)
        back = dot(e, wqkv[...])
        vec[GAIN] += column_sum(back * normal)
        vec[SHIFT] += column_sum(back)
        out[rows, :] = (grad[rows, :] + norm_back(back, normal, inverse, sm[GAIN : GAIN + 1])).astype(out.dtype)


def attn_pieces(acc_q, acc_m, sums):
    def qkv(s, p, lo, hi):
        at = (s // 2) * 384 + p * 128 + (s % 2) * 64
        return acc_q[at + lo : at + hi]

    return [(64, lambda s, lo, hi, p=p: qkv(s, p, lo, hi)) for p in range(3)] + [
        (64, lambda s, lo, hi: acc_m[64 * s + lo : 64 * s + hi]),
        (32, lambda s, lo, hi: sums[lo:hi]),
    ]


def ff_pieces(acc_e, acc_r):
    return [(256, lambda s, lo, hi: acc_e[s, lo:hi])] + [
        (64, lambda s, lo, hi, c=c: acc_r[c, 64 * s + lo : 64 * s + hi]) for c in range(4)
    ]


def part_rows(rows, parts):
    return -(-rows // (16 * parts)) * 16


def write_parts(pieces, first, ref):
    parts, _, r, _ = ref.shape
    for s in range(4):
        at = -first
        for rows, get in pieces + [(first + parts * r, None)]:
            for part in range(parts):
                lo, hi = max(at, part * r), min(at + rows, (part + 1) * r)
                if lo < hi:
                    new = jnp.zeros((hi - lo, D), f32) if get is None else get(s, lo - at, hi - at)
                    ref[part, s, lo - part * r : hi - part * r] = new.astype(ref.dtype)
            at += rows


def write_halves(core, pieces, keep, give):
    half = keep.shape[0] * keep.shape[2]
    for mine in range(2):

        @pl.when(core == mine)
        def _(mine=mine):
            write_parts(pieces, mine * half, keep)
            write_parts(pieces, (1 - mine) * half, give)


def clear(*refs):
    for ref in refs:
        ref[...] = jnp.zeros_like(ref)


def first_step(fn):
    pl.when(pl.program_id(0) == 0)(fn)


def last_step(fn):
    pl.when(pl.program_id(0) == pl.num_programs(0) - 1)(fn)


def attn_fwd_kernel(place, x, *refs):
    own, near, far = refs[0:3], refs[3:6], refs[6:9]
    middle, packed, probs, mixed, value, wqkv, wm, sm, qkv, out = refs[9:]

    @first_step
    def _():
        assemble_attn(0, place[0], place[1], own, near, far, wqkv, wm, sm)
        project(x, wqkv, sm, qkv)

    crops = [pl.program_id(0) * STEP_CROPS + i for i in range(STEP_CROPS)]
    attend_crops(place, crops, range(STEP_CROPS), qkv, packed, probs, out)

    @last_step
    def _():
        mix(out, qkv, (2, 5), sm, mixed)
        for orient in range(2):
            value[orient] = qkv[orient * 3 + 2, :ROWS, :].astype(bf16)
        mixer(x, mixed, wm, sm, middle)


def ff_fwd_kernel(place, middle, sm, *refs):
    own, near, far = refs[0:2], refs[2:5], refs[5:8]
    out, we, wr = refs[8:]

    @first_step
    def _():
        assemble_ff(0, place[0], place[1], own, near, far, we, wr)

    out[...] = ff_forward(middle[...], we, wr, sm)


def top_kernel(place, x, cotangent, *refs):
    attn_own, ff_own, rest = refs[0:3], refs[3:5], refs[5]
    (output, grad_out, grads) = refs[6:9]
    (wqkv, wm, sm, we, wr, qkv, out, packed, probs, mixed, middle, g, slope, e, e_low,
     acc_e, acc_r, acc_q, acc_m, vec) = refs[9:]

    assemble_top(place[0], attn_own, ff_own, rest, wqkv, wm, sm, we, wr)
    clear(acc_e, acc_r, acc_q, acc_m, vec)
    project(x, wqkv, sm, qkv)

    def ahead(i, _):
        crops = [i * STEP_CROPS + j for j in range(STEP_CROPS)]
        attend_crops(place, crops, crops, qkv, packed, probs, out)
        return 0

    lax.fori_loop(0, CROPS // STEP_CROPS, ahead, 0)
    mix(out, qkv, (2, 5), sm, mixed)
    mixer(x, mixed, wm, sm, middle)
    for rows in chunks():
        gs, slopes = {}, {}
        output[rows, :] = ff_forward(middle[rows, :], we, wr, sm, gs, slopes).astype(bf16)
        for s in range(4):
            g[rows, s * 256 : (s + 1) * 256] = gs[s]
            slope[rows, s * 256 : (s + 1) * 256] = slopes[s]
    for rows in chunks():
        held = lambda s: (g[rows, s * 256 : (s + 1) * 256], slope[rows, s * 256 : (s + 1) * 256])
        middle_here = middle[rows, :]
        middle[rows, :] = ff_backward(cotangent[rows, :].astype(f32), middle_here, we, wr, sm, acc_e, acc_r, vec, held)
    em = out
    mixer_back(middle, mixed, wm, acc_m, vec, em)

    def behind(i, _):
        crops = [i * STEP_CROPS + j for j in range(STEP_CROPS)]
        attend_crops_back(crops, crops, em, packed, probs, e)
        return 0

    lax.fori_loop(0, CROPS // STEP_CROPS, behind, 0)
    mix_back(em, qkv, (2, 5), sm, e, e_low, vec)
    project_back(middle, x, e_low, wqkv, sm, acc_q, vec, grad_out)
    write_parts(attn_pieces(acc_q, acc_m, jnp.sum(vec[...], axis=1)) + ff_pieces(acc_e, acc_r), 0, grads)


def ff_bwd_kernel(place, grad, middle, we, wr, sm, grad_mid, keep, give, vec, acc_e, acc_r):
    @first_step
    def _():
        clear(acc_e, acc_r, vec)

    grad_mid[...] = ff_backward(grad[...], middle[...], we, wr, sm, acc_e, acc_r, vec)

    @last_step
    def _():
        write_halves(place[1], ff_pieces(acc_e, acc_r), keep, give)


def attn_bwd_kernel(place, grad, x, packed, probs, mixed, value, wqkv, wm, sm, vec_in, patch_grad, keep, give, em, e, e_low, acc_q, acc_m, vec):
    @first_step
    def _():
        clear(acc_q, acc_m)
        vec[...] = vec_in[...]
        mixer_back(grad, mixed, wm, acc_m, vec, em)

    crops = [pl.program_id(0) * STEP_CROPS + i for i in range(STEP_CROPS)]
    attend_crops_back(crops, range(STEP_CROPS), em, packed, probs, e)

    @last_step
    def _():
        mix_back(em, value, (0, 1), sm, e, e_low, vec)
        project_back(grad, x, e_low, wqkv, sm, acc_q, vec, patch_grad)
        write_halves(place[1], attn_pieces(acc_q, acc_m, jnp.sum(vec[...], axis=1)), keep, give)


def whole(shape):
    return pl.BlockSpec(shape, lambda i, *_: (0,) * len(shape))


def rows_of(lanes, rows=CHUNK):
    return pl.BlockSpec((rows, lanes), lambda i, *_: (i, 0))


def crop_spec(*dims):
    return pl.BlockSpec((STEP_CROPS, 4) + dims, lambda i, *_: (i, 0, 0, 0))


def of_layer(layer, *dims):
    return pl.BlockSpec((1,) + dims, lambda i, *_: (layer,) + (0,) * len(dims))


def attn_specs(layer):
    return [of_layer(layer, 192, D), of_layer(layer, 64, D), whole((2, 32, D))]


def ff_specs(layer):
    return [of_layer(layer, D, D), of_layer(layer, 64, FF)]


def half_specs(rows):
    return [whole((rows, D))] * 6


def shape(dims, dtype=bf16):
    return jax.ShapeDtypeStruct(dims, dtype)


def params(micros):
    return dict(
        compiler_params=pltpu.CompilerParams(
            vmem_limit_bytes=58 * 1024 * 1024, dimension_semantics=("arbitrary",)
        ),
        cost_estimate=pl.CostEstimate(flops=int(micros * 1e9), bytes_accessed=1 << 20, transcendentals=0),
    )


v = pltpu.VMEM


def attn_fwd_call(place, x, unit):
    rows = unit[-1].shape[0]
    return pl.pallas_call(
        attn_fwd_kernel,
        grid_spec=pltpu.PrefetchScalarGridSpec(
            num_scalar_prefetch=1,
            grid=(CROPS // STEP_CROPS,),
            in_specs=[whole((ROWS, D))] + attn_specs(0) + half_specs(rows),
            out_specs=[whole((ROWS, D)), crop_spec(WIN, 384), crop_spec(WIN, 512), whole((ROWS, D)), whole((2, ROWS, 128)), whole((768, D)), whole((D, D)), whole((32, D))],
            scratch_shapes=[v((6, HELD, 128), f32), v((2, HELD, 128), f32)],
        ),
        out_shape=[shape((ROWS, D), f32), shape((CROPS, 4, WIN, 384)), shape((CROPS, 4, WIN, 512)), shape((ROWS, D)), shape((2, ROWS, 128)), shape((768, D)), shape((D, D)), shape((32, D), f32)],
        name="attn_fwd",
        **params(10),
    )(place, x, *unit)


def ff_fwd_call(place, middle, sm, unit):
    return pl.pallas_call(
        ff_fwd_kernel,
        grid_spec=pltpu.PrefetchScalarGridSpec(
            num_scalar_prefetch=1,
            grid=(ROWS // CHUNK,),
            in_specs=[rows_of(D), whole((32, D))] + ff_specs(0) + half_specs(HALF_FF),
            out_specs=[rows_of(D), whole((4, D, D)), whole((D, FF))],
        ),
        out_shape=[shape((ROWS, D), f32), shape((4, D, D)), shape((D, FF))],
        name="ff_fwd",
        **params(6),
    )(place, middle, sm, *unit)


def top_call(place, x, cotangent, weights, parts, r):
    dp, _, rest_rows, _ = weights[-1].shape
    return pl.pallas_call(
        top_kernel,
        grid_spec=pltpu.PrefetchScalarGridSpec(
            num_scalar_prefetch=1,
            grid=(1,),
            in_specs=[whole((ROWS, D)), whole((ROWS, D))] + attn_specs(1) + ff_specs(1) + [whole((dp, 3, rest_rows, D))],
            out_specs=[whole((ROWS, D)), whole((ROWS, D)), whole((parts, 4, r, D))],
            scratch_shapes=[
                v((768, D), bf16), v((D, D), bf16), v((32, D), f32), v((4, D, D), bf16), v((D, FF), bf16),
                v((6, HELD, 128), f32), v((2, HELD, 128), f32), v((CROPS, 4, WIN, 384), bf16), v((CROPS, 4, WIN, 512), bf16),
                v((ROWS, D), bf16), v((ROWS, D), f32), v((ROWS, FF), bf16), v((ROWS, FF), bf16),
                v((6, HELD, 128), f32), v((ROWS, 768), bf16),
                v((4, D, D), f32), v((4, D, D), f32), v((768, D), f32), v((D, D), f32), v((32, CROPS, D), f32),
            ],
        ),
        out_shape=[shape((ROWS, D)), shape((ROWS, D), f32), shape((parts, 4, r, D))],
        name="top_block",
        **params(30),
    )(place, x, cotangent, *weights)


def ff_bwd_call(place, grad, middle, we, wr, sm, parts, r):
    return pl.pallas_call(
        ff_bwd_kernel,
        grid_spec=pltpu.PrefetchScalarGridSpec(
            num_scalar_prefetch=1,
            grid=(ROWS // CHUNK,),
            in_specs=[rows_of(D), rows_of(D), whole((4, D, D)), whole((D, FF)), whole((32, D))],
            out_specs=[rows_of(D)] + [whole((parts, 4, r, D))] * 2 + [whole((32, CROPS, D))],
            scratch_shapes=[v((4, D, D), f32), v((4, D, D), f32)],
        ),
        out_shape=[shape((ROWS, D), f32)] + [shape((parts, 4, r, D))] * 2 + [shape((32, CROPS, D), f32)],
        name="ff_bwd",
        **params(10),
    )(place, grad, middle, we, wr, sm)


def attn_bwd_call(place, grad, x, packed, probs, mixed, value, wqkv, wm, sm, vec):
    return pl.pallas_call(
        attn_bwd_kernel,
        grid_spec=pltpu.PrefetchScalarGridSpec(
            num_scalar_prefetch=1,
            grid=(CROPS // STEP_CROPS,),
            in_specs=[whole((ROWS, D)), whole((ROWS, D)), crop_spec(WIN, 384), crop_spec(WIN, 512), whole((ROWS, D)), whole((2, ROWS, 128)), whole((768, D)), whole((D, D)), whole((32, D)), whole((32, CROPS, D))],
            out_specs=[whole((ROWS, D))] + [whole((1, 4, LOW_ROWS // 2, D))] * 2,
            scratch_shapes=[v((2, HELD, 128), f32), v((6, HELD, 128), f32), v((ROWS, 768), bf16), v((768, D), f32), v((D, D), f32), v((32, CROPS, D), f32)],
        ),
        out_shape=[shape((ROWS, D))] + [shape((1, 4, LOW_ROWS // 2, D))] * 2,
        name="attn_bwd",
        **params(16),
    )(place, grad, x, packed, probs, mixed, value, wqkv, wm, sm, vec)


def to_rows(x):
    return jnp.transpose(x, (1, 2, 0, 3)).reshape(ROWS, D)


def from_rows(x):
    return jnp.transpose(x.reshape(GRID, GRID, CROPS, D), (2, 0, 1, 3))


def pack_kernel(place, qkv, mixer_t, gain, shift, entry, taps, branch, hidden_bias, expand, reduce_t, half_a, half_f, vec, unit):
    me, core = place[0], place[1]
    lane = lax.broadcasted_iota(jnp.int32, (18, D), 1)
    row = lax.broadcasted_iota(jnp.int32, (14, D), 0)
    for layer in range(2):
        rows = jnp.concatenate(
            [ref[layer].astype(f32) for ref in (gain, shift, entry)] + [taps[:, layer].astype(f32), branch[layer].astype(f32)], axis=0
        )
        vectors = jnp.where(lane // 64 == me, jnp.concatenate([rows] * 4, axis=1), 0.0)
        hidden_rows = jnp.where(row == me, hidden_bias[layer : layer + 1].astype(f32), 0.0)
        vec[layer] = jnp.concatenate([vectors, hidden_rows], axis=0).astype(bf16)
    half_a[0:96] = qkv[0, pl.ds(pl.multiple_of(96 * core, 32), 96)]
    half_a[96:128] = mixer_t[0, pl.ds(pl.multiple_of(32 * core, 32), 32)]
    half_a[128:144] = vec[0, pl.ds(pl.multiple_of(16 * core, 16), 16)]
    half_f[0:128] = expand[0, pl.ds(pl.multiple_of(128 * core, 128), 128)]
    for c in range(4):
        half_f[128 + 32 * c : 160 + 32 * c] = reduce_t[0, pl.ds(pl.multiple_of(32 * core, 32), 32), c * 256 : (c + 1) * 256]
    unit[0:192] = qkv[1]
    unit[192:256] = mixer_t[1]
    unit[256:288] = vec[1]
    unit[288:544] = expand[1]
    for c in range(4):
        unit[544 + 64 * c : 608 + 64 * c] = reduce_t[1, :, c * 256 : (c + 1) * 256]
    if unit.shape[0] > UNIT:
        unit[UNIT:] = jnp.zeros((unit.shape[0] - UNIT, D), bf16)
    r = half_a.shape[0] - HALF_ATTN
    half_a[HALF_ATTN:] = unit[pl.ds(pl.multiple_of(place[3] * r, 16), r)]


def local_call(kernel, name, place, arrays, outs, scratch=()):
    return pl.pallas_call(
        kernel,
        grid_spec=pltpu.PrefetchScalarGridSpec(
            num_scalar_prefetch=1,
            grid=(1,),
            in_specs=[whole(x.shape) for x in arrays],
            out_specs=[whole(dims) for dims, _ in outs],
            scratch_shapes=list(scratch),
        ),
        out_shape=[shape(dims, dtype) for dims, dtype in outs],
        name=name,
        **params(1),
    )(place, *arrays)


def turn_mp(x, k):
    n = lax.axis_size("mp")
    return lax.ppermute(x, "mp", [(i, (i + k) % n) for i in range(n)])


def swap_dp(x, bits):
    n = lax.axis_size("dp")
    return lax.ppermute(x, "dp", [(i, i ^ bits) for i in range(n)])


def turn_all(x):
    return [turn_mp(x, k) for k in (1, 2, 3)]


def swap_core(xs):
    return [swap_dp(x, 1) for x in xs]


def pick(x, at):
    return lax.dynamic_index_in_dim(x, at, 0, keepdims=False)


def add_up(xs):
    total = xs[0].astype(f32)
    for x in xs[1:]:
        total = total + x.astype(f32)
    return total


def to_planes(keep, got, at):
    total = add_up([keep, got]).astype(bf16)
    return [pick(total, at ^ b) for b in range(keep.shape[0])]


def swap_planes(parts):
    return [parts[0]] + [swap_dp(part, 2 * b) for b, part in enumerate(parts) if b]


def to_shards(xs, me):
    total = add_up(xs)
    low = total.astype(bf16)
    return [pick(total, me)] + [pick(low, (me + k) % 4) for k in (1, 2, 3)]


def turn_shards(parts):
    return [parts[0]] + [turn_mp(part, k) for k, part in enumerate(parts) if k]


def unpack_kernel(planes, cut_f, cut_t, place, *refs):
    mine, other = refs[:planes], refs[planes : 2 * planes]
    packed, mixer_g, expand, reduce_g, gain, shift, entry, taps, branch, hidden_g, held, held_t = refs[2 * planes :]
    me, core = place[0], place[1]
    r_f, r_t = cut_t - cut_f, mine[0].shape[0] - cut_t
    for which, parts in ((core, mine), (1 - core, other)):
        total = parts[0][:cut_f].astype(f32)
        for part in parts[1:]:
            total = total + part[:cut_f].astype(f32)
        held[which, :cut_f] = total
        for b in range(planes):
            at = place[2] ^ b
            held[which, pl.ds(pl.multiple_of(cut_f + at * r_f, 16), r_f)] = parts[b][cut_f:cut_t].astype(f32)
            held_t[pl.ds(pl.multiple_of((2 * at + which) * r_t, 16), r_t)] = parts[b][cut_t:].astype(f32)

    def rows(which, lo, hi):
        if which is None:
            return held_t[lo:hi]
        start, half = which
        out = []
        for c in range(2):
            a, b = max(lo, c * half), min(hi, (c + 1) * half)
            if a < b:
                out.append(held[c, start + a - c * half : start + b - c * half])
        return out[0] if len(out) == 1 else jnp.concatenate(out, axis=0)

    low_a, low_f = (0, cut_f), (cut_f, planes * r_f)
    for layer, attn, ff, ff_at in ((0, low_a, low_f, 0), (1, None, None, 288)):
        packed[layer] = rows(attn, 0, 192)
        mixer_g[layer] = rows(attn, 192, 256)
        expand[layer] = rows(ff, ff_at, ff_at + 256)
        for c in range(4):
            at = ff_at + 256 + 64 * c
            reduce_g[layer, :, c * 256 : (c + 1) * 256] = rows(ff, at, at + 64)
        vectors = rows(attn, 256, 288)
        mine_lanes = vectors[:, :64]
        for s in range(1, 4):
            mine_lanes = jnp.where(me == s, vectors[:, 64 * s : 64 * (s + 1)], mine_lanes)
        gain[layer] = mine_lanes[GAIN : GAIN + 2]
        shift[layer] = mine_lanes[SHIFT : SHIFT + 2]
        entry[layer] = mine_lanes[ENTRY : ENTRY + 2]
        branch[layer] = mine_lanes[BRANCH : BRANCH + 2]
        for t in range(10):
            taps[t, layer : layer + 1] = mine_lanes[TAPS + t : TAPS + t + 1]
        row = vectors[HIDDEN : HIDDEN + 1]
        for s in range(1, 4):
            row = jnp.where(me == s, vectors[HIDDEN + s : HIDDEN + s + 1], row)
        hidden_g[layer : layer + 1] = row


def body(patches, validity, norm_gain, norm_shift, qkv_weight, entry_bias, stencil, mixer_weight, branch_bias, expand_weight, hidden_bias, reduce_weight, cotangent):
    dp = lax.axis_size("dp")
    planes = dp // 2
    me, at_dp = lax.axis_index("mp"), lax.axis_index("dp")
    heights = jnp.sum(validity[:, :, 0], axis=1)
    widths = jnp.sum(validity[:, 0, :], axis=1)
    place = jnp.stack([me, at_dp % 2, at_dp // 2, at_dp]).astype(jnp.int32)
    sizes = jnp.concatenate([jnp.stack([me, at_dp % 2]), jnp.stack([heights, widths], axis=1).reshape(-1)]).astype(jnp.int32)

    qkv_t = jnp.transpose(qkv_weight, (0, 2, 3, 1)).reshape(2, 192, D)
    mixer_t = jnp.transpose(mixer_weight, (0, 2, 1))
    reduce_t = jnp.transpose(reduce_weight, (0, 2, 1))
    vectors = (norm_gain, norm_shift, entry_bias, jnp.transpose(stencil, (1, 0, 2)), branch_bias, hidden_bias)

    arrays = [qkv_t, mixer_t, norm_gain, norm_shift, entry_bias, jnp.transpose(stencil, (1, 0, 2)), branch_bias, hidden_bias, expand_weight, reduce_t]
    r_t, r_f = part_rows(UNIT, dp), part_rows(FF_ROWS, dp)
    outs = [(HALF_ATTN + r_t, D), (HALF_FF, D), (2, 32, D)]
    half_a0, half_f0, vec = local_call(
        pack_kernel, "pack", place, arrays, [(dims, bf16) for dims in outs], [v((dp * r_t, D), bf16)]
    )
    attn_own, ff_own = [qkv_t, mixer_t, vec], [expand_weight, reduce_t]

    near_a0 = turn_all(half_a0)
    near_1 = jnp.stack([x[HALF_ATTN:] for x in near_a0])
    near_f0 = turn_all(half_f0)
    far_a0 = swap_core(near_a0)
    x, top_grad = to_rows(patches), to_rows(cotangent)
    near_1, x = lax.optimization_barrier((near_1, x))
    rest_1 = lax.all_gather(near_1, "dp", axis=0, tiled=False)
    middle, packed, probs, mixed, value, wqkv, wm, sm = attn_fwd_call(sizes, x, attn_own + near_a0 + far_a0)
    near_f0, middle = lax.optimization_barrier((near_f0, middle))
    far_f0 = swap_core(near_f0)
    state, we, wr = ff_fwd_call(sizes, middle, sm, ff_own + near_f0 + far_f0)
    output, grad, grads_1 = top_call(sizes, state, top_grad, attn_own + ff_own + [rest_1], dp, r_t)
    sums_1 = lax.psum_scatter(grads_1, "dp", scatter_dimension=0, tiled=False)

    grad_mid, keep_f, give_f, vec = ff_bwd_call(place, grad, middle, we, wr, sm, planes, r_f)
    got_f = swap_dp(give_f, 1)
    patch_grad, keep_a, give_a = attn_bwd_call(place, grad_mid, x, packed, probs, mixed, value, wqkv, wm, sm, vec)
    got_f, keep_a, give_a = lax.optimization_barrier((got_f, keep_a, give_a))

    got_a = swap_dp(give_a, 1)
    planes_f = swap_planes(to_planes(keep_f, got_f, place[2]))
    shards_a = to_shards([keep_a[0], got_a[0]], me)
    mp_a = turn_shards(shards_a)
    planes_f, sums_1 = lax.optimization_barrier((planes_f, sums_1, shards_a))[:2]
    low = add_up(planes_f).astype(bf16)
    mp_f = turn_shards(to_shards([jnp.concatenate([low, sums_1], axis=1)], me))
    share = jnp.concatenate([add_up(mp_a), add_up(mp_f)], axis=0).astype(bf16)
    mine = swap_planes([share] * planes)
    other = swap_core(mine)
    outs = [(2, 192, D), (2, 64, D), (2, D, D), (2, 64, FF), (2, 2, 64), (2, 2, 64), (2, 2, 64), (10, 2, 64), (2, 2, 64), (2, D)]
    cut_f = LOW_ROWS // 2
    cut_t = cut_f + r_f
    held = [v((2, cut_f + planes * r_f, D), f32), v((dp * r_t, D), f32)]
    packed_g, mixer_g, expand_g, reduce_g, gain_g, shift_g, entry_g, taps_g, branch_g, hidden_g = local_call(
        functools.partial(unpack_kernel, planes, cut_f, cut_t), "unpack", place, mine + other, [(dims, f32) for dims in outs], held
    )
    return (
        from_rows(output), from_rows(patch_grad), gain_g, shift_g,
        jnp.transpose(packed_g.reshape(2, 3, 64, D), (0, 3, 1, 2)), entry_g, jnp.transpose(taps_g, (1, 0, 2)),
        jnp.transpose(mixer_g, (0, 2, 1)), branch_g, expand_g, hidden_g, jnp.transpose(reduce_g, (0, 2, 1)),
    )


def solution(mesh):
    crops = P(("dp", "mp"), None, None, None)
    lanes = P(None, None, "mp")
    deep = P(None, None, None, "mp")
    return jax.shard_map(
        body,
        mesh=mesh,
        in_specs=(crops, P(("dp", "mp"), None, None), lanes, lanes, deep, lanes, lanes, lanes, lanes, lanes, P(None, "mp"), lanes, crops),
        out_specs=(crops, crops, lanes, lanes, deep, lanes, lanes, lanes, lanes, lanes, P(None, "mp"), lanes),
        check_vma=False,
    )
```

profile of v0, /device:TPU:0, one launch (start us, length us, event | category | flops | bytes accessed | tf_op | source)
XLA Modules:
  0.0 170.8 jit_solution(6761640201255324248)
XLA Ops:
  7.8 2.8 %pack.1 = (bf16[256,256]{1,0:T(8,128)(2,1)}, bf16[256,256]{1,0:T(8,128)(2,1)}, bf16[2,32,256]{2,1,0:T(8,128)(2,1)}) custom-call(s32[4]{0:T(128)} %pad_add_fusion.2.place, bf16[2,192,256]{2,1,0:T(8,128)(2,1)} %bitcast.80, bf16[2,64,256]{2,1,0:T(8,128)(2,1)} %bitcast.83, bf16[2,2,64]{2,1,0:T(2,128)(2,1)} %gain.1, bf16[2,2,64]{2,1,0:T(2,128)(2,1)} %shift.1, ...), custom_call_target="tpu_custom_call" | custom-call | flops 1000000000 | bytes 1048576 | tf_op jit(solution)/shard_map/pack/pallas_call | solution.py:791
  10.7 5.0 %collective-permute-start.5 = (bf16[256,256]{1,0:T(8,128)(2,1)}, bf16[256,256]{1,0:T(8,128)(2,1)S(1)}, u32[]{:S(2)}, u32[]{:S(2)}) collective-permute-start(bf16[256,256]{1,0:T(8,128)(2,1)} %get-tuple-element.61), channel_id=1, source_target_pairs={{0,3},{1,0},{2,1},{3,2},{4,7},{5,4},{6,5},{7,6},{8,11},{9,8},{10,9... | collective-permute-start | bytes 393224 | tf_op jit(solution)/shard_map/ppermute | solution.py:808
  15.7 1.0 collective-permute-start.3
  16.7 3.2 %collective-permute-done.5.refs_5_ = bf16[256,256]{1,0:T(8,128)(2,1)S(1)} collective-permute-done((bf16[256,256]{1,0:T(8,128)(2,1)}, bf16[256,256]{1,0:T(8,128)(2,1)S(1)}, u32[]{:S(2)}, u32[]{:S(2)}) %collective-permute-start.5) | collective-permute-done | bytes 131104 | tf_op jit(solution)/shard_map/ppermute | solution.py:808
  19.9 7.2 %collective-permute-done.4.refs_4_ = bf16[256,256]{1,0:T(8,128)(2,1)S(1)} collective-permute-done((bf16[256,256]{1,0:T(8,128)(2,1)}, bf16[256,256]{1,0:T(8,128)(2,1)S(1)}, u32[]{:S(2)}, u32[]{:S(2)}) %collective-permute-start.4) | collective-permute-done | bytes 131104 | tf_op jit(solution)/shard_map/ppermute | solution.py:808
  28.8 1.9 %collective-permute-start.1 = (bf16[256,256]{1,0:T(8,128)(2,1)}, bf16[256,256]{1,0:T(8,128)(2,1)S(1)}, u32[]{:S(2)}, u32[]{:S(2)}) collective-permute-start(bf16[256,256]{1,0:T(8,128)(2,1)} %get-tuple-element.60), channel_id=1, source_target_pairs={{0,2},{1,3},{2,0},{3,1},{4,6},{5,7},{6,4},{7,5},{8,10},{9,11},{10,... | collective-permute-start | bytes 393224 | tf_op jit(solution)/shard_map/ppermute | solution.py:808
  32.4 2.8 %collective-permute-start.2 = (bf16[256,256]{1,0:T(8,128)(2,1)}, bf16[256,256]{1,0:T(8,128)(2,1)S(1)}, u32[]{:S(2)}, u32[]{:S(2)}) collective-permute-start(bf16[256,256]{1,0:T(8,128)(2,1)} %get-tuple-element.60), channel_id=1, source_target_pairs={{0,3},{1,0},{2,1},{3,2},{4,7},{5,4},{6,5},{7,6},{8,11},{9,8},{10,9... | collective-permute-start | bytes 393224 | tf_op jit(solution)/shard_map/ppermute | solution.py:808
  35.9 13.1 %attn_fwd.1 = (f32[1568,256]{1,0:T(8,128)}, bf16[8,4,112,384]{3,2,1,0:T(8,128)(2,1)}, bf16[8,4,112,512]{3,2,1,0:T(8,128)(2,1)}, bf16[1568,256]{1,0:T(8,128)(2,1)...) custom-call(s32[18]{0:T(128)} %pad_add_fusion.1.place, ...), custom_call_target="tpu_custom_call" | custom-call | flops 10000000000 | bytes 1048576 | tf_op jit(solution)/shard_map/attn_fwd/pallas_call | solution.py:668
  51.6 6.2 %ff_fwd.1 = (f32[1568,256]{1,0:T(8,128)}, bf16[4,256,256]{2,1,0:T(8,128)(2,1)}, bf16[256,1024]{1,0:T(8,128)(2,1)}) custom-call(s32[18]{0:T(128)} %pad_add_fusion.1.place, f32[1568,256]{1,0:T(8,128)} %get-tuple-element.65.middle, f32[32,256]{1,0:T(8,128)} %get-tuple-element.66.sm, bf16[2,256,256]{2,1,0:T(8,128)(2,1)} %refs_3_.1, ...), custom_call_target="tpu_custom_call" | custom-call | flops 6000000000 | bytes 1048576 | tf_op jit(solution)/shard_map/ff_fwd/pallas_call | solution.py:684
  57.8 34.0 %top_block.1 = (bf16[1568,256]{1,0:T(8,128)(2,1)}, f32[1568,256]{1,0:T(8,128)}, bf16[8,4,112,256]{3,2,1,0:T(8,128)(2,1)}) custom-call(s32[18]{0:T(128)} %pad_add_fusion.1.place, f32[1568,256]{1,0:T(8,128)} %get-tuple-element.70.x, bf16[1568,256]{1,0:T(8,128)(2,1)} %bitcast.74, bf16[2,192,256]{2,1,0:T(8,128)(2,1)} %bitcast.82, bf16[2,64,256]{2,1,0:T(8,128)(2,1)} %bitcast.85, ...), custom_call_target="tpu_custom_call" | custom-call | flops 30000001024 | bytes 1048576 | tf_op jit(solution)/shard_map/top_block/pallas_call | solution.py:700
  91.8 10.6 %ff_bwd.1 = (f32[1568,256]{1,0:T(8,128)}, bf16[4,4,64,256]{3,2,1,0:T(8,128)(2,1)}, bf16[4,4,64,256]{3,2,1,0:T(8,128)(2,1)}, f32[32,8,256]{2,1,0:T(8,128)}) custom-call(s32[4]{0:T(128)} %pad_add_fusion.2.place, f32[1568,256]{1,0:T(8,128)} %get-tuple-element.73.grad, f32[1568,256]{1,0:T(8,128)} %get-tuple-element.65.middle, ...), custom_call_target="tpu_custom_call" | custom-call | flops 10000000000 | bytes 1048576 | tf_op jit(solution)/shard_map/ff_bwd/pallas_call | solution.py:722
  102.7 17.6 %attn_bwd.1 = (bf16[1568,256]{1,0:T(8,128)(2,1)}, bf16[1,4,144,256]{3,2,1,0:T(8,128)(2,1)}, bf16[1,4,144,256]{3,2,1,0:T(8,128)(2,1)}) custom-call(s32[4]{0:T(128)} %pad_add_fusion.2.place, f32[1568,256]{1,0:T(8,128)} %get-tuple-element.76.grad, bf16[1568,256]{1,0:T(8,128)(2,1)} %bitcast.76, bf16[8,4,112,384]{3,2,1,0:T(8,128)(2,1)} %get-tuple-element.77.packed, ...), custom_call_target="tpu_custom_call" | custom-call | flops 16000000000 | bytes 1048576 | tf_op jit(solution)/shard_map/attn_bwd/pallas_call | solution.py:738
  120.8 1.3 collective-permute-done.13
  122.3 1.2 collective-permute-start.15
  123.5 2.6 %collective-permute-start.16 = (bf16[144,256]{1,0:T(8,128)(2,1)S(1)}, bf16[144,256]{1,0:T(8,128)(2,1)S(1)}, u32[]{:S(2)}, u32[]{:S(2)}) collective-permute-start(bf16[144,256]{1,0:T(8,128)(2,1)S(1)} %get-tuple-element.120), channel_id=1, source_target_pairs={{0,3},{1,0},{2,1},{3,2},{4,7},{5,4},{6,5},{7,6},{8,11},{9,8},{10,9... | collective-permute-start | bytes 221192 | tf_op jit(solution)/shard_map/ppermute | solution.py:808
  126.2 1.6 collective-permute-start.17
  127.7 1.5 collective-permute-start.18
  129.3 2.4 %collective-permute-start.19 = (bf16[4,64,256]{2,1,0:T(8,128)(2,1)S(1)}, bf16[4,64,256]{2,1,0:T(8,128)(2,1)S(1)}, u32[]{:S(2)}, u32[]{:S(2)}) collective-permute-start(bf16[4,64,256]{2,1,0:T(8,128)(2,1)S(1)} %get-tuple-element.112), channel_id=1, source_target_pairs={{0,24},{4,28},{8,16},{12,20},{16,8},{20,12},{24,0},{28,4},{1,25},{... | collective-permute-start | bytes 393224 | tf_op jit(solution)/shard_map/ppermute | solution.py:813
  132.1 2.4 %collective-permute-done.18 = bf16[4,64,256]{2,1,0:T(8,128)(2,1)S(1)} collective-permute-done((bf16[4,64,256]{2,1,0:T(8,128)(2,1)S(1)}, bf16[4,64,256]{2,1,0:T(8,128)(2,1)S(1)}, u32[]{:S(2)}, u32[]{:S(2)}) %collective-permute-start.18) | collective-permute-done | bytes 131104 | tf_op jit(solution)/shard_map/ppermute | solution.py:813
  134.6 1.1 collective-permute-done.19
  135.8 0.9 fusion.7
  136.7 1.5 collective-permute-start.20
  138.2 1.7 collective-permute-start.21
  139.9 2.2 %collective-permute-start.22 = (bf16[176,256]{1,0:T(8,128)(2,1)S(1)}, bf16[176,256]{1,0:T(8,128)(2,1)S(1)}, u32[]{:S(2)}, u32[]{:S(2)}) collective-permute-start(bf16[176,256]{1,0:T(8,128)(2,1)S(1)} %get-tuple-element.118), channel_id=1, source_target_pairs={{0,3},{1,0},{2,1},{3,2},{4,7},{5,4},{6,5},{7,6},{8,11},{9,8},{10,9... | collective-permute-start | bytes 270344 | tf_op jit(solution)/shard_map/ppermute | solution.py:808
  142.1 2.0 %collective-permute-done.20 = bf16[176,256]{1,0:T(8,128)(2,1)S(1)} collective-permute-done((bf16[176,256]{1,0:T(8,128)(2,1)S(1)}, bf16[176,256]{1,0:T(8,128)(2,1)S(1)}, u32[]{:S(2)}, u32[]{:S(2)}) %collective-permute-start.20) | collective-permute-done | bytes 90144 | tf_op jit(solution)/shard_map/ppermute | solution.py:808
  144.1 2.8 %collective-permute-done.21 = bf16[176,256]{1,0:T(8,128)(2,1)S(1)} collective-permute-done((bf16[176,256]{1,0:T(8,128)(2,1)S(1)}, bf16[176,256]{1,0:T(8,128)(2,1)S(1)}, u32[]{:S(2)}, u32[]{:S(2)}) %collective-permute-start.21) | collective-permute-done | bytes 90144 | tf_op jit(solution)/shard_map/ppermute | solution.py:808
  146.9 0.9 fusion.2
  147.8 0.9 collective-permute-start.23
  149.2 2.1 %collective-permute-start.25 = (bf16[320,256]{1,0:T(8,128)(2,1)S(1)}, bf16[320,256]{1,0:T(8,128)(2,1)S(1)}, u32[]{:S(2)}, u32[]{:S(2)}) collective-permute-start(bf16[320,256]{1,0:T(8,128)(2,1)S(1)} %pad_maximum_fusion.1.refs_0_), channel_id=1, source_target_pairs={{0,24},{4,28},{8,16},{12,20},{16,8},{20,12},{24,0},{28,4},{1,25},{... | collective-permute-start | bytes 491528 | tf_op jit(solution)/shard_map/ppermute | solution.py:813
  151.4 3.3 %collective-permute-done.23.refs_1_ = bf16[320,256]{1,0:T(8,128)(2,1)S(1)} collective-permute-done((bf16[320,256]{1,0:T(8,128)(2,1)S(1)}, bf16[320,256]{1,0:T(8,128)(2,1)S(1)}, u32[]{:S(2)}, u32[]{:S(2)}) %collective-permute-start.23) | collective-permute-done | bytes 163872 | tf_op jit(solution)/shard_map/ppermute | solution.py:813
  154.6 3.0 %collective-permute-done.24.refs_2_ = bf16[320,256]{1,0:T(8,128)(2,1)S(1)} collective-permute-done((bf16[320,256]{1,0:T(8,128)(2,1)S(1)}, bf16[320,256]{1,0:T(8,128)(2,1)S(1)}, u32[]{:S(2)}, u32[]{:S(2)}) %collective-permute-start.24) | collective-permute-done | bytes 163872 | tf_op jit(solution)/shard_map/ppermute | solution.py:813
  160.4 3.6 %unpack.1 = (f32[2,192,256]{2,1,0:T(8,128)}, f32[2,64,256]{2,1,0:T(8,128)}, f32[2,256,256]{2,1,0:T(8,128)}, f32[2,64,1024]{2,1,0:T(8,128)}, f32[2,2,64]{2,1,0:T(...) custom-call(s32[4]{0:T(128)} %pad_add_fusion.2.place, ...), custom_call_target="tpu_custom_call" | custom-call | flops 1000000000 | bytes 1048576 | tf_op jit(solution)/shard_map/unpack/pallas_call | solution.py:791
  (107 shorter events, 11.9 us)
Async XLA Ops:
  7.2 50.6 %all-gather.3.cloned.1.call-start = ((), (), s32[]{:S(2)}) async-start(), calls=%async_computation.2 | async-start | bytes 1548288 | tf_op jit(solution)/shard_map/all_gather | solution.py:932
  10.7 9.3 %collective-permute-start.5 = (bf16[256,256]{1,0:T(8,128)(2,1)}, bf16[256,256]{1,0:T(8,128)(2,1)S(1)}, u32[]{:S(2)}, u32[]{:S(2)}) collective-permute-start(bf16[256,256]{1,0:T(8,128)(2,1)} %get-tuple-element.61), channel_id=1, source_target_pairs={{0,3},{1,0},{2,1},{3,2},{4,7},{5,4},{6,5},{7,6},{8,11},{9,8},{10,9... | collective-permute-start | bytes 393224 | tf_op jit(solution)/shard_map/ppermute | solution.py:808
  15.7 11.4 %collective-permute-start.4 = (bf16[256,256]{1,0:T(8,128)(2,1)}, bf16[256,256]{1,0:T(8,128)(2,1)S(1)}, u32[]{:S(2)}, u32[]{:S(2)}) collective-permute-start(bf16[256,256]{1,0:T(8,128)(2,1)} %get-tuple-element.61), channel_id=1, source_target_pairs={{0,2},{1,3},{2,0},{3,1},{4,6},{5,7},{6,4},{7,5},{8,10},{9,11},{10,... | collective-permute-start | bytes 393224 | tf_op jit(solution)/shard_map/ppermute | solution.py:808
  15.7 11.4 %collective-permute-start.3 = (bf16[256,256]{1,0:T(8,128)(2,1)}, bf16[256,256]{1,0:T(8,128)(2,1)S(1)}, u32[]{:S(2)}, u32[]{:S(2)}) collective-permute-start(bf16[256,256]{1,0:T(8,128)(2,1)} %get-tuple-element.61), channel_id=1, source_target_pairs={{0,1},{1,2},{2,3},{3,0},{4,5},{5,6},{6,7},{7,4},{8,9},{9,10},{10,1... | collective-permute-start | bytes 393224 | tf_op jit(solution)/shard_map/ppermute | solution.py:808
  27.9 107.8 %reduce-scatter.2.cloned.1.call-start = ((), (), s32[]{:S(2)}) async-start(), calls=%async_computation.1 | async-start | bytes 2064384 | tf_op jit(solution)/shard_map/reduce_scatter | solution.py:938
  27.9 21.0 %collective-permute-start = (bf16[256,256]{1,0:T(8,128)(2,1)}, bf16[256,256]{1,0:T(8,128)(2,1)S(1)}, u32[]{:S(2)}, u32[]{:S(2)}) collective-permute-start(bf16[256,256]{1,0:T(8,128)(2,1)} %get-tuple-element.60), channel_id=1, source_target_pairs={{0,1},{1,2},{2,3},{3,0},{4,5},{5,6},{6,7},{7,4},{8,9},{9,10},{10,1... | collective-permute-start | bytes 393224 | tf_op jit(solution)/shard_map/ppermute | solution.py:808
  28.8 20.2 %collective-permute-start.1 = (bf16[256,256]{1,0:T(8,128)(2,1)}, bf16[256,256]{1,0:T(8,128)(2,1)S(1)}, u32[]{:S(2)}, u32[]{:S(2)}) collective-permute-start(bf16[256,256]{1,0:T(8,128)(2,1)} %get-tuple-element.60), channel_id=1, source_target_pairs={{0,2},{1,3},{2,0},{3,1},{4,6},{5,7},{6,4},{7,5},{8,10},{9,11},{10,... | collective-permute-start | bytes 393224 | tf_op jit(solution)/shard_map/ppermute | solution.py:808
  30.9 1.4 collective-permute-start.6
  31.0 4.2 %collective-permute-start.7 = (bf16[256,256]{1,0:T(8,128)(2,1)S(1)}, bf16[256,256]{1,0:T(8,128)(2,1)S(1)}, u32[]{:S(2)}, u32[]{:S(2)}) collective-permute-start(bf16[256,256]{1,0:T(8,128)(2,1)S(1)} %collective-permute-done.4.refs_4_), channel_id=1, source_target_pairs={{0,4},{4,0},{8,12},{12,8},{16,20},{20,16},{24,28},{28,24},{1,5},{5... | collective-permute-start | bytes 393224 | tf_op jit(solution)/shard_map/ppermute | solution.py:813
  31.5 3.7 %collective-permute-start.8 = (bf16[256,256]{1,0:T(8,128)(2,1)S(1)}, bf16[256,256]{1,0:T(8,128)(2,1)S(1)}, u32[]{:S(2)}, u32[]{:S(2)}) collective-permute-start(bf16[256,256]{1,0:T(8,128)(2,1)S(1)} %collective-permute-done.5.refs_5_), channel_id=1, source_target_pairs={{0,4},{4,0},{8,12},{12,8},{16,20},{20,16},{24,28},{28,24},{1,5},{5... | collective-permute-start | bytes 393224 | tf_op jit(solution)/shard_map/ppermute | solution.py:813
  32.4 16.7 %collective-permute-start.2 = (bf16[256,256]{1,0:T(8,128)(2,1)}, bf16[256,256]{1,0:T(8,128)(2,1)S(1)}, u32[]{:S(2)}, u32[]{:S(2)}) collective-permute-start(bf16[256,256]{1,0:T(8,128)(2,1)} %get-tuple-element.60), channel_id=1, source_target_pairs={{0,3},{1,0},{2,1},{3,2},{4,7},{5,4},{6,5},{7,6},{8,11},{9,8},{10,9... | collective-permute-start | bytes 393224 | tf_op jit(solution)/shard_map/ppermute | solution.py:808
  49.0 1.4 collective-permute-start.10
  49.3 1.4 collective-permute-start.11
  49.6 1.3 collective-permute-start.9
  102.5 17.8 %collective-permute-start.12 = (bf16[4,4,64,256]{3,2,1,0:T(8,128)(2,1)}, bf16[4,4,64,256]{3,2,1,0:T(8,128)(2,1)S(1)}, u32[]{:S(2)}, u32[]{:S(2)}) collective-permute-start(bf16[4,4,64,256]{3,2,1,0:T(8,128)(2,1)} %get-tuple-element.85), channel_id=1, source_target_pairs={{0,4},{4,0},{8,12},{12,8},{16,20},{20,16},{24,28},{28,24},{1,5},{5... | collective-permute-start | bytes 1572872 | tf_op jit(solution)/shard_map/ppermute | solution.py:813
  120.3 1.9 %collective-permute-start.13 = (bf16[1,4,144,256]{3,2,1,0:T(8,128)(2,1)}, bf16[1,4,144,256]{3,2,1,0:T(8,128)(2,1)S(1)}, u32[]{:S(2)}, u32[]{:S(2)}) collective-permute-start(bf16[1,4,144,256]{3,2,1,0:T(8,128)(2,1)} %get-tuple-element.89), channel_id=1, source_target_pairs={{0,4},{4,0},{8,12},{12,8},{16,20},{20,16},{24,28},{28,24},{1,5},{5... | collective-permute-start | bytes 884744 | tf_op jit(solution)/shard_map/ppermute | solution.py:813
  122.2 7.0 %collective-permute-start.14 = (bf16[144,256]{1,0:T(8,128)(2,1)S(1)}, bf16[144,256]{1,0:T(8,128)(2,1)S(1)}, u32[]{:S(2)}, u32[]{:S(2)}) collective-permute-start(bf16[144,256]{1,0:T(8,128)(2,1)S(1)} %get-tuple-element.119), channel_id=1, source_target_pairs={{0,1},{1,2},{2,3},{3,0},{4,5},{5,6},{6,7},{7,4},{8,9},{9,10},{10,1... | collective-permute-start | bytes 221192 | tf_op jit(solution)/shard_map/ppermute | solution.py:808
  122.3 9.4 %collective-permute-start.15 = (bf16[144,256]{1,0:T(8,128)(2,1)S(1)}, bf16[144,256]{1,0:T(8,128)(2,1)S(1)}, u32[]{:S(2)}, u32[]{:S(2)}) collective-permute-start(bf16[144,256]{1,0:T(8,128)(2,1)S(1)} %get-tuple-element.121), channel_id=1, source_target_pairs={{0,2},{1,3},{2,0},{3,1},{4,6},{5,7},{6,4},{7,5},{8,10},{9,11},{10,... | collective-permute-start | bytes 221192 | tf_op jit(solution)/shard_map/ppermute | solution.py:808
  123.5 8.2 %collective-permute-start.16 = (bf16[144,256]{1,0:T(8,128)(2,1)S(1)}, bf16[144,256]{1,0:T(8,128)(2,1)S(1)}, u32[]{:S(2)}, u32[]{:S(2)}) collective-permute-start(bf16[144,256]{1,0:T(8,128)(2,1)S(1)} %get-tuple-element.120), channel_id=1, source_target_pairs={{0,3},{1,0},{2,1},{3,2},{4,7},{5,4},{6,5},{7,6},{8,11},{9,8},{10,9... | collective-permute-start | bytes 221192 | tf_op jit(solution)/shard_map/ppermute | solution.py:808
  126.2 6.0 %collective-permute-start.17 = (bf16[4,64,256]{2,1,0:T(8,128)(2,1)S(1)}, bf16[4,64,256]{2,1,0:T(8,128)(2,1)S(1)}, u32[]{:S(2)}, u32[]{:S(2)}) collective-permute-start(bf16[4,64,256]{2,1,0:T(8,128)(2,1)S(1)} %get-tuple-element.114), channel_id=1, source_target_pairs={{0,8},{4,12},{8,0},{12,4},{16,24},{20,28},{24,16},{28,20},{1,9},{5... | collective-permute-start | bytes 393224 | tf_op jit(solution)/shard_map/ppermute | solution.py:813
  127.7 6.8 %collective-permute-start.18 = (bf16[4,64,256]{2,1,0:T(8,128)(2,1)S(1)}, bf16[4,64,256]{2,1,0:T(8,128)(2,1)S(1)}, u32[]{:S(2)}, u32[]{:S(2)}) collective-permute-start(bf16[4,64,256]{2,1,0:T(8,128)(2,1)S(1)} %get-tuple-element.113), channel_id=1, source_target_pairs={{0,16},{4,20},{8,24},{12,28},{16,0},{20,4},{24,8},{28,12},{1,17},{... | collective-permute-start | bytes 393224 | tf_op jit(solution)/shard_map/ppermute | solution.py:813
  129.3 6.4 %collective-permute-start.19 = (bf16[4,64,256]{2,1,0:T(8,128)(2,1)S(1)}, bf16[4,64,256]{2,1,0:T(8,128)(2,1)S(1)}, u32[]{:S(2)}, u32[]{:S(2)}) collective-permute-start(bf16[4,64,256]{2,1,0:T(8,128)(2,1)S(1)} %get-tuple-element.112), channel_id=1, source_target_pairs={{0,24},{4,28},{8,16},{12,20},{16,8},{20,12},{24,0},{28,4},{1,25},{... | collective-permute-start | bytes 393224 | tf_op jit(solution)/shard_map/ppermute | solution.py:813
  136.7 7.4 %collective-permute-start.20 = (bf16[176,256]{1,0:T(8,128)(2,1)S(1)}, bf16[176,256]{1,0:T(8,128)(2,1)S(1)}, u32[]{:S(2)}, u32[]{:S(2)}) collective-permute-start(bf16[176,256]{1,0:T(8,128)(2,1)S(1)} %get-tuple-element.116), channel_id=1, source_target_pairs={{0,1},{1,2},{2,3},{3,0},{4,5},{5,6},{6,7},{7,4},{8,9},{9,10},{10,1... | collective-permute-start | bytes 270344 | tf_op jit(solution)/shard_map/ppermute | solution.py:808
  138.2 8.7 %collective-permute-start.21 = (bf16[176,256]{1,0:T(8,128)(2,1)S(1)}, bf16[176,256]{1,0:T(8,128)(2,1)S(1)}, u32[]{:S(2)}, u32[]{:S(2)}) collective-permute-start(bf16[176,256]{1,0:T(8,128)(2,1)S(1)} %get-tuple-element.117), channel_id=1, source_target_pairs={{0,2},{1,3},{2,0},{3,1},{4,6},{5,7},{6,4},{7,5},{8,10},{9,11},{10,... | collective-permute-start | bytes 270344 | tf_op jit(solution)/shard_map/ppermute | solution.py:808
  139.9 7.0 %collective-permute-start.22 = (bf16[176,256]{1,0:T(8,128)(2,1)S(1)}, bf16[176,256]{1,0:T(8,128)(2,1)S(1)}, u32[]{:S(2)}, u32[]{:S(2)}) collective-permute-start(bf16[176,256]{1,0:T(8,128)(2,1)S(1)} %get-tuple-element.118), channel_id=1, source_target_pairs={{0,3},{1,0},{2,1},{3,2},{4,7},{5,4},{6,5},{7,6},{8,11},{9,8},{10,9... | collective-permute-start | bytes 270344 | tf_op jit(solution)/shard_map/ppermute | solution.py:808
  147.8 6.8 %collective-permute-start.23 = (bf16[320,256]{1,0:T(8,128)(2,1)S(1)}, bf16[320,256]{1,0:T(8,128)(2,1)S(1)}, u32[]{:S(2)}, u32[]{:S(2)}) collective-permute-start(bf16[320,256]{1,0:T(8,128)(2,1)S(1)} %pad_maximum_fusion.1.refs_0_), channel_id=1, source_target_pairs={{0,8},{4,12},{8,0},{12,4},{16,24},{20,28},{24,16},{28,20},{1,9},{5... | collective-permute-start | bytes 491528 | tf_op jit(solution)/shard_map/ppermute | solution.py:813
  148.7 9.0 %collective-permute-start.24 = (bf16[320,256]{1,0:T(8,128)(2,1)S(1)}, bf16[320,256]{1,0:T(8,128)(2,1)S(1)}, u32[]{:S(2)}, u32[]{:S(2)}) collective-permute-start(bf16[320,256]{1,0:T(8,128)(2,1)S(1)} %pad_maximum_fusion.1.refs_0_), channel_id=1, source_target_pairs={{0,16},{4,20},{8,24},{12,28},{16,0},{20,4},{24,8},{28,12},{1,17},{... | collective-permute-start | bytes 491528 | tf_op jit(solution)/shard_map/ppermute | solution.py:813
  149.2 8.4 %collective-permute-start.25 = (bf16[320,256]{1,0:T(8,128)(2,1)S(1)}, bf16[320,256]{1,0:T(8,128)(2,1)S(1)}, u32[]{:S(2)}, u32[]{:S(2)}) collective-permute-start(bf16[320,256]{1,0:T(8,128)(2,1)S(1)} %pad_maximum_fusion.1.refs_0_), channel_id=1, source_target_pairs={{0,24},{4,28},{8,16},{12,20},{16,8},{20,12},{24,0},{28,4},{1,25},{... | collective-permute-start | bytes 491528 | tf_op jit(solution)/shard_map/ppermute | solution.py:813
  151.4 6.8 %collective-permute-start.26 = (bf16[320,256]{1,0:T(8,128)(2,1)S(1)}, bf16[320,256]{1,0:T(8,128)(2,1)S(1)}, u32[]{:S(2)}, u32[]{:S(2)}) collective-permute-start(bf16[320,256]{1,0:T(8,128)(2,1)S(1)} %pad_maximum_fusion.1.refs_0_), channel_id=1, source_target_pairs={{0,4},{4,0},{8,12},{12,8},{16,20},{20,16},{24,28},{28,24},{1,5},{5... | collective-permute-start | bytes 491528 | tf_op jit(solution)/shard_map/ppermute | solution.py:813
  154.6 3.6 %collective-permute-start.27 = (bf16[320,256]{1,0:T(8,128)(2,1)S(1)}, bf16[320,256]{1,0:T(8,128)(2,1)S(1)}, u32[]{:S(2)}, u32[]{:S(2)}) collective-permute-start(bf16[320,256]{1,0:T(8,128)(2,1)S(1)} %collective-permute-done.23.refs_1_), channel_id=1, source_target_pairs={{0,4},{4,0},{8,12},{12,8},{16,20},{20,16},{24,28},{28,24},{1,5},{5... | collective-permute-start | bytes 491528 | tf_op jit(solution)/shard_map/ppermute | solution.py:813
  157.7 1.4 collective-permute-start.28
  157.7 1.6 collective-permute-start.29
  (23 other events, 109.3 us)
Sparse Core Ops, SparseCore 0:
  28.0 25.1 all-gather.2
  91.9 38.6 reduce-scatter.1
where the time goes:
time: 171 us
  Pallas kernels  87.9 us (51%)
  starting transfers between devices  32.5 us (19%)
  waiting for transfers between devices  29.1 us (17%)
  between operations  14.4 us (8%)
  other arithmetic  4.28 us (3%)
  local copies, waits for them, and re-layouts  2.65 us (2%)
    pallas_call x1, Pallas kernels, top_call(): pl.pallas_call(top_kernel, grid_spec=pltpu.PrefetchScalarGridSpec(num_sca...  34 us
    ppermute x12, starting transfers between devices, turn_mp(): return lax.ppermute(x, 'mp', [(i, (i + k) % n) for i in range(n)])  20.9 us
    pallas_call x1, Pallas kernels, attn_bwd_call(): pl.pallas_call(attn_bwd_kernel, grid_spec=pltpu.PrefetchScalarGridSpec(nu...  17.6 us
    ppermute x12, waiting for transfers between devices, turn_mp(): return lax.ppermute(x, 'mp', [(i, (i + k) % n) for i in range(n)])  15.3 us
    ppermute x18, waiting for transfers between devices, swap_dp(): return lax.ppermute(x, 'dp', [(i, i ^ bits) for i in range(n)])  13.8 us
    pallas_call x1, Pallas kernels, attn_fwd_call(): pl.pallas_call(attn_fwd_kernel, grid_spec=pltpu.PrefetchScalarGridSpec(nu...  13.1 us
    ppermute x18, starting transfers between devices, swap_dp(): return lax.ppermute(x, 'dp', [(i, i ^ bits) for i in range(n)])  11.6 us
    pallas_call x1, Pallas kernels, ff_bwd_call(): pl.pallas_call(ff_bwd_kernel, grid_spec=pltpu.PrefetchScalarGridSpec(num_...  10.6 us
  transfers between devices with their start and end apart: 32, of which 15 were waited for; matrix products, arithmetic and copies ran while one was open for 1% of the time, Pallas kernels for 28%

commit v1 on v0

--- a/solution.py
+++ b/solution.py
@@ -106,57 +106,74 @@
         ref[block, pl.ds(at, STRIPE, stride=CROPS), :] = x[line * 8 : line * 8 + STRIPE]
 
 
-def heads_apart(x, inside=None):
-    lane = lax.broadcasted_iota(jnp.int32, (WIN, 128), 1) // HEAD
-    rest = jnp.zeros((128 - WIN, 128), bf16)
-    blocks = []
+def fill_head_masks(masks):
+    lane = lax.broadcasted_iota(jnp.int32, (WIN, 256), 1) % 128 // HEAD
     for head in range(HALF_HEADS):
-        keep = lane == head
-        if inside is not None:
-            keep = keep & inside
-        blocks.append(jnp.where(keep, x, 0.0).astype(bf16))
-        blocks.append(rest)
-    return jnp.concatenate(blocks, axis=0)
-
-
-def by_head(flat_turned, probs):
+        masks[head] = jnp.where(lane == head, 1.0, 0.0).astype(bf16)
+
+
+def heads_down(x, masks):
+    return jnp.concatenate([x * masks[head] for head in range(HALF_HEADS)], axis=0)
+
+
+def fold_heads(x):
+    head = lax.broadcasted_iota(jnp.int32, (WIN, 256), 1) % 128 // HEAD
+    parts = [x[h * WIN : (h + 1) * WIN] for h in range(HALF_HEADS)]
+    low, high = jnp.where(head == 0, parts[0], parts[1]), jnp.where(head == 2, parts[2], parts[3])
+    return jnp.where(head < 2, low, high)
+
+
+def windows_apart(x):
+    none, rest = jnp.zeros((WIN, 128), x.dtype), jnp.zeros((128 - WIN, 256), x.dtype)
+    first = jnp.concatenate([x[:, :128], none], axis=1)
+    second = jnp.concatenate([none, x[:, 128:]], axis=1)
+    return jnp.concatenate([first, rest, second, rest], axis=0)
+
+
+def by_head(turned, probs):
     parts = []
     for head in range(HALF_HEADS):
-        parts.append(
-            dot(flat_turned[head * HEAD : (head + 1) * HEAD], probs[:, head * 128 : (head + 1) * 128])
-        )
+        left = jnp.concatenate([turned[w * 128 + head * HEAD : w * 128 + (head + 1) * HEAD] for w in range(2)], axis=0)
+        both = dot(left, probs[head * WIN : (head + 1) * WIN])
+        parts.append((both[:HEAD, :128], both[HEAD:, 128:]))
+    return [jnp.concatenate([part[w] for part in parts], axis=0).T[:WIN] for w in range(2)]
+
+
+def head_probs(scores, bias):
+    scores = scores * (factor * log2_e) + bias
+    raised = jnp.exp2(scores - jnp.max(scores, axis=0, keepdims=True))
+    return (raised * (1.0 / jnp.sum(raised, axis=0, keepdims=True))).astype(bf16)
+
+
+def head_grad_scores(grad_probs, probs):
+    wide = probs.astype(f32)
+    inner = jnp.sum(grad_probs * wide, axis=0, keepdims=True)
+    return (wide * (grad_probs - inner)).astype(bf16)
+
+
+def each_head(fn, *arrays):
+    parts = [fn(*(x[h * WIN : (h + 1) * WIN] for x in arrays)) for h in range(HALF_HEADS)]
     return jnp.concatenate(parts, axis=0)
 
 
-def attend(queries, keys, values, biases):
-    apart = [heads_apart(x) for x in queries]
+def attend(queries, keys, values, biases, masks):
+    apart = [windows_apart(x.astype(bf16)) for x in queries]
+    scores = [dot_nt(heads_down(k.astype(bf16), masks), q) for k, q in zip(keys, apart)]
     value_turned = [x.T.astype(bf16) for x in values]
-    scores = [dot_nt(k.astype(bf16), q) for k, q in zip(keys, apart)]
-    scores = [s * (factor * log2_e) + jnp.concatenate([b] * HALF_HEADS, axis=1) for s, b in zip(scores, biases)]
-    peaks = [jnp.max(s, axis=0, keepdims=True) for s in scores]
-    raised = [jnp.exp2(s - p) for s, p in zip(scores, peaks)]
-    shares = [1.0 / jnp.sum(r, axis=0, keepdims=True) for r in raised]
-    probs = [(r * s).astype(bf16) for r, s in zip(raised, shares)]
-    outs = [by_head(v, p) for v, p in zip(value_turned, probs)]
-    return [o.T[:WIN] for o in outs], probs
-
-
-def attend_back(grads, queries, keys, values, probs, insides):
-    grad_apart = [heads_apart(x, i) for x, i in zip(grads, insides)]
-    grad_probs = [dot_nt(v, g) for v, g in zip(values, grad_apart)]
+    probs = [each_head(lambda s, b=b: head_probs(s, b), s) for s, b in zip(scores, biases)]
+    return [by_head(v, p) for v, p in zip(value_turned, probs)], probs
+
+
+def attend_back(grads, queries, keys, values, probs, masks):
+    grad_apart = [windows_apart(x) for x in grads]
+    grad_probs = [dot_nt(heads_down(v, masks), g) for v, g in zip(values, grad_apart)]
     key_turned = [x.astype(f32).T.astype(bf16) for x in keys]
-    grad_value = [dot(p, g) for p, g in zip(probs, grad_apart)]
-    wide = [p.astype(f32) for p in probs]
-    inner = [jnp.sum(g * w, axis=0, keepdims=True) for g, w in zip(grad_probs, wide)]
-    grad_scores = [(w * (g - i)).astype(bf16) for w, g, i in zip(wide, grad_probs, inner)]
-    apart = [heads_apart(x) for x in queries]
-    grad_key = [dot(s, q) * factor for s, q in zip(grad_scores, apart)]
-    grad_query = [by_head(k, s) for k, s in zip(key_turned, grad_scores)]
-    grad_query = [g.T[:WIN] * factor for g in grad_query]
+    grad_value = [fold_heads(dot(p, g)) for p, g in zip(probs, grad_apart)]
+    grad_scores = [each_head(head_grad_scores, g, p) for g, p in zip(grad_probs, probs)]
+    apart = [windows_apart(x) for x in queries]
+    grad_key = [fold_heads(dot(s, q)) * factor for s, q in zip(grad_scores, apart)]
+    grad_query = [[x * factor for x in by_head(k, s)] for k, s in zip(key_turned, grad_scores)]
     return grad_query, grad_key, grad_value
-
-
-WINDOWS = [(orient, window) for orient in range(2) for window in range(2)]
 
 
 def steps_along(x, orient):
@@ -269,12 +286,12 @@
             wr[pl.ds(pl.multiple_of(shard * 64 + at, 16), n), c * 256 : (c + 1) * 256] = value
 
     for p in range(3):
-        put(me, 64 * p, qkv[0, 64 * p : 64 * (p + 1)])
-    put(me, 192, mixer_t[0])
+        put(me, 64 * p, qkv[1, 64 * p : 64 * (p + 1)])
+    put(me, 192, mixer_t[1])
     sm[...] = vec[1].astype(f32)
-    put(me, 288, expand[0])
+    put(me, 288, expand[1])
     for c in range(4):
-        put(me, 544 + 64 * c, reduce_t[0, :, c * 256 : (c + 1) * 256])
+        put(me, 544 + 64 * c, reduce_t[1, :, c * 256 : (c + 1) * 256])
     dp, _, r, _ = rest.shape
     edges = list(range(0, 257, 64)) + [288] + [544 + 64 * c for c in range(5)]
     for k in range(3):
@@ -308,38 +325,43 @@
     qkv[:, ROWS:HELD, :] = jnp.zeros((6, HELD - ROWS, 128), f32)
 
 
-def attend_crops(place, crops, slots, qkv, packed, probs_ref, out):
+def load_pair(ref, block, crop, orient):
+    return jnp.concatenate([load_window(ref, block, crop, orient, window) for window in range(2)], axis=1)
+
+
+def attend_crops(place, crops, slots, masks, qkv, packed, probs_ref, out):
     at, lists = [], ([], [], [], [])
     for crop, slot in zip(crops, slots):
         height, width = place[2 + 2 * crop], place[3 + 2 * crop]
-        for n, (orient, window) in enumerate(WINDOWS):
-            three = [load_window(qkv, orient * 3 + p, crop, orient, window) for p in range(3)]
-            packed[slot, n] = jnp.concatenate(three, axis=1).astype(bf16)
-            entries = (*three, key_bias(orient, window, height, width))
-            for held, new in zip(lists, entries):
+        for orient in range(2):
+            three = [load_pair(qkv, orient * 3 + p, crop, orient) for p in range(3)]
+            for p, x in enumerate(three):
+                packed[slot, orient, p] = x.astype(bf16)
+            bias = jnp.concatenate([key_bias(orient, window, height, width) for window in range(2)], axis=1)
+            for held, new in zip(lists, (*three, bias)):
                 held.append(new)
-            at.append((crop, slot, n, orient, window))
-    outs, probs = attend(*lists)
-    for (crop, slot, n, orient, window), o, p in zip(at, outs, probs):
-        probs_ref[slot, n] = p
-        store_window(out, orient, crop, orient, window, o)
-
-
-def attend_crops_back(crops, slots, em, packed, probs_ref, e):
-    at, lists = [], ([], [], [], [], [], [])
+            at.append((crop, slot, orient))
+    outs, probs = attend(*lists, masks)
+    for (crop, slot, orient), both, p in zip(at, outs, probs):
+        probs_ref[slot, orient] = p
+        for window in range(2):
+            store_window(out, orient, crop, orient, window, both[window])
+
+
+def attend_crops_back(crops, slots, masks, em, packed, probs_ref, e_at):
+    at, lists = [], ([], [], [], [], [])
     for crop, slot in zip(crops, slots):
-        for n, (orient, window) in enumerate(WINDOWS):
-            grad = load_window(em, orient, crop, orient, window)
-            entries = (
-                grad, packed[slot, n, :, :128], packed[slot, n, :, 128:256], packed[slot, n, :, 256:],
-                probs_ref[slot, n], window_row_inside(orient),
-            )
-            for held, new in zip(lists, entries):
+        for orient in range(2):
+            inside = jnp.concatenate([window_row_inside(orient)] * 2, axis=1)
+            grad = jnp.where(inside, load_pair(em, orient, crop, orient), 0.0).astype(bf16)
+            for held, new in zip(lists, (grad, *(packed[slot, orient, p] for p in range(3)), probs_ref[slot, orient])):
                 held.append(new)
-            at.append((crop, orient, window))
-    for (crop, orient, window), dq, dk, dv in zip(at, *attend_back(*lists)):
-        for p, part in enumerate((dq, dk, dv)):
-            store_window(e, orient * 3 + p, crop, orient, window, part)
+            at.append((crop, orient))
+    for (crop, orient), dq, dk, dv in zip(at, *attend_back(*lists, masks)):
+        for window in range(2):
+            lanes = slice(window * 128, (window + 1) * 128)
+            for p, part in enumerate((dq[window], dk[:, lanes], dv[:, lanes])):
+                store_window(*e_at(orient, p), crop, orient, window, part)
 
 
 def taps_of(sm, orient):
@@ -428,7 +450,7 @@
     em[:, ROWS:HELD, :] = jnp.zeros((2, HELD - ROWS, 128), f32)
 
 
-def mix_back(em, value, value_at, sm, e, e_low, vec):
+def mix_back(em, value, value_at, sm, e_at, e_low, vec):
     taps = [taps_of(sm, orient) for orient in range(2)]
 
     def line(i, _):
@@ -436,7 +458,7 @@
         for orient in range(2):
             lanes = slice(orient * 128, (orient + 1) * 128)
             base = orient * 384
-            eq, ek, ev = [e[orient * 3 + p, rows, :] for p in range(3)]
+            eq, ek, ev = [ref[block, rows, :] for ref, block in (e_at(orient, p) for p in range(3))]
             ev = ev + stencil_line(em, orient, taps[orient], i, orient, True)
             e_low[rows, base : base + 384] = jnp.concatenate([eq, ek, ev], axis=1).astype(bf16)
             vec[ENTRY, :, lanes] += column_sum(eq)
@@ -519,15 +541,16 @@
 
 def attn_fwd_kernel(place, x, *refs):
     own, near, far = refs[0:3], refs[3:6], refs[6:9]
-    middle, packed, probs, mixed, value, wqkv, wm, sm, qkv, out = refs[9:]
+    middle, packed, probs, mixed, value, wqkv, wm, sm, qkv, out, masks = refs[9:]
 
     @first_step
     def _():
         assemble_attn(0, place[0], place[1], own, near, far, wqkv, wm, sm)
+        fill_head_masks(masks)
         project(x, wqkv, sm, qkv)
 
     crops = [pl.program_id(0) * STEP_CROPS + i for i in range(STEP_CROPS)]
-    attend_crops(place, crops, range(STEP_CROPS), qkv, packed, probs, out)
+    attend_crops(place, crops, range(STEP_CROPS), masks, qkv, packed, probs, out)
 
     @last_step
     def _():
@@ -551,16 +574,17 @@
 def top_kernel(place, x, cotangent, *refs):
     attn_own, ff_own, rest = refs[0:3], refs[3:5], refs[5]
     (output, grad_out, grads) = refs[6:9]
-    (wqkv, wm, sm, we, wr, qkv, out, packed, probs, mixed, middle, g, slope, e, e_low,
-     acc_e, acc_r, acc_q, acc_m, vec) = refs[9:]
+    (wqkv, wm, sm, we, wr, qkv, out, packed, probs, mixed, middle, g, slope, dv,
+     acc_e, acc_r, acc_q, acc_m, vec, masks) = refs[9:]
 
     assemble_top(place[0], attn_own, ff_own, rest, wqkv, wm, sm, we, wr)
     clear(acc_e, acc_r, acc_q, acc_m, vec)
+    fill_head_masks(masks)
     project(x, wqkv, sm, qkv)
 
     def ahead(i, _):
         crops = [i * STEP_CROPS + j for j in range(STEP_CROPS)]
-        attend_crops(place, crops, crops, qkv, packed, probs, out)
+        attend_crops(place, crops, crops, masks, qkv, packed, probs, out)
         return 0
 
     lax.fori_loop(0, CROPS // STEP_CROPS, ahead, 0)
@@ -576,16 +600,20 @@
         held = lambda s: (g[rows, s * 256 : (s + 1) * 256], slope[rows, s * 256 : (s + 1) * 256])
         middle_here = middle[rows, :]
         middle[rows, :] = ff_backward(cotangent[rows, :].astype(f32), middle_here, we, wr, sm, acc_e, acc_r, vec, held)
-    em = out
+    em, e_low = out, g.at[:, 0:768]
+
+    def e_at(orient, p):
+        return (dv, orient) if p == 2 else (qkv, orient * 3 + p)
+
     mixer_back(middle, mixed, wm, acc_m, vec, em)
 
     def behind(i, _):
         crops = [i * STEP_CROPS + j for j in range(STEP_CROPS)]
-        attend_crops_back(crops, crops, em, packed, probs, e)
+        attend_crops_back(crops, crops, masks, em, packed, probs, e_at)
         return 0
 
     lax.fori_loop(0, CROPS // STEP_CROPS, behind, 0)
-    mix_back(em, qkv, (2, 5), sm, e, e_low, vec)
+    mix_back(em, qkv, (2, 5), sm, e_at, e_low, vec)
     project_back(middle, x, e_low, wqkv, sm, acc_q, vec, grad_out)
     write_parts(attn_pieces(acc_q, acc_m, jnp.sum(vec[...], axis=1)) + ff_pieces(acc_e, acc_r), 0, grads)
 
@@ -602,19 +630,20 @@
         write_halves(place[1], ff_pieces(acc_e, acc_r), keep, give)
 
 
-def attn_bwd_kernel(place, grad, x, packed, probs, mixed, value, wqkv, wm, sm, vec_in, patch_grad, keep, give, em, e, e_low, acc_q, acc_m, vec):
+def attn_bwd_kernel(place, grad, x, packed, probs, mixed, value, wqkv, wm, sm, vec_in, patch_grad, keep, give, em, e, e_low, acc_q, acc_m, vec, masks):
     @first_step
     def _():
+        fill_head_masks(masks)
         clear(acc_q, acc_m)
         vec[...] = vec_in[...]
         mixer_back(grad, mixed, wm, acc_m, vec, em)
 
     crops = [pl.program_id(0) * STEP_CROPS + i for i in range(STEP_CROPS)]
-    attend_crops_back(crops, range(STEP_CROPS), em, packed, probs, e)
+    attend_crops_back(crops, range(STEP_CROPS), masks, em, packed, probs, lambda orient, p: (e, orient * 3 + p))
 
     @last_step
     def _():
-        mix_back(em, value, (0, 1), sm, e, e_low, vec)
+        mix_back(em, value, (0, 1), sm, lambda orient, p: (e, orient * 3 + p), e_low, vec)
         project_back(grad, x, e_low, wqkv, sm, acc_q, vec, patch_grad)
         write_halves(place[1], attn_pieces(acc_q, acc_m, jnp.sum(vec[...], axis=1)), keep, give)
 
@@ -628,7 +657,7 @@
 
 
 def crop_spec(*dims):
-    return pl.BlockSpec((STEP_CROPS, 4) + dims, lambda i, *_: (i, 0, 0, 0))
+    return pl.BlockSpec((STEP_CROPS,) + dims, lambda i, *_: (i,) + (0,) * len(dims))
 
 
 def of_layer(layer, *dims):
@@ -651,13 +680,29 @@
     return jax.ShapeDtypeStruct(dims, dtype)
 
 
-def params(micros):
+def far(dims, dtype=bf16):
+    return pltpu.HBM(dims, dtype)
+
+
+def params(micros, mib=16, grid=True):
+    steps = dict(dimension_semantics=("arbitrary",)) if grid else {}
     return dict(
-        compiler_params=pltpu.CompilerParams(
-            vmem_limit_bytes=58 * 1024 * 1024, dimension_semantics=("arbitrary",)
-        ),
+        compiler_params=pltpu.CompilerParams(vmem_limit_bytes=mib * 1024 * 1024, **steps),
         cost_estimate=pl.CostEstimate(flops=int(micros * 1e9), bytes_accessed=1 << 20, transcendentals=0),
     )
+
+
+def held_call(kernel, name, place, arrays, outs, scratch, micros, mib):
+    there = pl.BlockSpec(memory_space=pltpu.VMEM)
+    return pl.pallas_call(
+        kernel,
+        in_specs=[pl.BlockSpec(memory_space=pltpu.SMEM)] + [there] * len(arrays),
+        out_specs=[there] * len(outs),
+        out_shape=[shape(dims, dtype) for dims, dtype in outs],
+        scratch_shapes=list(scratch),
+        name=name,
+        **params(micros, mib, False),
+    )(place, *arrays)
 
 
 v = pltpu.VMEM
@@ -671,12 +716,12 @@
             num_scalar_prefetch=1,
             grid=(CROPS // STEP_CROPS,),
             in_specs=[whole((ROWS, D))] + attn_specs(0) + half_specs(rows),
-            out_specs=[whole((ROWS, D)), crop_spec(WIN, 384), crop_spec(WIN, 512), whole((ROWS, D)), whole((2, ROWS, 128)), whole((768, D)), whole((D, D)), whole((32, D))],
-            scratch_shapes=[v((6, HELD, 128), f32), v((2, HELD, 128), f32)],
+            out_specs=[whole((ROWS, D)), crop_spec(2, 3, WIN, 256), crop_spec(2, 4 * WIN, 256), whole((ROWS, D)), whole((2, ROWS, 128)), whole((768, D)), whole((D, D)), whole((32, D))],
+            scratch_shapes=[v((6, HELD, 128), f32), v((2, HELD, 128), f32), v((HALF_HEADS, WIN, 256), bf16)],
         ),
-        out_shape=[shape((ROWS, D), f32), shape((CROPS, 4, WIN, 384)), shape((CROPS, 4, WIN, 512)), shape((ROWS, D)), shape((2, ROWS, 128)), shape((768, D)), shape((D, D)), shape((32, D), f32)],
+        out_shape=[far((ROWS, D), f32), far((CROPS, 2, 3, WIN, 256)), far((CROPS, 2, 4 * WIN, 256)), far((ROWS, D)), far((2, ROWS, 128)), far((768, D)), far((D, D)), shape((32, D), f32)],
         name="attn_fwd",
-        **params(10),
+        **params(10, 20),
     )(place, x, *unit)
 
 
@@ -689,33 +734,22 @@
             in_specs=[rows_of(D), whole((32, D))] + ff_specs(0) + half_specs(HALF_FF),
             out_specs=[rows_of(D), whole((4, D, D)), whole((D, FF))],
         ),
-        out_shape=[shape((ROWS, D), f32), shape((4, D, D)), shape((D, FF))],
+        out_shape=[shape((ROWS, D), f32), far((4, D, D)), far((D, FF))],
         name="ff_fwd",
-        **params(6),
+        **params(6, 16),
     )(place, middle, sm, *unit)
 
 
 def top_call(place, x, cotangent, weights, parts, r):
-    dp, _, rest_rows, _ = weights[-1].shape
-    return pl.pallas_call(
-        top_kernel,
-        grid_spec=pltpu.PrefetchScalarGridSpec(
-            num_scalar_prefetch=1,
-            grid=(1,),
-            in_specs=[whole((ROWS, D)), whole((ROWS, D))] + attn_specs(1) + ff_specs(1) + [whole((dp, 3, rest_rows, D))],
-            out_specs=[whole((ROWS, D)), whole((ROWS, D)), whole((parts, 4, r, D))],
-            scratch_shapes=[
+    scratch = [
                 v((768, D), bf16), v((D, D), bf16), v((32, D), f32), v((4, D, D), bf16), v((D, FF), bf16),
-                v((6, HELD, 128), f32), v((2, HELD, 128), f32), v((CROPS, 4, WIN, 384), bf16), v((CROPS, 4, WIN, 512), bf16),
+                v((6, HELD, 128), f32), v((2, HELD, 128), f32), v((CROPS, 2, 3, WIN, 256), bf16), v((CROPS, 2, 4 * WIN, 256), bf16),
                 v((ROWS, D), bf16), v((ROWS, D), f32), v((ROWS, FF), bf16), v((ROWS, FF), bf16),
-                v((6, HELD, 128), f32), v((ROWS, 768), bf16),
-                v((4, D, D), f32), v((4, D, D), f32), v((768, D), f32), v((D, D), f32), v((32, CROPS, D), f32),
-            ],
-        ),
-        out_shape=[shape((ROWS, D)), shape((ROWS, D), f32), shape((parts, 4, r, D))],
-        name="top_block",
-        **params(30),
-    )(place, x, cotangent, *weights)
+                v((2, HELD, 128), f32),
+                v((4, D, D), f32), v((4, D, D), f32), v((768, D), f32), v((D, D), f32), v((32, CROPS, D), f32), v((HALF_HEADS, WIN, 256), bf16),
+    ]
+    outs = [((ROWS, D), bf16), ((ROWS, D), f32), ((parts, 4, r, D), bf16)]
+    return held_call(top_kernel, "top_block", place, [x, cotangent, *weights], outs, scratch, 30, 49)
 
 
 def ff_bwd_call(place, grad, middle, we, wr, sm, parts, r):
@@ -730,7 +764,7 @@
         ),
         out_shape=[shape((ROWS, D), f32)] + [shape((parts, 4, r, D))] * 2 + [shape((32, CROPS, D), f32)],
         name="ff_bwd",
-        **params(10),
+        **params(10, 20),
     )(place, grad, middle, we, wr, sm)
 
 
@@ -740,13 +774,13 @@
         grid_spec=pltpu.PrefetchScalarGridSpec(
             num_scalar_prefetch=1,
             grid=(CROPS // STEP_CROPS,),
-            in_specs=[whole((ROWS, D)), whole((ROWS, D)), crop_spec(WIN, 384), crop_spec(WIN, 512), whole((ROWS, D)), whole((2, ROWS, 128)), whole((768, D)), whole((D, D)), whole((32, D)), whole((32, CROPS, D))],
+            in_specs=[whole((ROWS, D)), whole((ROWS, D)), crop_spec(2, 3, WIN, 256), crop_spec(2, 4 * WIN, 256), whole((ROWS, D)), whole((2, ROWS, 128)), whole((768, D)), whole((D, D)), whole((32, D)), whole((32, CROPS, D))],
             out_specs=[whole((ROWS, D))] + [whole((1, 4, LOW_ROWS // 2, D))] * 2,
-            scratch_shapes=[v((2, HELD, 128), f32), v((6, HELD, 128), f32), v((ROWS, 768), bf16), v((768, D), f32), v((D, D), f32), v((32, CROPS, D), f32)],
+            scratch_shapes=[v((2, HELD, 128), f32), v((6, HELD, 128), f32), v((ROWS, 768), bf16), v((768, D), f32), v((D, D), f32), v((32, CROPS, D), f32), v((HALF_HEADS, WIN, 256), bf16)],
         ),
         out_shape=[shape((ROWS, D))] + [shape((1, 4, LOW_ROWS // 2, D))] * 2,
         name="attn_bwd",
-        **params(16),
+        **params(16, 36),
     )(place, grad, x, packed, probs, mixed, value, wqkv, wm, sm, vec)
 
 
@@ -799,7 +833,7 @@
         ),
         out_shape=[shape(dims, dtype) for dims, dtype in outs],
         name=name,
-        **params(1),
+        **params(1, 58),
     )(place, *arrays)
 
 
@@ -956,8 +990,8 @@
     cut_f = LOW_ROWS // 2
     cut_t = cut_f + r_f
     held = [v((2, cut_f + planes * r_f, D), f32), v((dp * r_t, D), f32)]
-    packed_g, mixer_g, expand_g, reduce_g, gain_g, shift_g, entry_g, taps_g, branch_g, hidden_g = local_call(
-        functools.partial(unpack_kernel, planes, cut_f, cut_t), "unpack", place, mine + other, [(dims, f32) for dims in outs], held
+    packed_g, mixer_g, expand_g, reduce_g, gain_g, shift_g, entry_g, taps_g, branch_g, hidden_g = held_call(
+        functools.partial(unpack_kernel, planes, cut_f, cut_t), "unpack", place, mine + other, [(dims, f32) for dims in outs], held, 2, 16
     )
     return (
         from_rows(output), from_rows(patch_grad), gain_g, shift_g,

time: 171 us -> 165 us (0.965)
  Pallas kernels: 87.9 us -> 72.3 us
  local copies, waits for them, and re-layouts: 2.65 us -> 10.2 us
  waiting for transfers between devices: 29.1 us -> 32.5 us
    unnamed x46 -> x48, local copies, waits for them, and re-layouts: 2.41 us -> 10 us
    pallas_call x1, Pallas kernels: 17.6 us -> 13.6 us  [attn_bwd_call(): pl.pallas_call(attn_bwd_kernel, grid_spec=pltpu.PrefetchScalarGridSpec(nu...]
    pallas_call x2 -> x1, Pallas kernels: 6.4 us -> 2.83 us  [local_call(): pl.pallas_call(kernel, grid_spec=pltpu.PrefetchScalarGridSpec(num_scalar_...]
    ppermute x18, waiting for transfers between devices: 13.8 us -> 17 us  [swap_dp(): return lax.ppermute(x, 'dp', [(i, i ^ bits) for i in range(n)])]
    pallas_call x1, Pallas kernels: 10.6 us -> 7.64 us  [ff_bwd_call(): pl.pallas_call(ff_bwd_kernel, grid_spec=pltpu.PrefetchScalarGridSpec(num_...]
    pallas_call x1, Pallas kernels: 6.15 us -> 3.69 us  [ff_fwd_call(): pl.pallas_call(ff_fwd_kernel, grid_spec=pltpu.PrefetchScalarGridSpec(num_...]
    pallas_call x1, Pallas kernels: 13.1 us -> 11.2 us  [attn_fwd_call(): pl.pallas_call(attn_fwd_kernel, grid_spec=pltpu.PrefetchScalarGridSpec(nu...]
    pallas_call x1 -> x2, Pallas kernels: 34 us -> 33.3 us  [held_call(): pl.pallas_call(kernel, in_specs=[pl.BlockSpec(memory_space=pltpu.SMEM)] +...]
  transfers between devices with their start and end apart: 32 -> 32, of which waited for: 15 -> 16; matrix products, arithmetic and copies ran while one was open for 1% -> 1% of each run, Pallas kernels for 28% -> 22%
where the time goes in v1:
time: 165 us
  Pallas kernels  72.3 us (44%)
  waiting for transfers between devices  32.5 us (20%)
  starting transfers between devices  31.6 us (19%)
  between operations  14.3 us (9%)
  local copies, waits for them, and re-layouts  10.2 us (6%)
  other arithmetic  3.75 us (2%)
    pallas_call x2, Pallas kernels, held_call(): pl.pallas_call(kernel, in_specs=[pl.BlockSpec(memory_space=pltpu.SMEM)] +...  33.3 us
    ppermute x12, starting transfers between devices, turn_mp(): return lax.ppermute(x, 'mp', [(i, (i + k) % n) for i in range(n)])  20.3 us
    ppermute x18, waiting for transfers between devices, swap_dp(): return lax.ppermute(x, 'dp', [(i, i ^ bits) for i in range(n)])  17 us
    ppermute x12, waiting for transfers between devices, turn_mp(): return lax.ppermute(x, 'mp', [(i, (i + k) % n) for i in range(n)])  15.5 us
    pallas_call x1, Pallas kernels, attn_bwd_call(): pl.pallas_call(attn_bwd_kernel, grid_spec=pltpu.PrefetchScalarGridSpec(nu...  13.6 us
    ppermute x18, starting transfers between devices, swap_dp(): return lax.ppermute(x, 'dp', [(i, i ^ bits) for i in range(n)])  11.3 us
    pallas_call x1, Pallas kernels, attn_fwd_call(): pl.pallas_call(attn_fwd_kernel, grid_spec=pltpu.PrefetchScalarGridSpec(nu...  11.2 us
    unnamed x48, local copies, waits for them, and re-layouts  10 us
  transfers between devices with their start and end apart: 32, of which 16 were waited for; matrix products, arithmetic and copies ran while one was open for 1% of the time, Pallas kernels for 22%

profile of v1, /device:TPU:0, one launch (start us, length us, event | category | flops | bytes accessed | tf_op | source)
XLA Modules:
  0.0 164.8 jit_solution(8861129800071467507)
XLA Ops:
  7.8 2.8 %pack.1 = (bf16[256,256]{1,0:T(8,128)(2,1)}, bf16[256,256]{1,0:T(8,128)(2,1)}, bf16[2,32,256]{2,1,0:T(8,128)(2,1)}) custom-call(s32[4]{0:T(128)} %pad_add_fusion.2.place, bf16[2,192,256]{2,1,0:T(8,128)(2,1)} %bitcast.76, bf16[2,64,256]{2,1,0:T(8,128)(2,1)} %bitcast.79, bf16[2,2,64]{2,1,0:T(2,128)(2,1)} %gain.1, bf16[2,2,64]{2,1,0:T(2,128)(2,1)} %shift.1, ...), custom_call_target="tpu_custom_call" | custom-call | flops 1000000000 | bytes 1048576 | tf_op jit(solution)/shard_map/pack/pallas_call | solution.py:825
  10.7 5.0 %collective-permute-start.5 = (bf16[256,256]{1,0:T(8,128)(2,1)}, bf16[256,256]{1,0:T(8,128)(2,1)S(1)}, u32[]{:S(2)}, u32[]{:S(2)}) collective-permute-start(bf16[256,256]{1,0:T(8,128)(2,1)} %get-tuple-element.61), channel_id=1, source_target_pairs={{0,3},{1,0},{2,1},{3,2},{4,7},{5,4},{6,5},{7,6},{8,11},{9,8},{10,9... | collective-permute-start | bytes 393224 | tf_op jit(solution)/shard_map/ppermute | solution.py:842
  16.7 3.2 %collective-permute-done.5.refs_5_ = bf16[256,256]{1,0:T(8,128)(2,1)S(1)} collective-permute-done((bf16[256,256]{1,0:T(8,128)(2,1)}, bf16[256,256]{1,0:T(8,128)(2,1)S(1)}, u32[]{:S(2)}, u32[]{:S(2)}) %collective-permute-start.5) | collective-permute-done | bytes 131104 | tf_op jit(solution)/shard_map/ppermute | solution.py:842
  19.9 7.2 %collective-permute-done.4.refs_4_ = bf16[256,256]{1,0:T(8,128)(2,1)S(1)} collective-permute-done((bf16[256,256]{1,0:T(8,128)(2,1)}, bf16[256,256]{1,0:T(8,128)(2,1)S(1)}, u32[]{:S(2)}, u32[]{:S(2)}) %collective-permute-start.4) | collective-permute-done | bytes 131104 | tf_op jit(solution)/shard_map/ppermute | solution.py:842
  28.8 1.9 %collective-permute-start.1 = (bf16[256,256]{1,0:T(8,128)(2,1)}, bf16[256,256]{1,0:T(8,128)(2,1)S(1)}, u32[]{:S(2)}, u32[]{:S(2)}) collective-permute-start(bf16[256,256]{1,0:T(8,128)(2,1)} %get-tuple-element.60), channel_id=1, source_target_pairs={{0,2},{1,3},{2,0},{3,1},{4,6},{5,7},{6,4},{7,5},{8,10},{9,11},{10,... | collective-permute-start | bytes 393224 | tf_op jit(solution)/shard_map/ppermute | solution.py:842
  32.3 2.8 %collective-permute-start.2 = (bf16[256,256]{1,0:T(8,128)(2,1)}, bf16[256,256]{1,0:T(8,128)(2,1)S(1)}, u32[]{:S(2)}, u32[]{:S(2)}) collective-permute-start(bf16[256,256]{1,0:T(8,128)(2,1)} %get-tuple-element.60), channel_id=1, source_target_pairs={{0,3},{1,0},{2,1},{3,2},{4,7},{5,4},{6,5},{7,6},{8,11},{9,8},{10,9... | collective-permute-start | bytes 393224 | tf_op jit(solution)/shard_map/ppermute | solution.py:842
  36.0 11.2 %attn_fwd.1 = (f32[1568,256]{1,0:T(8,128)}, bf16[8,2,3,112,256]{4,3,2,1,0:T(8,128)(2,1)}, bf16[8,2,448,256]{3,2,1,0:T(8,128)(2,1)}, bf16[1568,256]{1,0:T(8,128)(...) custom-call(s32[18]{0:T(128)S(1)} %pad_add_fusion.1.place, ...), custom_call_target="tpu_custom_call" | custom-call | flops 10000000000 | bytes 1048576 | tf_op jit(solution)/shard_map/attn_fwd/pallas_call | solution.py:713
  49.2 1.4 copy-done.8
  50.6 3.7 %ff_fwd.1 = (f32[1568,256]{1,0:T(8,128)S(1)}, bf16[4,256,256]{2,1,0:T(8,128)(2,1)}, bf16[256,1024]{1,0:T(8,128)(2,1)}) custom-call(s32[18]{0:T(128)S(1)} %pad_add_fusion.1.place, f32[1568,256]{1,0:T(8,128)S(1)} %copy-done.8, f32[32,256]{1,0:T(8,128)S(1)} %get-tuple-element.66.sm, bf16[2,256,256]{2,1,0:T(8,128)(2,1)S(1)} %copy-done.4, ...), custom_call_target="tpu_custom_call" | custom-call | flops 6000000000 | bytes 1048576 | tf_op jit(solution)/shard_map/ff_fwd/pallas_call | solution.py:729
  55.5 1.3 copy-done.1
  56.8 31.2 %top_block.1 = (bf16[1568,256]{1,0:T(8,128)(2,1)}, f32[1568,256]{1,0:T(8,128)S(1)}, bf16[8,4,112,256]{3,2,1,0:T(8,128)(2,1)}) custom-call(s32[18]{0:T(128)S(1)} %pad_add_fusion.1.place, f32[1568,256]{1,0:T(8,128)} %copy-done.10, bf16[1568,256]{1,0:T(8,128)(2,1)S(1)} %bitcast.70, bf16[2,192,256]{2,1,0:T(8,128)(2,1)S(1)} %bitcast.78, ...), custom_call_target="tpu_custom_call" | custom-call | flops 30000001024 | bytes 1048576 | tf_op jit(solution)/shard_map/top_block/pallas_call | solution.py:697
  88.0 1.1 copy-done.15
  90.4 1.4 copy-done.9
  91.8 1.5 copy-done.16
  93.4 7.6 %ff_bwd.1 = (f32[1568,256]{1,0:T(8,128)S(1)}, bf16[4,4,64,256]{3,2,1,0:T(8,128)(2,1)S(1)}, bf16[4,4,64,256]{3,2,1,0:T(8,128)(2,1)S(1)}, f32[32,8,256]{2,1,0:T(8,128)S(1)}) custom-call(s32[4]{0:T(128)S(1)} %copy-done, f32[1568,256]{1,0:T(8,128)S(1)} %copy-done.16, f32[1568,256]{1,0:T(8,128)S(1)} %copy-done.9, bf16[4,256,256]{2,1,0:T(8,128)(2,1)S(1)} %copy-done.17, ...), custom_call_target="tpu_custom_call" | custom-call | flops 10000000000 | bytes 1048576 | tf_op jit(solution)/shard_map/ff_bwd/pallas_call | solution.py:756
  101.2 13.6 %attn_bwd.1 = (bf16[1568,256]{1,0:T(8,128)(2,1)}, bf16[1,4,144,256]{3,2,1,0:T(8,128)(2,1)S(1)}, bf16[1,4,144,256]{3,2,1,0:T(8,128)(2,1)S(1)}) custom-call(s32[4]{0:T(128)S(1)} %copy-done, f32[1568,256]{1,0:T(8,128)S(1)} %get-tuple-element.76.grad, bf16[1568,256]{1,0:T(8,128)(2,1)S(1)} %bitcast.72, bf16[8,2,3,112,256]{4,3,2,1,0:T(8,128)(2,1)S(1)} %copy-done.14, ...), custom_call_target="tpu_custom_call" | custom-call | flops 16000000000 | bytes 1048576 | tf_op jit(solution)/shard_map/attn_bwd/pallas_call | solution.py:772
  116.6 1.6 collective-permute-start.15
  118.2 2.2 %collective-permute-start.16 = (bf16[144,256]{1,0:T(8,128)(2,1)S(1)}, bf16[144,256]{1,0:T(8,128)(2,1)S(1)}, u32[]{:S(2)}, u32[]{:S(2)}) collective-permute-start(bf16[144,256]{1,0:T(8,128)(2,1)S(1)} %get-tuple-element.120), channel_id=1, source_target_pairs={{0,3},{1,0},{2,1},{3,2},{4,7},{5,4},{6,5},{7,6},{8,11},{9,8},{10,9... | collective-permute-start | bytes 221192 | tf_op jit(solution)/shard_map/ppermute | solution.py:842
  120.5 1.4 collective-permute-start.17
  122.0 1.5 collective-permute-start.18
  123.6 2.4 %collective-permute-start.19 = (bf16[4,64,256]{2,1,0:T(8,128)(2,1)S(1)}, bf16[4,64,256]{2,1,0:T(8,128)(2,1)S(1)}, u32[]{:S(2)}, u32[]{:S(2)}) collective-permute-start(bf16[4,64,256]{2,1,0:T(8,128)(2,1)S(1)} %get-tuple-element.112), channel_id=1, source_target_pairs={{0,24},{4,28},{8,16},{12,20},{16,8},{20,12},{24,0},{28,4},{1,25},{... | collective-permute-start | bytes 393224 | tf_op jit(solution)/shard_map/ppermute | solution.py:847
  126.0 3.1 %collective-permute-done.17 = bf16[4,64,256]{2,1,0:T(8,128)(2,1)S(1)} collective-permute-done((bf16[4,64,256]{2,1,0:T(8,128)(2,1)S(1)}, bf16[4,64,256]{2,1,0:T(8,128)(2,1)S(1)}, u32[]{:S(2)}, u32[]{:S(2)}) %collective-permute-start.17) | collective-permute-done | bytes 131104 | tf_op jit(solution)/shard_map/ppermute | solution.py:847
  129.1 3.0 %collective-permute-done.18 = bf16[4,64,256]{2,1,0:T(8,128)(2,1)S(1)} collective-permute-done((bf16[4,64,256]{2,1,0:T(8,128)(2,1)S(1)}, bf16[4,64,256]{2,1,0:T(8,128)(2,1)S(1)}, u32[]{:S(2)}, u32[]{:S(2)}) %collective-permute-start.18) | collective-permute-done | bytes 131104 | tf_op jit(solution)/shard_map/ppermute | solution.py:847
  133.1 1.5 collective-permute-start.20
  135.4 2.4 %collective-permute-start.22 = (bf16[176,256]{1,0:T(8,128)(2,1)S(1)}, bf16[176,256]{1,0:T(8,128)(2,1)S(1)}, u32[]{:S(2)}, u32[]{:S(2)}) collective-permute-start(bf16[176,256]{1,0:T(8,128)(2,1)S(1)} %get-tuple-element.118), channel_id=1, source_target_pairs={{0,3},{1,0},{2,1},{3,2},{4,7},{5,4},{6,5},{7,6},{8,11},{9,8},{10,9... | collective-permute-start | bytes 270344 | tf_op jit(solution)/shard_map/ppermute | solution.py:842
  137.8 2.5 %collective-permute-done.20 = bf16[176,256]{1,0:T(8,128)(2,1)S(1)} collective-permute-done((bf16[176,256]{1,0:T(8,128)(2,1)S(1)}, bf16[176,256]{1,0:T(8,128)(2,1)S(1)}, u32[]{:S(2)}, u32[]{:S(2)}) %collective-permute-start.20) | collective-permute-done | bytes 90144 | tf_op jit(solution)/shard_map/ppermute | solution.py:842
  140.4 2.4 %collective-permute-done.21 = bf16[176,256]{1,0:T(8,128)(2,1)S(1)} collective-permute-done((bf16[176,256]{1,0:T(8,128)(2,1)S(1)}, bf16[176,256]{1,0:T(8,128)(2,1)S(1)}, u32[]{:S(2)}, u32[]{:S(2)}) %collective-permute-start.21) | collective-permute-done | bytes 90144 | tf_op jit(solution)/shard_map/ppermute | solution.py:842
  143.7 1.7 %collective-permute-start.23 = (bf16[320,256]{1,0:T(8,128)(2,1)S(1)}, bf16[320,256]{1,0:T(8,128)(2,1)S(1)}, u32[]{:S(2)}, u32[]{:S(2)}) collective-permute-start(bf16[320,256]{1,0:T(8,128)(2,1)S(1)} %pad_maximum_fusion.1.refs_0_), channel_id=1, source_target_pairs={{0,8},{4,12},{8,0},{12,4},{16,24},{20,28},{24,16},{28,20},{1,9},{5... | collective-permute-start | bytes 491528 | tf_op jit(solution)/shard_map/ppermute | solution.py:847
  146.0 1.2 collective-permute-start.25
  147.2 3.3 %collective-permute-done.23.refs_1_ = bf16[320,256]{1,0:T(8,128)(2,1)S(1)} collective-permute-done((bf16[320,256]{1,0:T(8,128)(2,1)S(1)}, bf16[320,256]{1,0:T(8,128)(2,1)S(1)}, u32[]{:S(2)}, u32[]{:S(2)}) %collective-permute-start.23) | collective-permute-done | bytes 163872 | tf_op jit(solution)/shard_map/ppermute | solution.py:847
  150.5 3.7 %collective-permute-done.24.refs_2_ = bf16[320,256]{1,0:T(8,128)(2,1)S(1)} collective-permute-done((bf16[320,256]{1,0:T(8,128)(2,1)S(1)}, bf16[320,256]{1,0:T(8,128)(2,1)S(1)}, u32[]{:S(2)}, u32[]{:S(2)}) %collective-permute-start.24) | collective-permute-done | bytes 163872 | tf_op jit(solution)/shard_map/ppermute | solution.py:847
  155.9 2.1 %unpack.1 = (f32[2,192,256]{2,1,0:T(8,128)}, f32[2,64,256]{2,1,0:T(8,128)}, f32[2,256,256]{2,1,0:T(8,128)}, f32[2,64,1024]{2,1,0:T(8,128)}, f32[2,2,64]{2,1,0:T(...) custom-call(s32[4]{0:T(128)S(1)} %copy-done, ...), custom_call_target="tpu_custom_call" | custom-call | flops 2000000000 | bytes 1048576 | tf_op jit(solution)/shard_map/unpack/pallas_call | solution.py:697
  (109 shorter events, 17.1 us)
Async XLA Ops:
  7.2 48.3 %all-gather.3.cloned.1.call-start = ((), (), s32[]{:S(2)}) async-start(), calls=%async_computation.2 | async-start | bytes 1548288 | tf_op jit(solution)/shard_map/all_gather | solution.py:966
  10.7 9.3 %collective-permute-start.5 = (bf16[256,256]{1,0:T(8,128)(2,1)}, bf16[256,256]{1,0:T(8,128)(2,1)S(1)}, u32[]{:S(2)}, u32[]{:S(2)}) collective-permute-start(bf16[256,256]{1,0:T(8,128)(2,1)} %get-tuple-element.61), channel_id=1, source_target_pairs={{0,3},{1,0},{2,1},{3,2},{4,7},{5,4},{6,5},{7,6},{8,11},{9,8},{10,9... | collective-permute-start | bytes 393224 | tf_op jit(solution)/shard_map/ppermute | solution.py:842
  15.7 11.4 %collective-permute-start.4 = (bf16[256,256]{1,0:T(8,128)(2,1)}, bf16[256,256]{1,0:T(8,128)(2,1)S(1)}, u32[]{:S(2)}, u32[]{:S(2)}) collective-permute-start(bf16[256,256]{1,0:T(8,128)(2,1)} %get-tuple-element.61), channel_id=1, source_target_pairs={{0,2},{1,3},{2,0},{3,1},{4,6},{5,7},{6,4},{7,5},{8,10},{9,11},{10,... | collective-permute-start | bytes 393224 | tf_op jit(solution)/shard_map/ppermute | solution.py:842
  15.7 11.4 %collective-permute-start.3 = (bf16[256,256]{1,0:T(8,128)(2,1)}, bf16[256,256]{1,0:T(8,128)(2,1)S(1)}, u32[]{:S(2)}, u32[]{:S(2)}) collective-permute-start(bf16[256,256]{1,0:T(8,128)(2,1)} %get-tuple-element.61), channel_id=1, source_target_pairs={{0,1},{1,2},{2,3},{3,0},{4,5},{5,6},{6,7},{7,4},{8,9},{9,10},{10,1... | collective-permute-start | bytes 393224 | tf_op jit(solution)/shard_map/ppermute | solution.py:842
  27.9 104.3 %reduce-scatter.2.cloned.1.call-start = ((), (), s32[]{:S(2)}) async-start(), calls=%async_computation.1 | async-start | bytes 2064384 | tf_op jit(solution)/shard_map/reduce_scatter | solution.py:972
  27.9 19.3 %collective-permute-start = (bf16[256,256]{1,0:T(8,128)(2,1)}, bf16[256,256]{1,0:T(8,128)(2,1)S(1)}, u32[]{:S(2)}, u32[]{:S(2)}) collective-permute-start(bf16[256,256]{1,0:T(8,128)(2,1)} %get-tuple-element.60), channel_id=1, source_target_pairs={{0,1},{1,2},{2,3},{3,0},{4,5},{5,6},{6,7},{7,4},{8,9},{9,10},{10,1... | collective-permute-start | bytes 393224 | tf_op jit(solution)/shard_map/ppermute | solution.py:842
  28.8 18.4 %collective-permute-start.1 = (bf16[256,256]{1,0:T(8,128)(2,1)}, bf16[256,256]{1,0:T(8,128)(2,1)S(1)}, u32[]{:S(2)}, u32[]{:S(2)}) collective-permute-start(bf16[256,256]{1,0:T(8,128)(2,1)} %get-tuple-element.60), channel_id=1, source_target_pairs={{0,2},{1,3},{2,0},{3,1},{4,6},{5,7},{6,4},{7,5},{8,10},{9,11},{10,... | collective-permute-start | bytes 393224 | tf_op jit(solution)/shard_map/ppermute | solution.py:842
  30.9 1.4 collective-permute-start.6
  31.0 4.2 %collective-permute-start.7 = (bf16[256,256]{1,0:T(8,128)(2,1)S(1)}, bf16[256,256]{1,0:T(8,128)(2,1)S(1)}, u32[]{:S(2)}, u32[]{:S(2)}) collective-permute-start(bf16[256,256]{1,0:T(8,128)(2,1)S(1)} %collective-permute-done.4.refs_4_), channel_id=1, source_target_pairs={{0,4},{4,0},{8,12},{12,8},{16,20},{20,16},{24,28},{28,24},{1,5},{5... | collective-permute-start | bytes 393224 | tf_op jit(solution)/shard_map/ppermute | solution.py:847
  31.5 3.7 %collective-permute-start.8 = (bf16[256,256]{1,0:T(8,128)(2,1)S(1)}, bf16[256,256]{1,0:T(8,128)(2,1)S(1)}, u32[]{:S(2)}, u32[]{:S(2)}) collective-permute-start(bf16[256,256]{1,0:T(8,128)(2,1)S(1)} %collective-permute-done.5.refs_5_), channel_id=1, source_target_pairs={{0,4},{4,0},{8,12},{12,8},{16,20},{20,16},{24,28},{28,24},{1,5},{5... | collective-permute-start | bytes 393224 | tf_op jit(solution)/shard_map/ppermute | solution.py:847
  32.3 14.9 %collective-permute-start.2 = (bf16[256,256]{1,0:T(8,128)(2,1)}, bf16[256,256]{1,0:T(8,128)(2,1)S(1)}, u32[]{:S(2)}, u32[]{:S(2)}) collective-permute-start(bf16[256,256]{1,0:T(8,128)(2,1)} %get-tuple-element.60), channel_id=1, source_target_pairs={{0,3},{1,0},{2,1},{3,2},{4,7},{5,4},{6,5},{7,6},{8,11},{9,8},{10,9... | collective-permute-start | bytes 393224 | tf_op jit(solution)/shard_map/ppermute | solution.py:842
  47.2 1.4 collective-permute-start.10
  47.3 1.5 collective-permute-start.11
  47.8 1.4 collective-permute-start.9
  101.0 13.8 %collective-permute-start.12 = (bf16[4,4,64,256]{3,2,1,0:T(8,128)(2,1)S(1)}, bf16[4,4,64,256]{3,2,1,0:T(8,128)(2,1)S(1)}, u32[]{:S(2)}, u32[]{:S(2)}) collective-permute-start(bf16[4,4,64,256]{3,2,1,0:T(8,128)(2,1)S(1)} %get-tuple-element.85), channel_id=1, source_target_pairs={{0,4},{4,0},{8,12},{12,8},{16,20},{20,16},{24,28},{28,24},{1,5},{5... | collective-permute-start | bytes 1572872 | tf_op jit(solution)/shard_map/ppermute | solution.py:847
  114.8 1.6 collective-permute-start.13
  116.6 7.1 %collective-permute-start.14 = (bf16[144,256]{1,0:T(8,128)(2,1)S(1)}, bf16[144,256]{1,0:T(8,128)(2,1)S(1)}, u32[]{:S(2)}, u32[]{:S(2)}) collective-permute-start(bf16[144,256]{1,0:T(8,128)(2,1)S(1)} %get-tuple-element.119), channel_id=1, source_target_pairs={{0,1},{1,2},{2,3},{3,0},{4,5},{5,6},{6,7},{7,4},{8,9},{9,10},{10,1... | collective-permute-start | bytes 221192 | tf_op jit(solution)/shard_map/ppermute | solution.py:842
  116.6 9.3 %collective-permute-start.15 = (bf16[144,256]{1,0:T(8,128)(2,1)S(1)}, bf16[144,256]{1,0:T(8,128)(2,1)S(1)}, u32[]{:S(2)}, u32[]{:S(2)}) collective-permute-start(bf16[144,256]{1,0:T(8,128)(2,1)S(1)} %get-tuple-element.121), channel_id=1, source_target_pairs={{0,2},{1,3},{2,0},{3,1},{4,6},{5,7},{6,4},{7,5},{8,10},{9,11},{10,... | collective-permute-start | bytes 221192 | tf_op jit(solution)/shard_map/ppermute | solution.py:842
  118.2 7.8 %collective-permute-start.16 = (bf16[144,256]{1,0:T(8,128)(2,1)S(1)}, bf16[144,256]{1,0:T(8,128)(2,1)S(1)}, u32[]{:S(2)}, u32[]{:S(2)}) collective-permute-start(bf16[144,256]{1,0:T(8,128)(2,1)S(1)} %get-tuple-element.120), channel_id=1, source_target_pairs={{0,3},{1,0},{2,1},{3,2},{4,7},{5,4},{6,5},{7,6},{8,11},{9,8},{10,9... | collective-permute-start | bytes 221192 | tf_op jit(solution)/shard_map/ppermute | solution.py:842
  120.5 8.6 %collective-permute-start.17 = (bf16[4,64,256]{2,1,0:T(8,128)(2,1)S(1)}, bf16[4,64,256]{2,1,0:T(8,128)(2,1)S(1)}, u32[]{:S(2)}, u32[]{:S(2)}) collective-permute-start(bf16[4,64,256]{2,1,0:T(8,128)(2,1)S(1)} %get-tuple-element.114), channel_id=1, source_target_pairs={{0,8},{4,12},{8,0},{12,4},{16,24},{20,28},{24,16},{28,20},{1,9},{5... | collective-permute-start | bytes 393224 | tf_op jit(solution)/shard_map/ppermute | solution.py:847
  122.0 10.2 %collective-permute-start.18 = (bf16[4,64,256]{2,1,0:T(8,128)(2,1)S(1)}, bf16[4,64,256]{2,1,0:T(8,128)(2,1)S(1)}, u32[]{:S(2)}, u32[]{:S(2)}) collective-permute-start(bf16[4,64,256]{2,1,0:T(8,128)(2,1)S(1)} %get-tuple-element.113), channel_id=1, source_target_pairs={{0,16},{4,20},{8,24},{12,28},{16,0},{20,4},{24,8},{28,12},{1,17},{... | collective-permute-start | bytes 393224 | tf_op jit(solution)/shard_map/ppermute | solution.py:847
  123.6 8.5 %collective-permute-start.19 = (bf16[4,64,256]{2,1,0:T(8,128)(2,1)S(1)}, bf16[4,64,256]{2,1,0:T(8,128)(2,1)S(1)}, u32[]{:S(2)}, u32[]{:S(2)}) collective-permute-start(bf16[4,64,256]{2,1,0:T(8,128)(2,1)S(1)} %get-tuple-element.112), channel_id=1, source_target_pairs={{0,24},{4,28},{8,16},{12,20},{16,8},{20,12},{24,0},{28,4},{1,25},{... | collective-permute-start | bytes 393224 | tf_op jit(solution)/shard_map/ppermute | solution.py:847
  133.1 7.2 %collective-permute-start.20 = (bf16[176,256]{1,0:T(8,128)(2,1)S(1)}, bf16[176,256]{1,0:T(8,128)(2,1)S(1)}, u32[]{:S(2)}, u32[]{:S(2)}) collective-permute-start(bf16[176,256]{1,0:T(8,128)(2,1)S(1)} %get-tuple-element.116), channel_id=1, source_target_pairs={{0,1},{1,2},{2,3},{3,0},{4,5},{5,6},{6,7},{7,4},{8,9},{9,10},{10,1... | collective-permute-start | bytes 270344 | tf_op jit(solution)/shard_map/ppermute | solution.py:842
  134.6 8.2 %collective-permute-start.21 = (bf16[176,256]{1,0:T(8,128)(2,1)S(1)}, bf16[176,256]{1,0:T(8,128)(2,1)S(1)}, u32[]{:S(2)}, u32[]{:S(2)}) collective-permute-start(bf16[176,256]{1,0:T(8,128)(2,1)S(1)} %get-tuple-element.117), channel_id=1, source_target_pairs={{0,2},{1,3},{2,0},{3,1},{4,6},{5,7},{6,4},{7,5},{8,10},{9,11},{10,... | collective-permute-start | bytes 270344 | tf_op jit(solution)/shard_map/ppermute | solution.py:842
  135.4 7.3 %collective-permute-start.22 = (bf16[176,256]{1,0:T(8,128)(2,1)S(1)}, bf16[176,256]{1,0:T(8,128)(2,1)S(1)}, u32[]{:S(2)}, u32[]{:S(2)}) collective-permute-start(bf16[176,256]{1,0:T(8,128)(2,1)S(1)} %get-tuple-element.118), channel_id=1, source_target_pairs={{0,3},{1,0},{2,1},{3,2},{4,7},{5,4},{6,5},{7,6},{8,11},{9,8},{10,9... | collective-permute-start | bytes 270344 | tf_op jit(solution)/shard_map/ppermute | solution.py:842
  143.7 6.9 %collective-permute-start.23 = (bf16[320,256]{1,0:T(8,128)(2,1)S(1)}, bf16[320,256]{1,0:T(8,128)(2,1)S(1)}, u32[]{:S(2)}, u32[]{:S(2)}) collective-permute-start(bf16[320,256]{1,0:T(8,128)(2,1)S(1)} %pad_maximum_fusion.1.refs_0_), channel_id=1, source_target_pairs={{0,8},{4,12},{8,0},{12,4},{16,24},{20,28},{24,16},{28,20},{1,9},{5... | collective-permute-start | bytes 491528 | tf_op jit(solution)/shard_map/ppermute | solution.py:847
  145.4 8.8 %collective-permute-start.24 = (bf16[320,256]{1,0:T(8,128)(2,1)S(1)}, bf16[320,256]{1,0:T(8,128)(2,1)S(1)}, u32[]{:S(2)}, u32[]{:S(2)}) collective-permute-start(bf16[320,256]{1,0:T(8,128)(2,1)S(1)} %pad_maximum_fusion.1.refs_0_), channel_id=1, source_target_pairs={{0,16},{4,20},{8,24},{12,28},{16,0},{20,4},{24,8},{28,12},{1,17},{... | collective-permute-start | bytes 491528 | tf_op jit(solution)/shard_map/ppermute | solution.py:847
  146.0 8.2 %collective-permute-start.25 = (bf16[320,256]{1,0:T(8,128)(2,1)S(1)}, bf16[320,256]{1,0:T(8,128)(2,1)S(1)}, u32[]{:S(2)}, u32[]{:S(2)}) collective-permute-start(bf16[320,256]{1,0:T(8,128)(2,1)S(1)} %pad_maximum_fusion.1.refs_0_), channel_id=1, source_target_pairs={{0,24},{4,28},{8,16},{12,20},{16,8},{20,12},{24,0},{28,4},{1,25},{... | collective-permute-start | bytes 491528 | tf_op jit(solution)/shard_map/ppermute | solution.py:847
  147.2 7.5 %collective-permute-start.26 = (bf16[320,256]{1,0:T(8,128)(2,1)S(1)}, bf16[320,256]{1,0:T(8,128)(2,1)S(1)}, u32[]{:S(2)}, u32[]{:S(2)}) collective-permute-start(bf16[320,256]{1,0:T(8,128)(2,1)S(1)} %pad_maximum_fusion.1.refs_0_), channel_id=1, source_target_pairs={{0,4},{4,0},{8,12},{12,8},{16,20},{20,16},{24,28},{28,24},{1,5},{5... | collective-permute-start | bytes 491528 | tf_op jit(solution)/shard_map/ppermute | solution.py:847
  150.5 4.2 %collective-permute-start.27 = (bf16[320,256]{1,0:T(8,128)(2,1)S(1)}, bf16[320,256]{1,0:T(8,128)(2,1)S(1)}, u32[]{:S(2)}, u32[]{:S(2)}) collective-permute-start(bf16[320,256]{1,0:T(8,128)(2,1)S(1)} %collective-permute-done.23.refs_1_), channel_id=1, source_target_pairs={{0,4},{4,0},{8,12},{12,8},{16,20},{20,16},{24,28},{28,24},{1,5},{5... | collective-permute-start | bytes 491528 | tf_op jit(solution)/shard_map/ppermute | solution.py:847
  154.2 1.4 collective-permute-start.28
  154.2 1.6 collective-permute-start.29
  (24 other events, 199.8 us)
Sparse Core Ops, SparseCore 0:
  28.0 25.1 all-gather.2
  89.3 41.5 reduce-scatter.1

commit v2 on v1

--- a/solution.py
+++ b/solution.py
@@ -382,9 +382,11 @@
     lax.fori_loop(0, GRID, line, 0)
 
 
-def mixer(x, mixed, wm, sm, middle):
+def mixer(x, mixed, wm, sm, *outs):
     for rows in chunks():
-        middle[rows, :] = x[rows, :].astype(f32) + (dot_nt(mixed[rows, :], wm[...]) + sm[BRANCH : BRANCH + 1])
+        middle = x[rows, :].astype(f32) + (dot_nt(mixed[rows, :], wm[...]) + sm[BRANCH : BRANCH + 1])
+        for out in outs:
+            out[rows, :] = middle
 
 
 def hidden(a2, we, sm, s):
@@ -541,7 +543,7 @@
 
 def attn_fwd_kernel(place, x, *refs):
     own, near, far = refs[0:3], refs[3:6], refs[6:9]
-    middle, packed, probs, mixed, value, wqkv, wm, sm, qkv, out, masks = refs[9:]
+    middle, again, packed, probs, mixed, value, wqkv, wm, sm, qkv, out, masks = refs[9:]
 
     @first_step
     def _():
@@ -557,7 +559,7 @@
         mix(out, qkv, (2, 5), sm, mixed)
         for orient in range(2):
             value[orient] = qkv[orient * 3 + 2, :ROWS, :].astype(bf16)
-        mixer(x, mixed, wm, sm, middle)
+        mixer(x, mixed, wm, sm, middle, again)
 
 
 def ff_fwd_kernel(place, middle, sm, *refs):
@@ -716,10 +718,10 @@
             num_scalar_prefetch=1,
             grid=(CROPS // STEP_CROPS,),
             in_specs=[whole((ROWS, D))] + attn_specs(0) + half_specs(rows),
-            out_specs=[whole((ROWS, D)), crop_spec(2, 3, WIN, 256), crop_spec(2, 4 * WIN, 256), whole((ROWS, D)), whole((2, ROWS, 128)), whole((768, D)), whole((D, D)), whole((32, D))],
+            out_specs=[whole((ROWS, D)), whole((ROWS, D)), crop_spec(2, 3, WIN, 256), crop_spec(2, 4 * WIN, 256), whole((ROWS, D)), whole((2, ROWS, 128)), whole((768, D)), whole((D, D)), whole((32, D))],
             scratch_shapes=[v((6, HELD, 128), f32), v((2, HELD, 128), f32), v((HALF_HEADS, WIN, 256), bf16)],
         ),
-        out_shape=[far((ROWS, D), f32), far((CROPS, 2, 3, WIN, 256)), far((CROPS, 2, 4 * WIN, 256)), far((ROWS, D)), far((2, ROWS, 128)), far((768, D)), far((D, D)), shape((32, D), f32)],
+        out_shape=[shape((ROWS, D), f32), far((ROWS, D), f32), far((CROPS, 2, 3, WIN, 256)), far((CROPS, 2, 4 * WIN, 256)), far((ROWS, D)), far((2, ROWS, 128)), far((768, D)), far((D, D)), shape((32, D), f32)],
         name="attn_fwd",
         **params(10, 20),
     )(place, x, *unit)
@@ -764,7 +766,7 @@
         ),
         out_shape=[shape((ROWS, D), f32)] + [shape((parts, 4, r, D))] * 2 + [shape((32, CROPS, D), f32)],
         name="ff_bwd",
-        **params(10, 20),
+        **params(10, 50),
     )(place, grad, middle, we, wr, sm)
 
 
@@ -964,14 +966,14 @@
     x, top_grad = to_rows(patches), to_rows(cotangent)
     near_1, x = lax.optimization_barrier((near_1, x))
     rest_1 = lax.all_gather(near_1, "dp", axis=0, tiled=False)
-    middle, packed, probs, mixed, value, wqkv, wm, sm = attn_fwd_call(sizes, x, attn_own + near_a0 + far_a0)
+    middle, again, packed, probs, mixed, value, wqkv, wm, sm = attn_fwd_call(sizes, x, attn_own + near_a0 + far_a0)
     near_f0, middle = lax.optimization_barrier((near_f0, middle))
     far_f0 = swap_core(near_f0)
     state, we, wr = ff_fwd_call(sizes, middle, sm, ff_own + near_f0 + far_f0)
     output, grad, grads_1 = top_call(sizes, state, top_grad, attn_own + ff_own + [rest_1], dp, r_t)
     sums_1 = lax.psum_scatter(grads_1, "dp", scatter_dimension=0, tiled=False)
 
-    grad_mid, keep_f, give_f, vec = ff_bwd_call(place, grad, middle, we, wr, sm, planes, r_f)
+    grad_mid, keep_f, give_f, vec = ff_bwd_call(place, grad, again, we, wr, sm, planes, r_f)
     got_f = swap_dp(give_f, 1)
     patch_grad, keep_a, give_a = attn_bwd_call(place, grad_mid, x, packed, probs, mixed, value, wqkv, wm, sm, vec)
     got_f, keep_a, give_a = lax.optimization_barrier((got_f, keep_a, give_a))

time: 165 us -> 164 us (level)
  local copies, waits for them, and re-layouts: 10.2 us -> 6.98 us
  Pallas kernels: 72.3 us -> 74 us
    unnamed x48 -> x42, local copies, waits for them, and re-layouts: 10 us -> 6.74 us
  transfers between devices with their start and end apart: 32 -> 32, of which waited for: 16 -> 16; matrix products, arithmetic and copies ran while one was open for 1% -> 1% of each run, Pallas kernels for 22% -> 23%
where the time goes in v2:
time: 164 us; the launch traced here: 163 us
  Pallas kernels  74 us (45%)
  starting transfers between devices  32.6 us (20%)
  waiting for transfers between devices  31.8 us (19%)
  between operations  14.3 us (9%)
  local copies, waits for them, and re-layouts  6.98 us (4%)
  other arithmetic  3.75 us (2%)
    pallas_call x2, Pallas kernels, held_call(): pl.pallas_call(kernel, in_specs=[pl.BlockSpec(memory_space=pltpu.SMEM)] +...  33.3 us
    ppermute x12, starting transfers between devices, turn_mp(): return lax.ppermute(x, 'mp', [(i, (i + k) % n) for i in range(n)])  21.7 us
    ppermute x18, waiting for transfers between devices, swap_dp(): return lax.ppermute(x, 'dp', [(i, i ^ bits) for i in range(n)])  16.7 us
    ppermute x12, waiting for transfers between devices, turn_mp(): return lax.ppermute(x, 'mp', [(i, (i + k) % n) for i in range(n)])  15.1 us
    pallas_call x1, Pallas kernels, attn_bwd_call(): pl.pallas_call(attn_bwd_kernel, grid_spec=pltpu.PrefetchScalarGridSpec(nu...  13.6 us
    pallas_call x1, Pallas kernels, attn_fwd_call(): pl.pallas_call(attn_fwd_kernel, grid_spec=pltpu.PrefetchScalarGridSpec(nu...  11.2 us
    ppermute x18, starting transfers between devices, swap_dp(): return lax.ppermute(x, 'dp', [(i, i ^ bits) for i in range(n)])  10.8 us
    pallas_call x1, Pallas kernels, ff_bwd_call(): pl.pallas_call(ff_bwd_kernel, grid_spec=pltpu.PrefetchScalarGridSpec(num_...  9.26 us
  transfers between devices with their start and end apart: 32, of which 16 were waited for; matrix products, arithmetic and copies ran while one was open for 1% of the time, Pallas kernels for 23%

profile of v2, /device:TPU:0, one launch (start us, length us, event | category | flops | bytes accessed | tf_op | source)
XLA Modules:
  0.0 163.4 jit_solution(5581356435981390309)
XLA Ops:
  7.8 2.8 %pack.1 = (bf16[256,256]{1,0:T(8,128)(2,1)}, bf16[256,256]{1,0:T(8,128)(2,1)}, bf16[2,32,256]{2,1,0:T(8,128)(2,1)}) custom-call(s32[4]{0:T(128)} %pad_add_fusion.2.place, bf16[2,192,256]{2,1,0:T(8,128)(2,1)} %bitcast.76, bf16[2,64,256]{2,1,0:T(8,128)(2,1)} %bitcast.79, bf16[2,2,64]{2,1,0:T(2,128)(2,1)} %gain.1, bf16[2,2,64]{2,1,0:T(2,128)(2,1)} %shift.1, ...), custom_call_target="tpu_custom_call" | custom-call | flops 1000000000 | bytes 1048576 | tf_op jit(solution)/shard_map/pack/pallas_call | solution.py:827
  10.7 5.0 %collective-permute-start.5 = (bf16[256,256]{1,0:T(8,128)(2,1)}, bf16[256,256]{1,0:T(8,128)(2,1)S(1)}, u32[]{:S(2)}, u32[]{:S(2)}) collective-permute-start(bf16[256,256]{1,0:T(8,128)(2,1)} %get-tuple-element.62), channel_id=1, source_target_pairs={{0,3},{1,0},{2,1},{3,2},{4,7},{5,4},{6,5},{7,6},{8,11},{9,8},{10,9... | collective-permute-start | bytes 393224 | tf_op jit(solution)/shard_map/ppermute | solution.py:844
  16.7 3.2 %collective-permute-done.5.refs_5_ = bf16[256,256]{1,0:T(8,128)(2,1)S(1)} collective-permute-done((bf16[256,256]{1,0:T(8,128)(2,1)}, bf16[256,256]{1,0:T(8,128)(2,1)S(1)}, u32[]{:S(2)}, u32[]{:S(2)}) %collective-permute-start.5) | collective-permute-done | bytes 131104 | tf_op jit(solution)/shard_map/ppermute | solution.py:844
  19.9 7.2 %collective-permute-done.4.refs_4_ = bf16[256,256]{1,0:T(8,128)(2,1)S(1)} collective-permute-done((bf16[256,256]{1,0:T(8,128)(2,1)}, bf16[256,256]{1,0:T(8,128)(2,1)S(1)}, u32[]{:S(2)}, u32[]{:S(2)}) %collective-permute-start.4) | collective-permute-done | bytes 131104 | tf_op jit(solution)/shard_map/ppermute | solution.py:844
  28.8 1.9 %collective-permute-start.1 = (bf16[256,256]{1,0:T(8,128)(2,1)}, bf16[256,256]{1,0:T(8,128)(2,1)S(1)}, u32[]{:S(2)}, u32[]{:S(2)}) collective-permute-start(bf16[256,256]{1,0:T(8,128)(2,1)} %get-tuple-element.61), channel_id=1, source_target_pairs={{0,2},{1,3},{2,0},{3,1},{4,6},{5,7},{6,4},{7,5},{8,10},{9,11},{10,... | collective-permute-start | bytes 393224 | tf_op jit(solution)/shard_map/ppermute | solution.py:844
  32.3 2.8 %collective-permute-start.2 = (bf16[256,256]{1,0:T(8,128)(2,1)}, bf16[256,256]{1,0:T(8,128)(2,1)S(1)}, u32[]{:S(2)}, u32[]{:S(2)}) collective-permute-start(bf16[256,256]{1,0:T(8,128)(2,1)} %get-tuple-element.61), channel_id=1, source_target_pairs={{0,3},{1,0},{2,1},{3,2},{4,7},{5,4},{6,5},{7,6},{8,11},{9,8},{10,9... | collective-permute-start | bytes 393224 | tf_op jit(solution)/shard_map/ppermute | solution.py:844
  36.0 11.2 %attn_fwd.1 = (f32[1568,256]{1,0:T(8,128)S(1)}, f32[1568,256]{1,0:T(8,128)}, bf16[8,2,3,112,256]{4,3,2,1,0:T(8,128)(2,1)}, bf16[8,2,448,256]{3,2,1,0:T(8,128)(2,...) custom-call(s32[18]{0:T(128)S(1)} %pad_add_fusion.1.place, ...), custom_call_target="tpu_custom_call" | custom-call | flops 10000000000 | bytes 1048576 | tf_op jit(solution)/shard_map/attn_fwd/pallas_call | solution.py:715
  49.2 3.7 %ff_fwd.1 = (f32[1568,256]{1,0:T(8,128)S(1)}, bf16[4,256,256]{2,1,0:T(8,128)(2,1)}, bf16[256,1024]{1,0:T(8,128)(2,1)}) custom-call(s32[18]{0:T(128)S(1)} %pad_add_fusion.1.place, f32[1568,256]{1,0:T(8,128)S(1)} %get-tuple-element.66.middle, f32[32,256]{1,0:T(8,128)S(1)} %get-tuple-element.67.sm, bf16[2,256,256]{2,1,0:T(8,128)(2,1)S(1)} %copy-done.4, ...), custom_call_target="tpu_custom_call" | custom-call | flops 6000000000 | bytes 1048576 | tf_op jit(solution)/shard_map/ff_fwd/pallas_call | solution.py:731
  52.9 1.1 copy-done.8
  54.0 1.3 copy-done.1
  55.4 31.2 %top_block.1 = (bf16[1568,256]{1,0:T(8,128)(2,1)}, f32[1568,256]{1,0:T(8,128)S(1)}, bf16[8,4,112,256]{3,2,1,0:T(8,128)(2,1)}) custom-call(s32[18]{0:T(128)S(1)} %pad_add_fusion.1.place, f32[1568,256]{1,0:T(8,128)} %copy-done.8, bf16[1568,256]{1,0:T(8,128)(2,1)S(1)} %bitcast.70, bf16[2,192,256]{2,1,0:T(8,128)(2,1)S(1)} %bitcast.78, ...), custom_call_target="tpu_custom_call" | custom-call | flops 30000001024 | bytes 1048576 | tf_op jit(solution)/shard_map/top_block/pallas_call | solution.py:699
  86.6 1.1 copy-done.13
  89.0 9.3 %ff_bwd.1 = (f32[1568,256]{1,0:T(8,128)S(1)}, bf16[4,4,64,256]{3,2,1,0:T(8,128)(2,1)S(1)}, bf16[4,4,64,256]{3,2,1,0:T(8,128)(2,1)S(1)}, f32[32,8,256]{2,1,0:T(8,128)S(1)}) custom-call(s32[4]{0:T(128)S(1)} %copy-done, f32[1568,256]{1,0:T(8,128)} %copy-done.13, f32[1568,256]{1,0:T(8,128)} %get-tuple-element.75.middle, bf16[4,256,256]{2,1,0:T(8,128)(2,1)S(1)} %copy-done.14, ...), custom_call_target="tpu_custom_call" | custom-call | flops 10000000000 | bytes 1048576 | tf_op jit(solution)/shard_map/ff_bwd/pallas_call | solution.py:758
  98.5 1.1 copy-done.17
  99.7 13.6 %attn_bwd.1 = (bf16[1568,256]{1,0:T(8,128)(2,1)}, bf16[1,4,144,256]{3,2,1,0:T(8,128)(2,1)S(1)}, bf16[1,4,144,256]{3,2,1,0:T(8,128)(2,1)S(1)}) custom-call(s32[4]{0:T(128)S(1)} %copy-done, f32[1568,256]{1,0:T(8,128)S(1)} %get-tuple-element.78.grad, bf16[1568,256]{1,0:T(8,128)(2,1)S(1)} %bitcast.72, bf16[8,2,3,112,256]{4,3,2,1,0:T(8,128)(2,1)S(1)} %copy-done.12, ...), custom_call_target="tpu_custom_call" | custom-call | flops 16000000000 | bytes 1048576 | tf_op jit(solution)/shard_map/attn_bwd/pallas_call | solution.py:774
  113.8 1.1 collective-permute-done.13
  115.8 2.4 %collective-permute-start.15 = (bf16[144,256]{1,0:T(8,128)(2,1)S(1)}, bf16[144,256]{1,0:T(8,128)(2,1)S(1)}, u32[]{:S(2)}, u32[]{:S(2)}) collective-permute-start(bf16[144,256]{1,0:T(8,128)(2,1)S(1)} %get-tuple-element.123), channel_id=1, source_target_pairs={{0,2},{1,3},{2,0},{3,1},{4,6},{5,7},{6,4},{7,5},{8,10},{9,11},{10,... | collective-permute-start | bytes 221192 | tf_op jit(solution)/shard_map/ppermute | solution.py:844
  118.2 1.4 collective-permute-start.16
  119.7 1.5 collective-permute-start.17
  122.1 2.5 %collective-permute-start.19 = (bf16[4,64,256]{2,1,0:T(8,128)(2,1)S(1)}, bf16[4,64,256]{2,1,0:T(8,128)(2,1)S(1)}, u32[]{:S(2)}, u32[]{:S(2)}) collective-permute-start(bf16[4,64,256]{2,1,0:T(8,128)(2,1)S(1)} %get-tuple-element.114), channel_id=1, source_target_pairs={{0,24},{4,28},{8,16},{12,20},{16,8},{20,12},{24,0},{28,4},{1,25},{... | collective-permute-start | bytes 393224 | tf_op jit(solution)/shard_map/ppermute | solution.py:849
  124.7 3.3 %collective-permute-done.17 = bf16[4,64,256]{2,1,0:T(8,128)(2,1)S(1)} collective-permute-done((bf16[4,64,256]{2,1,0:T(8,128)(2,1)S(1)}, bf16[4,64,256]{2,1,0:T(8,128)(2,1)S(1)}, u32[]{:S(2)}, u32[]{:S(2)}) %collective-permute-start.17) | collective-permute-done | bytes 131104 | tf_op jit(solution)/shard_map/ppermute | solution.py:849
  128.0 3.0 %collective-permute-done.18 = bf16[4,64,256]{2,1,0:T(8,128)(2,1)S(1)} collective-permute-done((bf16[4,64,256]{2,1,0:T(8,128)(2,1)S(1)}, bf16[4,64,256]{2,1,0:T(8,128)(2,1)S(1)}, u32[]{:S(2)}, u32[]{:S(2)}) %collective-permute-start.18) | collective-permute-done | bytes 131104 | tf_op jit(solution)/shard_map/ppermute | solution.py:849
  132.0 1.6 collective-permute-start.20
  133.6 1.0 collective-permute-start.21
  134.6 2.8 %collective-permute-start.22 = (bf16[176,256]{1,0:T(8,128)(2,1)S(1)}, bf16[176,256]{1,0:T(8,128)(2,1)S(1)}, u32[]{:S(2)}, u32[]{:S(2)}) collective-permute-start(bf16[176,256]{1,0:T(8,128)(2,1)S(1)} %get-tuple-element.120), channel_id=1, source_target_pairs={{0,3},{1,0},{2,1},{3,2},{4,7},{5,4},{6,5},{7,6},{8,11},{9,8},{10,9... | collective-permute-start | bytes 270344 | tf_op jit(solution)/shard_map/ppermute | solution.py:844
  137.4 1.7 %collective-permute-done.20 = bf16[176,256]{1,0:T(8,128)(2,1)S(1)} collective-permute-done((bf16[176,256]{1,0:T(8,128)(2,1)S(1)}, bf16[176,256]{1,0:T(8,128)(2,1)S(1)}, u32[]{:S(2)}, u32[]{:S(2)}) %collective-permute-start.20) | collective-permute-done | bytes 90144 | tf_op jit(solution)/shard_map/ppermute | solution.py:844
  139.1 2.9 %collective-permute-done.21 = bf16[176,256]{1,0:T(8,128)(2,1)S(1)} collective-permute-done((bf16[176,256]{1,0:T(8,128)(2,1)S(1)}, bf16[176,256]{1,0:T(8,128)(2,1)S(1)}, u32[]{:S(2)}, u32[]{:S(2)}) %collective-permute-start.21) | collective-permute-done | bytes 90144 | tf_op jit(solution)/shard_map/ppermute | solution.py:844
  143.6 1.4 collective-permute-start.24
  144.9 1.5 collective-permute-start.25
  146.5 3.2 %collective-permute-done.23.refs_1_ = bf16[320,256]{1,0:T(8,128)(2,1)S(1)} collective-permute-done((bf16[320,256]{1,0:T(8,128)(2,1)S(1)}, bf16[320,256]{1,0:T(8,128)(2,1)S(1)}, u32[]{:S(2)}, u32[]{:S(2)}) %collective-permute-start.23) | collective-permute-done | bytes 163872 | tf_op jit(solution)/shard_map/ppermute | solution.py:849
  149.7 3.2 %collective-permute-done.24.refs_2_ = bf16[320,256]{1,0:T(8,128)(2,1)S(1)} collective-permute-done((bf16[320,256]{1,0:T(8,128)(2,1)S(1)}, bf16[320,256]{1,0:T(8,128)(2,1)S(1)}, u32[]{:S(2)}, u32[]{:S(2)}) %collective-permute-start.24) | collective-permute-done | bytes 163872 | tf_op jit(solution)/shard_map/ppermute | solution.py:849
  154.5 2.1 %unpack.1 = (f32[2,192,256]{2,1,0:T(8,128)}, f32[2,64,256]{2,1,0:T(8,128)}, f32[2,256,256]{2,1,0:T(8,128)}, f32[2,64,1024]{2,1,0:T(8,128)}, f32[2,2,64]{2,1,0:T(...) custom-call(s32[4]{0:T(128)S(1)} %copy-done, ...), custom_call_target="tpu_custom_call" | custom-call | flops 2000000000 | bytes 1048576 | tf_op jit(solution)/shard_map/unpack/pallas_call | solution.py:699
  (103 shorter events, 15.6 us)
Async XLA Ops:
  7.2 46.9 %all-gather.3.cloned.1.call-start = ((), (), s32[]{:S(2)}) async-start(), calls=%async_computation.2 | async-start | bytes 1548288 | tf_op jit(solution)/shard_map/all_gather | solution.py:968
  10.7 9.3 %collective-permute-start.5 = (bf16[256,256]{1,0:T(8,128)(2,1)}, bf16[256,256]{1,0:T(8,128)(2,1)S(1)}, u32[]{:S(2)}, u32[]{:S(2)}) collective-permute-start(bf16[256,256]{1,0:T(8,128)(2,1)} %get-tuple-element.62), channel_id=1, source_target_pairs={{0,3},{1,0},{2,1},{3,2},{4,7},{5,4},{6,5},{7,6},{8,11},{9,8},{10,9... | collective-permute-start | bytes 393224 | tf_op jit(solution)/shard_map/ppermute | solution.py:844
  15.7 11.4 %collective-permute-start.4 = (bf16[256,256]{1,0:T(8,128)(2,1)}, bf16[256,256]{1,0:T(8,128)(2,1)S(1)}, u32[]{:S(2)}, u32[]{:S(2)}) collective-permute-start(bf16[256,256]{1,0:T(8,128)(2,1)} %get-tuple-element.62), channel_id=1, source_target_pairs={{0,2},{1,3},{2,0},{3,1},{4,6},{5,7},{6,4},{7,5},{8,10},{9,11},{10,... | collective-permute-start | bytes 393224 | tf_op jit(solution)/shard_map/ppermute | solution.py:844
  15.7 11.4 %collective-permute-start.3 = (bf16[256,256]{1,0:T(8,128)(2,1)}, bf16[256,256]{1,0:T(8,128)(2,1)S(1)}, u32[]{:S(2)}, u32[]{:S(2)}) collective-permute-start(bf16[256,256]{1,0:T(8,128)(2,1)} %get-tuple-element.62), channel_id=1, source_target_pairs={{0,1},{1,2},{2,3},{3,0},{4,5},{5,6},{6,7},{7,4},{8,9},{9,10},{10,1... | collective-permute-start | bytes 393224 | tf_op jit(solution)/shard_map/ppermute | solution.py:844
  27.9 103.1 %reduce-scatter.2.cloned.1.call-start = ((), (), s32[]{:S(2)}) async-start(), calls=%async_computation.1 | async-start | bytes 2064384 | tf_op jit(solution)/shard_map/reduce_scatter | solution.py:974
  27.9 19.3 %collective-permute-start = (bf16[256,256]{1,0:T(8,128)(2,1)}, bf16[256,256]{1,0:T(8,128)(2,1)S(1)}, u32[]{:S(2)}, u32[]{:S(2)}) collective-permute-start(bf16[256,256]{1,0:T(8,128)(2,1)} %get-tuple-element.61), channel_id=1, source_target_pairs={{0,1},{1,2},{2,3},{3,0},{4,5},{5,6},{6,7},{7,4},{8,9},{9,10},{10,1... | collective-permute-start | bytes 393224 | tf_op jit(solution)/shard_map/ppermute | solution.py:844
  28.8 18.4 %collective-permute-start.1 = (bf16[256,256]{1,0:T(8,128)(2,1)}, bf16[256,256]{1,0:T(8,128)(2,1)S(1)}, u32[]{:S(2)}, u32[]{:S(2)}) collective-permute-start(bf16[256,256]{1,0:T(8,128)(2,1)} %get-tuple-element.61), channel_id=1, source_target_pairs={{0,2},{1,3},{2,0},{3,1},{4,6},{5,7},{6,4},{7,5},{8,10},{9,11},{10,... | collective-permute-start | bytes 393224 | tf_op jit(solution)/shard_map/ppermute | solution.py:844
  30.9 1.4 collective-permute-start.6
  31.0 4.2 %collective-permute-start.7 = (bf16[256,256]{1,0:T(8,128)(2,1)S(1)}, bf16[256,256]{1,0:T(8,128)(2,1)S(1)}, u32[]{:S(2)}, u32[]{:S(2)}) collective-permute-start(bf16[256,256]{1,0:T(8,128)(2,1)S(1)} %collective-permute-done.4.refs_4_), channel_id=1, source_target_pairs={{0,4},{4,0},{8,12},{12,8},{16,20},{20,16},{24,28},{28,24},{1,5},{5... | collective-permute-start | bytes 393224 | tf_op jit(solution)/shard_map/ppermute | solution.py:849
  31.5 3.7 %collective-permute-start.8 = (bf16[256,256]{1,0:T(8,128)(2,1)S(1)}, bf16[256,256]{1,0:T(8,128)(2,1)S(1)}, u32[]{:S(2)}, u32[]{:S(2)}) collective-permute-start(bf16[256,256]{1,0:T(8,128)(2,1)S(1)} %collective-permute-done.5.refs_5_), channel_id=1, source_target_pairs={{0,4},{4,0},{8,12},{12,8},{16,20},{20,16},{24,28},{28,24},{1,5},{5... | collective-permute-start | bytes 393224 | tf_op jit(solution)/shard_map/ppermute | solution.py:849
  32.3 14.9 %collective-permute-start.2 = (bf16[256,256]{1,0:T(8,128)(2,1)}, bf16[256,256]{1,0:T(8,128)(2,1)S(1)}, u32[]{:S(2)}, u32[]{:S(2)}) collective-permute-start(bf16[256,256]{1,0:T(8,128)(2,1)} %get-tuple-element.61), channel_id=1, source_target_pairs={{0,3},{1,0},{2,1},{3,2},{4,7},{5,4},{6,5},{7,6},{8,11},{9,8},{10,9... | collective-permute-start | bytes 393224 | tf_op jit(solution)/shard_map/ppermute | solution.py:844
  47.2 1.4 collective-permute-start.10
  47.3 1.5 collective-permute-start.11
  47.8 1.3 collective-permute-start.9
  98.3 15.1 %collective-permute-start.12 = (bf16[4,4,64,256]{3,2,1,0:T(8,128)(2,1)S(1)}, bf16[4,4,64,256]{3,2,1,0:T(8,128)(2,1)S(1)}, u32[]{:S(2)}, u32[]{:S(2)}) collective-permute-start(bf16[4,4,64,256]{3,2,1,0:T(8,128)(2,1)S(1)} %get-tuple-element.87), channel_id=1, source_target_pairs={{0,4},{4,0},{8,12},{12,8},{16,20},{20,16},{24,28},{28,24},{1,5},{5... | collective-permute-start | bytes 1572872 | tf_op jit(solution)/shard_map/ppermute | solution.py:849
  113.3 1.6 collective-permute-start.13
  115.0 7.0 %collective-permute-start.14 = (bf16[144,256]{1,0:T(8,128)(2,1)S(1)}, bf16[144,256]{1,0:T(8,128)(2,1)S(1)}, u32[]{:S(2)}, u32[]{:S(2)}) collective-permute-start(bf16[144,256]{1,0:T(8,128)(2,1)S(1)} %get-tuple-element.121), channel_id=1, source_target_pairs={{0,1},{1,2},{2,3},{3,0},{4,5},{5,6},{6,7},{7,4},{8,9},{9,10},{10,1... | collective-permute-start | bytes 221192 | tf_op jit(solution)/shard_map/ppermute | solution.py:844
  115.8 8.8 %collective-permute-start.15 = (bf16[144,256]{1,0:T(8,128)(2,1)S(1)}, bf16[144,256]{1,0:T(8,128)(2,1)S(1)}, u32[]{:S(2)}, u32[]{:S(2)}) collective-permute-start(bf16[144,256]{1,0:T(8,128)(2,1)S(1)} %get-tuple-element.123), channel_id=1, source_target_pairs={{0,2},{1,3},{2,0},{3,1},{4,6},{5,7},{6,4},{7,5},{8,10},{9,11},{10,... | collective-permute-start | bytes 221192 | tf_op jit(solution)/shard_map/ppermute | solution.py:844
  118.2 6.4 %collective-permute-start.16 = (bf16[144,256]{1,0:T(8,128)(2,1)S(1)}, bf16[144,256]{1,0:T(8,128)(2,1)S(1)}, u32[]{:S(2)}, u32[]{:S(2)}) collective-permute-start(bf16[144,256]{1,0:T(8,128)(2,1)S(1)} %get-tuple-element.122), channel_id=1, source_target_pairs={{0,3},{1,0},{2,1},{3,2},{4,7},{5,4},{6,5},{7,6},{8,11},{9,8},{10,9... | collective-permute-start | bytes 221192 | tf_op jit(solution)/shard_map/ppermute | solution.py:844
  119.7 8.3 %collective-permute-start.17 = (bf16[4,64,256]{2,1,0:T(8,128)(2,1)S(1)}, bf16[4,64,256]{2,1,0:T(8,128)(2,1)S(1)}, u32[]{:S(2)}, u32[]{:S(2)}) collective-permute-start(bf16[4,64,256]{2,1,0:T(8,128)(2,1)S(1)} %get-tuple-element.116), channel_id=1, source_target_pairs={{0,8},{4,12},{8,0},{12,4},{16,24},{20,28},{24,16},{28,20},{1,9},{5... | collective-permute-start | bytes 393224 | tf_op jit(solution)/shard_map/ppermute | solution.py:849
  121.2 9.8 %collective-permute-start.18 = (bf16[4,64,256]{2,1,0:T(8,128)(2,1)S(1)}, bf16[4,64,256]{2,1,0:T(8,128)(2,1)S(1)}, u32[]{:S(2)}, u32[]{:S(2)}) collective-permute-start(bf16[4,64,256]{2,1,0:T(8,128)(2,1)S(1)} %get-tuple-element.115), channel_id=1, source_target_pairs={{0,16},{4,20},{8,24},{12,28},{16,0},{20,4},{24,8},{28,12},{1,17},{... | collective-permute-start | bytes 393224 | tf_op jit(solution)/shard_map/ppermute | solution.py:849
  122.1 8.9 %collective-permute-start.19 = (bf16[4,64,256]{2,1,0:T(8,128)(2,1)S(1)}, bf16[4,64,256]{2,1,0:T(8,128)(2,1)S(1)}, u32[]{:S(2)}, u32[]{:S(2)}) collective-permute-start(bf16[4,64,256]{2,1,0:T(8,128)(2,1)S(1)} %get-tuple-element.114), channel_id=1, source_target_pairs={{0,24},{4,28},{8,16},{12,20},{16,8},{20,12},{24,0},{28,4},{1,25},{... | collective-permute-start | bytes 393224 | tf_op jit(solution)/shard_map/ppermute | solution.py:849
  132.0 7.1 %collective-permute-start.20 = (bf16[176,256]{1,0:T(8,128)(2,1)S(1)}, bf16[176,256]{1,0:T(8,128)(2,1)S(1)}, u32[]{:S(2)}, u32[]{:S(2)}) collective-permute-start(bf16[176,256]{1,0:T(8,128)(2,1)S(1)} %get-tuple-element.118), channel_id=1, source_target_pairs={{0,1},{1,2},{2,3},{3,0},{4,5},{5,6},{6,7},{7,4},{8,9},{9,10},{10,1... | collective-permute-start | bytes 270344 | tf_op jit(solution)/shard_map/ppermute | solution.py:844
  133.6 8.5 %collective-permute-start.21 = (bf16[176,256]{1,0:T(8,128)(2,1)S(1)}, bf16[176,256]{1,0:T(8,128)(2,1)S(1)}, u32[]{:S(2)}, u32[]{:S(2)}) collective-permute-start(bf16[176,256]{1,0:T(8,128)(2,1)S(1)} %get-tuple-element.119), channel_id=1, source_target_pairs={{0,2},{1,3},{2,0},{3,1},{4,6},{5,7},{6,4},{7,5},{8,10},{9,11},{10,... | collective-permute-start | bytes 270344 | tf_op jit(solution)/shard_map/ppermute | solution.py:844
  134.6 7.4 %collective-permute-start.22 = (bf16[176,256]{1,0:T(8,128)(2,1)S(1)}, bf16[176,256]{1,0:T(8,128)(2,1)S(1)}, u32[]{:S(2)}, u32[]{:S(2)}) collective-permute-start(bf16[176,256]{1,0:T(8,128)(2,1)S(1)} %get-tuple-element.120), channel_id=1, source_target_pairs={{0,3},{1,0},{2,1},{3,2},{4,7},{5,4},{6,5},{7,6},{8,11},{9,8},{10,9... | collective-permute-start | bytes 270344 | tf_op jit(solution)/shard_map/ppermute | solution.py:844
  142.9 6.8 %collective-permute-start.23 = (bf16[320,256]{1,0:T(8,128)(2,1)S(1)}, bf16[320,256]{1,0:T(8,128)(2,1)S(1)}, u32[]{:S(2)}, u32[]{:S(2)}) collective-permute-start(bf16[320,256]{1,0:T(8,128)(2,1)S(1)} %pad_maximum_fusion.1.refs_0_), channel_id=1, source_target_pairs={{0,8},{4,12},{8,0},{12,4},{16,24},{20,28},{24,16},{28,20},{1,9},{5... | collective-permute-start | bytes 491528 | tf_op jit(solution)/shard_map/ppermute | solution.py:849
  143.6 9.3 %collective-permute-start.24 = (bf16[320,256]{1,0:T(8,128)(2,1)S(1)}, bf16[320,256]{1,0:T(8,128)(2,1)S(1)}, u32[]{:S(2)}, u32[]{:S(2)}) collective-permute-start(bf16[320,256]{1,0:T(8,128)(2,1)S(1)} %pad_maximum_fusion.1.refs_0_), channel_id=1, source_target_pairs={{0,16},{4,20},{8,24},{12,28},{16,0},{20,4},{24,8},{28,12},{1,17},{... | collective-permute-start | bytes 491528 | tf_op jit(solution)/shard_map/ppermute | solution.py:849
  144.9 7.9 %collective-permute-start.25 = (bf16[320,256]{1,0:T(8,128)(2,1)S(1)}, bf16[320,256]{1,0:T(8,128)(2,1)S(1)}, u32[]{:S(2)}, u32[]{:S(2)}) collective-permute-start(bf16[320,256]{1,0:T(8,128)(2,1)S(1)} %pad_maximum_fusion.1.refs_0_), channel_id=1, source_target_pairs={{0,24},{4,28},{8,16},{12,20},{16,8},{20,12},{24,0},{28,4},{1,25},{... | collective-permute-start | bytes 491528 | tf_op jit(solution)/shard_map/ppermute | solution.py:849
  146.5 6.9 %collective-permute-start.26 = (bf16[320,256]{1,0:T(8,128)(2,1)S(1)}, bf16[320,256]{1,0:T(8,128)(2,1)S(1)}, u32[]{:S(2)}, u32[]{:S(2)}) collective-permute-start(bf16[320,256]{1,0:T(8,128)(2,1)S(1)} %pad_maximum_fusion.1.refs_0_), channel_id=1, source_target_pairs={{0,4},{4,0},{8,12},{12,8},{16,20},{20,16},{24,28},{28,24},{1,5},{5... | collective-permute-start | bytes 491528 | tf_op jit(solution)/shard_map/ppermute | solution.py:849
  149.7 3.7 %collective-permute-start.27 = (bf16[320,256]{1,0:T(8,128)(2,1)S(1)}, bf16[320,256]{1,0:T(8,128)(2,1)S(1)}, u32[]{:S(2)}, u32[]{:S(2)}) collective-permute-start(bf16[320,256]{1,0:T(8,128)(2,1)S(1)} %collective-permute-done.23.refs_1_), channel_id=1, source_target_pairs={{0,4},{4,0},{8,12},{12,8},{16,20},{20,16},{24,28},{28,24},{1,5},{5... | collective-permute-start | bytes 491528 | tf_op jit(solution)/shard_map/ppermute | solution.py:849
  152.9 1.4 collective-permute-start.28
  152.9 1.6 collective-permute-start.29
  (21 other events, 197.1 us)
Sparse Core Ops, SparseCore 0:
  28.0 25.1 all-gather.2
  87.9 41.9 reduce-scatter.1

commit v3 on v2

--- a/solution.py
+++ b/solution.py
@@ -975,11 +975,13 @@
 
     grad_mid, keep_f, give_f, vec = ff_bwd_call(place, grad, again, we, wr, sm, planes, r_f)
     got_f = swap_dp(give_f, 1)
+    parts_f = to_planes(keep_f, got_f, place[2])
+    grad_mid, parts_f = lax.optimization_barrier((grad_mid, parts_f))
+    planes_f = swap_planes(parts_f)
     patch_grad, keep_a, give_a = attn_bwd_call(place, grad_mid, x, packed, probs, mixed, value, wqkv, wm, sm, vec)
-    got_f, keep_a, give_a = lax.optimization_barrier((got_f, keep_a, give_a))
+    planes_f, keep_a, give_a = lax.optimization_barrier((planes_f, keep_a, give_a))
 
     got_a = swap_dp(give_a, 1)
-    planes_f = swap_planes(to_planes(keep_f, got_f, place[2]))
     shards_a = to_shards([keep_a[0], got_a[0]], me)
     mp_a = turn_shards(shards_a)
     planes_f, sums_1 = lax.optimization_barrier((planes_f, sums_1, shards_a))[:2]

time: 164 us -> 171 us (1.043)
  waiting for transfers between devices: 31.8 us -> 36.3 us
  local copies, waits for them, and re-layouts: 6.98 us -> 10.6 us
  starting transfers between devices: 32.6 us -> 30.8 us
    ppermute x12, waiting for transfers between devices: 15.1 us -> 20.1 us  [turn_mp(): return lax.ppermute(x, 'mp', [(i, (i + k) % n) for i in range(n)])]
    unnamed x42 -> x54, local copies, waits for them, and re-layouts: 6.74 us -> 10.4 us
    ppermute x18, waiting for transfers between devices: 16.7 us -> 13.3 us  [swap_dp(): return lax.ppermute(x, 'dp', [(i, i ^ bits) for i in range(n)])]
    reduce_scatter x1, waiting for transfers between devices: 0.01 us -> 2.81 us  [body(): sums_1 = lax.psum_scatter(grads_1, 'dp', scatter_dimension=0, tiled=False)]
  transfers between devices with their start and end apart: 32 -> 32, of which waited for: 16 -> 17; matrix products, arithmetic and copies ran while one was open for 1% -> 1% of each run, Pallas kernels for 23% -> 17%
where the time goes in v3:
time: 171 us
  Pallas kernels  73.7 us (43%)
  waiting for transfers between devices  36.3 us (21%)
  starting transfers between devices  30.8 us (18%)
  between operations  14.4 us (8%)
  local copies, waits for them, and re-layouts  10.6 us (6%)
  other arithmetic  4.79 us (3%)
    pallas_call x2, Pallas kernels, held_call(): pl.pallas_call(kernel, in_specs=[pl.BlockSpec(memory_space=pltpu.SMEM)] +...  33.4 us
    ppermute x12, starting transfers between devices, turn_mp(): return lax.ppermute(x, 'mp', [(i, (i + k) % n) for i in range(n)])  21.6 us
    ppermute x12, waiting for transfers between devices, turn_mp(): return lax.ppermute(x, 'mp', [(i, (i + k) % n) for i in range(n)])  20.1 us
    pallas_call x1, Pallas kernels, attn_bwd_call(): pl.pallas_call(attn_bwd_kernel, grid_spec=pltpu.PrefetchScalarGridSpec(nu...  13.6 us
    ppermute x18, waiting for transfers between devices, swap_dp(): return lax.ppermute(x, 'dp', [(i, i ^ bits) for i in range(n)])  13.3 us
    pallas_call x1, Pallas kernels, attn_fwd_call(): pl.pallas_call(attn_fwd_kernel, grid_spec=pltpu.PrefetchScalarGridSpec(nu...  11.2 us
    unnamed x54, local copies, waits for them, and re-layouts  10.4 us
    ppermute x18, starting transfers between devices, swap_dp(): return lax.ppermute(x, 'dp', [(i, i ^ bits) for i in range(n)])  9.1 us
  transfers between devices with their start and end apart: 32, of which 17 were waited for; matrix products, arithmetic and copies ran while one was open for 1% of the time, Pallas kernels for 17%

profile of v3, /device:TPU:0, one launch (start us, length us, event | category | flops | bytes accessed | tf_op | source)
XLA Modules:
  0.0 170.5 jit_solution(11907074907642446514)
XLA Ops:
  7.8 2.8 %pack.1 = (bf16[256,256]{1,0:T(8,128)(2,1)}, bf16[256,256]{1,0:T(8,128)(2,1)}, bf16[2,32,256]{2,1,0:T(8,128)(2,1)}) custom-call(s32[4]{0:T(128)} %pad_add_fusion.2.place, bf16[2,192,256]{2,1,0:T(8,128)(2,1)} %bitcast.76, bf16[2,64,256]{2,1,0:T(8,128)(2,1)} %bitcast.79, bf16[2,2,64]{2,1,0:T(2,128)(2,1)} %gain.1, bf16[2,2,64]{2,1,0:T(2,128)(2,1)} %shift.1, ...), custom_call_target="tpu_custom_call" | custom-call | flops 1000000000 | bytes 1048576 | tf_op jit(solution)/shard_map/pack/pallas_call | solution.py:827
  10.7 5.0 %collective-permute-start.5 = (bf16[256,256]{1,0:T(8,128)(2,1)}, bf16[256,256]{1,0:T(8,128)(2,1)S(1)}, u32[]{:S(2)}, u32[]{:S(2)}) collective-permute-start(bf16[256,256]{1,0:T(8,128)(2,1)} %get-tuple-element.70), channel_id=1, source_target_pairs={{0,3},{1,0},{2,1},{3,2},{4,7},{5,4},{6,5},{7,6},{8,11},{9,8},{10,9... | collective-permute-start | bytes 393224 | tf_op jit(solution)/shard_map/ppermute | solution.py:844
  16.7 3.2 %collective-permute-done.5.refs_5_ = bf16[256,256]{1,0:T(8,128)(2,1)S(1)} collective-permute-done((bf16[256,256]{1,0:T(8,128)(2,1)}, bf16[256,256]{1,0:T(8,128)(2,1)S(1)}, u32[]{:S(2)}, u32[]{:S(2)}) %collective-permute-start.5) | collective-permute-done | bytes 131104 | tf_op jit(solution)/shard_map/ppermute | solution.py:844
  19.9 7.2 %collective-permute-done.4.refs_4_ = bf16[256,256]{1,0:T(8,128)(2,1)S(1)} collective-permute-done((bf16[256,256]{1,0:T(8,128)(2,1)}, bf16[256,256]{1,0:T(8,128)(2,1)S(1)}, u32[]{:S(2)}, u32[]{:S(2)}) %collective-permute-start.4) | collective-permute-done | bytes 131104 | tf_op jit(solution)/shard_map/ppermute | solution.py:844
  28.8 1.9 %collective-permute-start.1 = (bf16[256,256]{1,0:T(8,128)(2,1)}, bf16[256,256]{1,0:T(8,128)(2,1)S(1)}, u32[]{:S(2)}, u32[]{:S(2)}) collective-permute-start(bf16[256,256]{1,0:T(8,128)(2,1)} %get-tuple-element.69), channel_id=1, source_target_pairs={{0,2},{1,3},{2,0},{3,1},{4,6},{5,7},{6,4},{7,5},{8,10},{9,11},{10,... | collective-permute-start | bytes 393224 | tf_op jit(solution)/shard_map/ppermute | solution.py:844
  32.3 2.8 %collective-permute-start.2 = (bf16[256,256]{1,0:T(8,128)(2,1)}, bf16[256,256]{1,0:T(8,128)(2,1)S(1)}, u32[]{:S(2)}, u32[]{:S(2)}) collective-permute-start(bf16[256,256]{1,0:T(8,128)(2,1)} %get-tuple-element.69), channel_id=1, source_target_pairs={{0,3},{1,0},{2,1},{3,2},{4,7},{5,4},{6,5},{7,6},{8,11},{9,8},{10,9... | collective-permute-start | bytes 393224 | tf_op jit(solution)/shard_map/ppermute | solution.py:844
  36.0 11.2 %attn_fwd.1 = (f32[1568,256]{1,0:T(8,128)S(1)}, f32[1568,256]{1,0:T(8,128)}, bf16[8,2,3,112,256]{4,3,2,1,0:T(8,128)(2,1)}, bf16[8,2,448,256]{3,2,1,0:T(8,128)(2,...) custom-call(s32[18]{0:T(128)S(1)} %pad_add_fusion.1.place, ...), custom_call_target="tpu_custom_call" | custom-call | flops 10000000000 | bytes 1048576 | tf_op jit(solution)/shard_map/attn_fwd/pallas_call | solution.py:715
  49.2 3.7 %ff_fwd.1 = (f32[1568,256]{1,0:T(8,128)S(1)}, bf16[4,256,256]{2,1,0:T(8,128)(2,1)}, bf16[256,1024]{1,0:T(8,128)(2,1)}) custom-call(s32[18]{0:T(128)S(1)} %pad_add_fusion.1.place, f32[1568,256]{1,0:T(8,128)S(1)} %get-tuple-element.74.middle, f32[32,256]{1,0:T(8,128)S(1)} %get-tuple-element.75.sm, bf16[2,256,256]{2,1,0:T(8,128)(2,1)S(1)} %copy-done.4, ...), custom_call_target="tpu_custom_call" | custom-call | flops 6000000000 | bytes 1048576 | tf_op jit(solution)/shard_map/ff_fwd/pallas_call | solution.py:731
  55.4 31.3 %top_block.1 = (bf16[1568,256]{1,0:T(8,128)(2,1)}, f32[1568,256]{1,0:T(8,128)S(1)}, bf16[8,4,112,256]{3,2,1,0:T(8,128)(2,1)}) custom-call(s32[18]{0:T(128)S(1)} %pad_add_fusion.1.place, f32[1568,256]{1,0:T(8,128)} %copy-done.8, bf16[1568,256]{1,0:T(8,128)(2,1)S(1)} %bitcast.70, bf16[2,192,256]{2,1,0:T(8,128)(2,1)S(1)} %bitcast.78, ...), custom_call_target="tpu_custom_call" | custom-call | flops 30000001024 | bytes 1048576 | tf_op jit(solution)/shard_map/top_block/pallas_call | solution.py:699
  87.9 9.0 %ff_bwd.1 = (f32[1568,256]{1,0:T(8,128)S(1)}, bf16[4,4,64,256]{3,2,1,0:T(8,128)(2,1)S(1)}, bf16[4,4,64,256]{3,2,1,0:T(8,128)(2,1)S(1)}, f32[32,8,256]{2,1,0:T(8,128)S(1)}) custom-call(s32[4]{0:T(128)S(1)} %copy-done, f32[1568,256]{1,0:T(8,128)} %copy-done.15, f32[1568,256]{1,0:T(8,128)} %get-tuple-element.83.middle, bf16[4,256,256]{2,1,0:T(8,128)(2,1)S(1)} %copy-done.16, ...), custom_call_target="tpu_custom_call" | custom-call | flops 10000000000 | bytes 1048576 | tf_op jit(solution)/shard_map/ff_bwd/pallas_call | solution.py:758
  98.3 1.8 %collective-permute-done.12 = bf16[4,4,64,256]{3,2,1,0:T(8,128)(2,1)} collective-permute-done((bf16[4,4,64,256]{3,2,1,0:T(8,128)(2,1)S(1)}, bf16[4,4,64,256]{3,2,1,0:T(8,128)(2,1)}, u32[]{:S(2)}, u32[]{:S(2)}) %collective-permute-start.12) | collective-permute-done | bytes 524320 | tf_op jit(solution)/shard_map/ppermute | solution.py:849
  101.3 1.6 collective-permute-start.13
  102.9 1.5 collective-permute-start.14
  104.9 2.2 %copy-done.11 = bf16[8,2,448,256]{3,2,1,0:T(8,128)(2,1)S(1)} copy-done((bf16[8,2,448,256]{3,2,1,0:T(8,128)(2,1)S(1)}, bf16[8,2,448,256]{3,2,1,0:T(8,128)(2,1)}, u32[]{:S(2)}) %copy-start.11) | copy-done | bytes 3670040
  107.1 1.9 %copy-done.12 = bf16[8,2,3,112,256]{4,3,2,1,0:T(8,128)(2,1)S(1)} copy-done((bf16[8,2,3,112,256]{4,3,2,1,0:T(8,128)(2,1)S(1)}, bf16[8,2,3,112,256]{4,3,2,1,0:T(8,128)(2,1)}, u32[]{:S(2)}) %copy-start.12) | copy-done | bytes 2752536
  109.0 13.6 %attn_bwd.1 = (bf16[1568,256]{1,0:T(8,128)(2,1)}, bf16[1,4,144,256]{3,2,1,0:T(8,128)(2,1)S(1)}, bf16[1,4,144,256]{3,2,1,0:T(8,128)(2,1)S(1)}) custom-call(s32[4]{0:T(128)S(1)} %copy-done, f32[1568,256]{1,0:T(8,128)S(1)} %copy-done.14, bf16[1568,256]{1,0:T(8,128)(2,1)S(1)} %bitcast.72, bf16[8,2,3,112,256]{4,3,2,1,0:T(8,128)(2,1)S(1)} %copy-done.12, ...), custom_call_target="tpu_custom_call" | custom-call | flops 16000000000 | bytes 1048576 | tf_op jit(solution)/shard_map/attn_bwd/pallas_call | solution.py:774
  123.3 1.6 collective-permute-done.16
  125.7 2.4 %collective-permute-start.18 = (bf16[144,256]{1,0:T(8,128)(2,1)S(1)}, bf16[144,256]{1,0:T(8,128)(2,1)S(1)}, u32[]{:S(2)}, u32[]{:S(2)}) collective-permute-start(bf16[144,256]{1,0:T(8,128)(2,1)S(1)} %get-tuple-element.139), channel_id=1, source_target_pairs={{0,2},{1,3},{2,0},{3,1},{4,6},{5,7},{6,4},{7,5},{8,10},{9,11},{10,... | collective-permute-start | bytes 221192 | tf_op jit(solution)/shard_map/ppermute | solution.py:844
  128.1 1.4 collective-permute-start.19
  129.5 2.5 %collective-permute-done.17 = bf16[144,256]{1,0:T(8,128)(2,1)S(1)} collective-permute-done((bf16[144,256]{1,0:T(8,128)(2,1)S(1)}, bf16[144,256]{1,0:T(8,128)(2,1)S(1)}, u32[]{:S(2)}, u32[]{:S(2)}) %collective-permute-start.17) | collective-permute-done | bytes 73760 | tf_op jit(solution)/shard_map/ppermute | solution.py:844
  132.0 2.4 %collective-permute-done.18 = bf16[144,256]{1,0:T(8,128)(2,1)S(1)} collective-permute-done((bf16[144,256]{1,0:T(8,128)(2,1)S(1)}, bf16[144,256]{1,0:T(8,128)(2,1)S(1)}, u32[]{:S(2)}, u32[]{:S(2)}) %collective-permute-start.18) | collective-permute-done | bytes 73760 | tf_op jit(solution)/shard_map/ppermute | solution.py:844
  134.5 2.8 %reduce-scatter.2.cloned.1.call-done = bf16[1,4,112,256]{3,2,1,0:T(8,128)(2,1)} async-done(((bf16[8,4,112,256]{3,2,1,0:T(8,128)(2,1)}), bf16[1,4,112,256]{3,2,1,0:T(8,128)(2,1)}) %reduce-scatter.2.cloned.1.call-update) | async-done | bytes 229392 | tf_op jit(solution)/shard_map/reduce_scatter | solution.py:974
  138.3 1.5 collective-permute-start.20
  139.8 2.4 %collective-permute-start.21 = (bf16[176,256]{1,0:T(8,128)(2,1)S(1)}, bf16[176,256]{1,0:T(8,128)(2,1)S(1)}, u32[]{:S(2)}, u32[]{:S(2)}) collective-permute-start(bf16[176,256]{1,0:T(8,128)(2,1)S(1)} %get-tuple-element.135), channel_id=1, source_target_pairs={{0,2},{1,3},{2,0},{3,1},{4,6},{5,7},{6,4},{7,5},{8,10},{9,11},{10,... | collective-permute-start | bytes 270344 | tf_op jit(solution)/shard_map/ppermute | solution.py:844
  142.2 1.4 collective-permute-start.22
  143.7 1.9 %collective-permute-done.20 = bf16[176,256]{1,0:T(8,128)(2,1)S(1)} collective-permute-done((bf16[176,256]{1,0:T(8,128)(2,1)S(1)}, bf16[176,256]{1,0:T(8,128)(2,1)S(1)}, u32[]{:S(2)}, u32[]{:S(2)}) %collective-permute-start.20) | collective-permute-done | bytes 90144 | tf_op jit(solution)/shard_map/ppermute | solution.py:844
  145.5 3.0 %collective-permute-done.21 = bf16[176,256]{1,0:T(8,128)(2,1)S(1)} collective-permute-done((bf16[176,256]{1,0:T(8,128)(2,1)S(1)}, bf16[176,256]{1,0:T(8,128)(2,1)S(1)}, u32[]{:S(2)}, u32[]{:S(2)}) %collective-permute-start.21) | collective-permute-done | bytes 90144 | tf_op jit(solution)/shard_map/ppermute | solution.py:844
  149.4 1.5 collective-permute-start.23
  151.5 1.5 collective-permute-start.25
  153.0 3.5 %collective-permute-done.23.refs_1_ = bf16[320,256]{1,0:T(8,128)(2,1)S(1)} collective-permute-done((bf16[320,256]{1,0:T(8,128)(2,1)S(1)}, bf16[320,256]{1,0:T(8,128)(2,1)S(1)}, u32[]{:S(2)}, u32[]{:S(2)}) %collective-permute-start.23) | collective-permute-done | bytes 163872 | tf_op jit(solution)/shard_map/ppermute | solution.py:849
  156.5 3.5 %collective-permute-done.24.refs_2_ = bf16[320,256]{1,0:T(8,128)(2,1)S(1)} collective-permute-done((bf16[320,256]{1,0:T(8,128)(2,1)S(1)}, bf16[320,256]{1,0:T(8,128)(2,1)S(1)}, u32[]{:S(2)}, u32[]{:S(2)}) %collective-permute-start.24) | collective-permute-done | bytes 163872 | tf_op jit(solution)/shard_map/ppermute | solution.py:849
  161.6 2.1 %unpack.1 = (f32[2,192,256]{2,1,0:T(8,128)}, f32[2,64,256]{2,1,0:T(8,128)}, f32[2,256,256]{2,1,0:T(8,128)}, f32[2,64,1024]{2,1,0:T(8,128)}, f32[2,2,64]{2,1,0:T(...) custom-call(s32[4]{0:T(128)S(1)} %copy-done, ...), custom_call_target="tpu_custom_call" | custom-call | flops 2000000000 | bytes 1048576 | tf_op jit(solution)/shard_map/unpack/pallas_call | solution.py:699
  (115 shorter events, 20.0 us)
Async XLA Ops:
  7.2 46.9 %all-gather.3.cloned.1.call-start = ((), (), s32[]{:S(2)}) async-start(), calls=%async_computation.2 | async-start | bytes 1548288 | tf_op jit(solution)/shard_map/all_gather | solution.py:968
  10.7 9.3 %collective-permute-start.5 = (bf16[256,256]{1,0:T(8,128)(2,1)}, bf16[256,256]{1,0:T(8,128)(2,1)S(1)}, u32[]{:S(2)}, u32[]{:S(2)}) collective-permute-start(bf16[256,256]{1,0:T(8,128)(2,1)} %get-tuple-element.70), channel_id=1, source_target_pairs={{0,3},{1,0},{2,1},{3,2},{4,7},{5,4},{6,5},{7,6},{8,11},{9,8},{10,9... | collective-permute-start | bytes 393224 | tf_op jit(solution)/shard_map/ppermute | solution.py:844
  15.7 11.4 %collective-permute-start.4 = (bf16[256,256]{1,0:T(8,128)(2,1)}, bf16[256,256]{1,0:T(8,128)(2,1)S(1)}, u32[]{:S(2)}, u32[]{:S(2)}) collective-permute-start(bf16[256,256]{1,0:T(8,128)(2,1)} %get-tuple-element.70), channel_id=1, source_target_pairs={{0,2},{1,3},{2,0},{3,1},{4,6},{5,7},{6,4},{7,5},{8,10},{9,11},{10,... | collective-permute-start | bytes 393224 | tf_op jit(solution)/shard_map/ppermute | solution.py:844
  15.7 11.4 %collective-permute-start.3 = (bf16[256,256]{1,0:T(8,128)(2,1)}, bf16[256,256]{1,0:T(8,128)(2,1)S(1)}, u32[]{:S(2)}, u32[]{:S(2)}) collective-permute-start(bf16[256,256]{1,0:T(8,128)(2,1)} %get-tuple-element.70), channel_id=1, source_target_pairs={{0,1},{1,2},{2,3},{3,0},{4,5},{5,6},{6,7},{7,4},{8,9},{9,10},{10,1... | collective-permute-start | bytes 393224 | tf_op jit(solution)/shard_map/ppermute | solution.py:844
  27.9 109.4 %reduce-scatter.2.cloned.1.call-start = ((), (), s32[]{:S(2)}) async-start(), calls=%async_computation.1 | async-start | bytes 2064384 | tf_op jit(solution)/shard_map/reduce_scatter | solution.py:974
  27.9 19.3 %collective-permute-start = (bf16[256,256]{1,0:T(8,128)(2,1)}, bf16[256,256]{1,0:T(8,128)(2,1)S(1)}, u32[]{:S(2)}, u32[]{:S(2)}) collective-permute-start(bf16[256,256]{1,0:T(8,128)(2,1)} %get-tuple-element.69), channel_id=1, source_target_pairs={{0,1},{1,2},{2,3},{3,0},{4,5},{5,6},{6,7},{7,4},{8,9},{9,10},{10,1... | collective-permute-start | bytes 393224 | tf_op jit(solution)/shard_map/ppermute | solution.py:844
  28.8 18.4 %collective-permute-start.1 = (bf16[256,256]{1,0:T(8,128)(2,1)}, bf16[256,256]{1,0:T(8,128)(2,1)S(1)}, u32[]{:S(2)}, u32[]{:S(2)}) collective-permute-start(bf16[256,256]{1,0:T(8,128)(2,1)} %get-tuple-element.69), channel_id=1, source_target_pairs={{0,2},{1,3},{2,0},{3,1},{4,6},{5,7},{6,4},{7,5},{8,10},{9,11},{10,... | collective-permute-start | bytes 393224 | tf_op jit(solution)/shard_map/ppermute | solution.py:844
  30.9 1.4 collective-permute-start.6
  31.0 4.2 %collective-permute-start.7 = (bf16[256,256]{1,0:T(8,128)(2,1)S(1)}, bf16[256,256]{1,0:T(8,128)(2,1)S(1)}, u32[]{:S(2)}, u32[]{:S(2)}) collective-permute-start(bf16[256,256]{1,0:T(8,128)(2,1)S(1)} %collective-permute-done.4.refs_4_), channel_id=1, source_target_pairs={{0,4},{4,0},{8,12},{12,8},{16,20},{20,16},{24,28},{28,24},{1,5},{5... | collective-permute-start | bytes 393224 | tf_op jit(solution)/shard_map/ppermute | solution.py:849
  31.5 3.7 %collective-permute-start.8 = (bf16[256,256]{1,0:T(8,128)(2,1)S(1)}, bf16[256,256]{1,0:T(8,128)(2,1)S(1)}, u32[]{:S(2)}, u32[]{:S(2)}) collective-permute-start(bf16[256,256]{1,0:T(8,128)(2,1)S(1)} %collective-permute-done.5.refs_5_), channel_id=1, source_target_pairs={{0,4},{4,0},{8,12},{12,8},{16,20},{20,16},{24,28},{28,24},{1,5},{5... | collective-permute-start | bytes 393224 | tf_op jit(solution)/shard_map/ppermute | solution.py:849
  32.3 14.9 %collective-permute-start.2 = (bf16[256,256]{1,0:T(8,128)(2,1)}, bf16[256,256]{1,0:T(8,128)(2,1)S(1)}, u32[]{:S(2)}, u32[]{:S(2)}) collective-permute-start(bf16[256,256]{1,0:T(8,128)(2,1)} %get-tuple-element.69), channel_id=1, source_target_pairs={{0,3},{1,0},{2,1},{3,2},{4,7},{5,4},{6,5},{7,6},{8,11},{9,8},{10,9... | collective-permute-start | bytes 393224 | tf_op jit(solution)/shard_map/ppermute | solution.py:844
  47.2 1.4 collective-permute-start.10
  47.3 1.5 collective-permute-start.11
  47.8 1.3 collective-permute-start.9
  98.0 2.0 %collective-permute-start.12 = (bf16[4,4,64,256]{3,2,1,0:T(8,128)(2,1)S(1)}, bf16[4,4,64,256]{3,2,1,0:T(8,128)(2,1)}, u32[]{:S(2)}, u32[]{:S(2)}) collective-permute-start(bf16[4,4,64,256]{3,2,1,0:T(8,128)(2,1)S(1)} %get-tuple-element.88), channel_id=1, source_target_pairs={{0,4},{4,0},{8,12},{12,8},{16,20},{20,16},{24,28},{28,24},{1,5},{5... | collective-permute-start | bytes 1572872 | tf_op jit(solution)/shard_map/ppermute | solution.py:849
  101.3 21.3 %collective-permute-start.13 = (bf16[4,64,256]{2,1,0:T(8,128)(2,1)S(1)}, bf16[4,64,256]{2,1,0:T(8,128)(2,1)S(1)}, u32[]{:S(2)}, u32[]{:S(2)}) collective-permute-start(bf16[4,64,256]{2,1,0:T(8,128)(2,1)S(1)} %get-tuple-element.99), channel_id=1, source_target_pairs={{0,8},{4,12},{8,0},{12,4},{16,24},{20,28},{24,16},{28,20},{1,9},{5... | collective-permute-start | bytes 393224 | tf_op jit(solution)/shard_map/ppermute | solution.py:849
  102.9 19.7 %collective-permute-start.14 = (bf16[4,64,256]{2,1,0:T(8,128)(2,1)S(1)}, bf16[4,64,256]{2,1,0:T(8,128)(2,1)S(1)}, u32[]{:S(2)}, u32[]{:S(2)}) collective-permute-start(bf16[4,64,256]{2,1,0:T(8,128)(2,1)S(1)} %get-tuple-element.100), channel_id=1, source_target_pairs={{0,16},{4,20},{8,24},{12,28},{16,0},{20,4},{24,8},{28,12},{1,17},{... | collective-permute-start | bytes 393224 | tf_op jit(solution)/shard_map/ppermute | solution.py:849
  104.4 18.2 %collective-permute-start.15 = (bf16[4,64,256]{2,1,0:T(8,128)(2,1)S(1)}, bf16[4,64,256]{2,1,0:T(8,128)(2,1)S(1)}, u32[]{:S(2)}, u32[]{:S(2)}) collective-permute-start(bf16[4,64,256]{2,1,0:T(8,128)(2,1)S(1)} %get-tuple-element.101), channel_id=1, source_target_pairs={{0,24},{4,28},{8,16},{12,20},{16,8},{20,12},{24,0},{28,4},{1,25},{... | collective-permute-start | bytes 393224 | tf_op jit(solution)/shard_map/ppermute | solution.py:849
  123.3 1.6 collective-permute-start.16
  125.0 7.0 %collective-permute-start.17 = (bf16[144,256]{1,0:T(8,128)(2,1)S(1)}, bf16[144,256]{1,0:T(8,128)(2,1)S(1)}, u32[]{:S(2)}, u32[]{:S(2)}) collective-permute-start(bf16[144,256]{1,0:T(8,128)(2,1)S(1)} %get-tuple-element.137), channel_id=1, source_target_pairs={{0,1},{1,2},{2,3},{3,0},{4,5},{5,6},{6,7},{7,4},{8,9},{9,10},{10,1... | collective-permute-start | bytes 221192 | tf_op jit(solution)/shard_map/ppermute | solution.py:844
  125.7 8.7 %collective-permute-start.18 = (bf16[144,256]{1,0:T(8,128)(2,1)S(1)}, bf16[144,256]{1,0:T(8,128)(2,1)S(1)}, u32[]{:S(2)}, u32[]{:S(2)}) collective-permute-start(bf16[144,256]{1,0:T(8,128)(2,1)S(1)} %get-tuple-element.139), channel_id=1, source_target_pairs={{0,2},{1,3},{2,0},{3,1},{4,6},{5,7},{6,4},{7,5},{8,10},{9,11},{10,... | collective-permute-start | bytes 221192 | tf_op jit(solution)/shard_map/ppermute | solution.py:844
  128.1 6.3 %collective-permute-start.19 = (bf16[144,256]{1,0:T(8,128)(2,1)S(1)}, bf16[144,256]{1,0:T(8,128)(2,1)S(1)}, u32[]{:S(2)}, u32[]{:S(2)}) collective-permute-start(bf16[144,256]{1,0:T(8,128)(2,1)S(1)} %get-tuple-element.138), channel_id=1, source_target_pairs={{0,3},{1,0},{2,1},{3,2},{4,7},{5,4},{6,5},{7,6},{8,11},{9,8},{10,9... | collective-permute-start | bytes 221192 | tf_op jit(solution)/shard_map/ppermute | solution.py:844
  138.3 7.3 %collective-permute-start.20 = (bf16[176,256]{1,0:T(8,128)(2,1)S(1)}, bf16[176,256]{1,0:T(8,128)(2,1)S(1)}, u32[]{:S(2)}, u32[]{:S(2)}) collective-permute-start(bf16[176,256]{1,0:T(8,128)(2,1)S(1)} %get-tuple-element.134), channel_id=1, source_target_pairs={{0,1},{1,2},{2,3},{3,0},{4,5},{5,6},{6,7},{7,4},{8,9},{9,10},{10,1... | collective-permute-start | bytes 270344 | tf_op jit(solution)/shard_map/ppermute | solution.py:844
  139.8 8.7 %collective-permute-start.21 = (bf16[176,256]{1,0:T(8,128)(2,1)S(1)}, bf16[176,256]{1,0:T(8,128)(2,1)S(1)}, u32[]{:S(2)}, u32[]{:S(2)}) collective-permute-start(bf16[176,256]{1,0:T(8,128)(2,1)S(1)} %get-tuple-element.135), channel_id=1, source_target_pairs={{0,2},{1,3},{2,0},{3,1},{4,6},{5,7},{6,4},{7,5},{8,10},{9,11},{10,... | collective-permute-start | bytes 270344 | tf_op jit(solution)/shard_map/ppermute | solution.py:844
  142.2 6.3 %collective-permute-start.22 = (bf16[176,256]{1,0:T(8,128)(2,1)S(1)}, bf16[176,256]{1,0:T(8,128)(2,1)S(1)}, u32[]{:S(2)}, u32[]{:S(2)}) collective-permute-start(bf16[176,256]{1,0:T(8,128)(2,1)S(1)} %get-tuple-element.136), channel_id=1, source_target_pairs={{0,3},{1,0},{2,1},{3,2},{4,7},{5,4},{6,5},{7,6},{8,11},{9,8},{10,9... | collective-permute-start | bytes 270344 | tf_op jit(solution)/shard_map/ppermute | solution.py:844
  149.4 7.1 %collective-permute-start.23 = (bf16[320,256]{1,0:T(8,128)(2,1)S(1)}, bf16[320,256]{1,0:T(8,128)(2,1)S(1)}, u32[]{:S(2)}, u32[]{:S(2)}) collective-permute-start(bf16[320,256]{1,0:T(8,128)(2,1)S(1)} %pad_maximum_fusion.1.refs_0_), channel_id=1, source_target_pairs={{0,8},{4,12},{8,0},{12,4},{16,24},{20,28},{24,16},{28,20},{1,9},{5... | collective-permute-start | bytes 491528 | tf_op jit(solution)/shard_map/ppermute | solution.py:849
  150.9 9.1 %collective-permute-start.24 = (bf16[320,256]{1,0:T(8,128)(2,1)S(1)}, bf16[320,256]{1,0:T(8,128)(2,1)S(1)}, u32[]{:S(2)}, u32[]{:S(2)}) collective-permute-start(bf16[320,256]{1,0:T(8,128)(2,1)S(1)} %pad_maximum_fusion.1.refs_0_), channel_id=1, source_target_pairs={{0,16},{4,20},{8,24},{12,28},{16,0},{20,4},{24,8},{28,12},{1,17},{... | collective-permute-start | bytes 491528 | tf_op jit(solution)/shard_map/ppermute | solution.py:849
  151.5 8.5 %collective-permute-start.25 = (bf16[320,256]{1,0:T(8,128)(2,1)S(1)}, bf16[320,256]{1,0:T(8,128)(2,1)S(1)}, u32[]{:S(2)}, u32[]{:S(2)}) collective-permute-start(bf16[320,256]{1,0:T(8,128)(2,1)S(1)} %pad_maximum_fusion.1.refs_0_), channel_id=1, source_target_pairs={{0,24},{4,28},{8,16},{12,20},{16,8},{20,12},{24,0},{28,4},{1,25},{... | collective-permute-start | bytes 491528 | tf_op jit(solution)/shard_map/ppermute | solution.py:849
  153.0 7.5 %collective-permute-start.26 = (bf16[320,256]{1,0:T(8,128)(2,1)S(1)}, bf16[320,256]{1,0:T(8,128)(2,1)S(1)}, u32[]{:S(2)}, u32[]{:S(2)}) collective-permute-start(bf16[320,256]{1,0:T(8,128)(2,1)S(1)} %pad_maximum_fusion.1.refs_0_), channel_id=1, source_target_pairs={{0,4},{4,0},{8,12},{12,8},{16,20},{20,16},{24,28},{28,24},{1,5},{5... | collective-permute-start | bytes 491528 | tf_op jit(solution)/shard_map/ppermute | solution.py:849
  156.5 4.0 %collective-permute-start.27 = (bf16[320,256]{1,0:T(8,128)(2,1)S(1)}, bf16[320,256]{1,0:T(8,128)(2,1)S(1)}, u32[]{:S(2)}, u32[]{:S(2)}) collective-permute-start(bf16[320,256]{1,0:T(8,128)(2,1)S(1)} %collective-permute-done.23.refs_1_), channel_id=1, source_target_pairs={{0,4},{4,0},{8,12},{12,8},{16,20},{20,16},{24,28},{28,24},{1,5},{5... | collective-permute-start | bytes 491528 | tf_op jit(solution)/shard_map/ppermute | solution.py:849
  160.0 1.4 collective-permute-start.28
  160.0 1.6 collective-permute-start.29
  (27 other events, 309.2 us)
Sparse Core Ops, SparseCore 0:
  28.0 25.1 all-gather.2
  98.4 38.8 reduce-scatter.1
